TPU v7x, 32 devices: a whole 2x2x4 slice. The times are simulated.
32 devices in a mesh: seq: 16 (over z, y, x), tp: 2 (over core).
Axes of the slice: x: 2, y: 2, z: 4, core: 2. Of those that a mesh axis runs over, the one named last changes fastest.
Arguments:
- tokens: bfloat16 [2048, 4096], P('seq'), may hold values from -6 to 6
- w_query: bfloat16 [4096, 2048], P('seq', 'tp'), may hold values from -0.09375 to 0.09375
- w_key: bfloat16 [4096, 2048], P('seq', 'tp'), may hold values from -0.09375 to 0.09375
- w_value: bfloat16 [4096, 2048], P('seq', 'tp'), may hold values from -0.09375 to 0.09375
- short_taps: float32 [3, 3, 2048], P(None, None, 'tp'), may hold values from -2.5 to 2.5
- decay_rates: float32 [16, 2048], P(None, 'tp'), may hold values from 4.8828125e-05 to 0.04
- residues: float32 [16, 2048], P(None, 'tp'), may hold values from -1.2 to 1.2
- skip_gain: float32 [2048], P('tp'), may hold values from 0.5 to 1.5
- w_out: bfloat16 [2048, 4096], P('tp', 'seq'), may hold values from -0.125 to 0.125
Outputs:
- mixed: bfloat16 [2048, 4096], P('seq', 'tp')
All inputs are finite; a program needn't handle non-finite values.
Results may differ from a plain program's by a relative error of at most 0.013.
Values may be sent and summed in bfloat16 or wider, within the bound.
No kernel may reach another device: no remote copies, remote signals or barrier semaphores. Data moves between devices by JAX's collectives and lax.ppermute only.
A program may use at most 128 MiB of HBM per device.

v0:
```python
import math

import jax
import jax.numpy as jnp
from jax import lax
from jax.sharding import PartitionSpec as P

SHORT = 3


HIGHEST = lax.Precision.HIGHEST


def passed_along(value, axis, by):
    size = lax.axis_size(axis)
    pairs = [(i, i + by) for i in range(size) if 0 <= i + by < size]
    return lax.ppermute(value, axis, pairs)


def from_partner(value, axis, distance):
    mask = 2**distance
    pairs = [(source, source ^ mask) for source in range(lax.axis_size(axis))]
    return lax.ppermute(value, axis, pairs)


def complex_mul(left_re, left_im, right_re, right_im):
    return (left_re * right_re - left_im * right_im, left_re * right_im + left_im * right_re)


def angle_table(product, modulus):
    phase = (product % modulus).astype(jnp.float32) * (2.0 * math.pi / modulus)
    return (jnp.cos(phase), jnp.sin(phase))


def along_rows(table, values):
    return jnp.einsum("rm,qmc->qrc", table, values, precision=HIGHEST)


def body(tokens, w_query, w_key, w_value, short_taps, decay_rates, residues, skip_gain, w_out):
    tok_rows = tokens.shape[0]
    seq_parts = lax.axis_size("seq")
    fft_len = 2 * seq_parts * tok_rows
    my_index = lax.axis_index("seq")
    slices = (
        lax.all_gather(w_query, "seq", axis=0, tiled=True),
        lax.all_gather(w_key, "seq", axis=0, tiled=True),
        lax.all_gather(w_value, "seq", axis=0, tiled=True),
    )
    projected = tuple(
        (jnp.dot(tokens, weight, preferred_element_type=jnp.float32) for weight in slices)
    )
    stacked = jnp.stack(projected)
    tail_rows = stacked[:, tok_rows - (SHORT - 1) :, :]
    prior = passed_along(tail_rows, "seq", 1)
    extended = jnp.concatenate([prior, stacked], axis=1)
    filtered = jnp.zeros_like(stacked)
    for lag in range(SHORT):
        filtered = (
            filtered
            + short_taps[:, lag, None, :]
            * extended[:, SHORT - 1 - lag : SHORT - 1 - lag + tok_rows, :]
        )
    drive = filtered[1] * filtered[2]
    positions = jnp.arange(tok_rows, dtype=jnp.int32)
    bit_count = seq_parts.bit_length() - 1
    two_slots = jnp.arange(2, dtype=jnp.int32)
    shift_cos, shift_sin = angle_table(my_index, 2 * seq_parts)
    state = jnp.stack(
        [
            jnp.stack([drive, drive * shift_cos]),
            jnp.stack([jnp.zeros_like(drive), -drive * shift_sin]),
        ]
    )
    for level in reversed(range(bit_count)):
        span = 1 << level
        partner = from_partner(state.astype(jnp.bfloat16), "seq", level).astype(state.dtype)
        is_upper = my_index >> level & 1
        turn_cos, turn_sin = angle_table(my_index % span, 2 * span)
        diff_re, diff_im = complex_mul(
            partner[0] - state[0], partner[1] - state[1], turn_cos, -turn_sin
        )
        state = jnp.where(is_upper == 1, jnp.stack([diff_re, diff_im]), state + partner)
    reversal = jnp.zeros((), jnp.int32)
    for level in range(bit_count):
        reversal = reversal + ((my_index >> level & 1) << bit_count - 1 - level)
    freq_index = 2 * reversal + two_slots
    spec_re, spec_im = (state[0], state[1])
    twist_cos, twist_sin = angle_table(freq_index[:, None] * positions[None, :], fft_len)
    twist_cos = twist_cos[:, :, None]
    twist_sin = twist_sin[:, :, None]
    spec_re, spec_im = complex_mul(spec_re, spec_im, twist_cos, -twist_sin)
    dft_cos, dft_sin = angle_table(positions[:, None] * positions[None, :], tok_rows)
    freq_re = along_rows(dft_cos, spec_re) + along_rows(dft_sin, spec_im)
    freq_im = along_rows(dft_cos, spec_im) - along_rows(dft_sin, spec_re)
    wave = freq_index[:, None] + 2 * seq_parts * positions[None, :]
    theta_cos, theta_sin = angle_table(wave, fft_len)
    half_sin = jnp.sin(wave.astype(jnp.float32) * (math.pi / fft_len))
    rates = decay_rates[:, None, None, :]
    factor = jnp.exp(-rates)
    denom_re = -jnp.expm1(-rates) + 2.0 * factor * (half_sin * half_sin)[None, :, :, None]
    denom_im = factor * theta_sin[None, :, :, None]
    whole_decay = rates * (tok_rows * seq_parts)
    is_even = (wave % 2 == 0)[None, :, :, None]
    numer = jnp.where(is_even, -jnp.expm1(-whole_decay), 1.0 + jnp.exp(-whole_decay))
    weights = residues[:, None, None, :] * numer / (denom_re * denom_re + denom_im * denom_im)
    resp_re = jnp.sum(weights * denom_re, axis=0) + skip_gain[None, None, :]
    resp_im = -jnp.sum(weights * denom_im, axis=0)
    prod_re, prod_im = complex_mul(freq_re, freq_im, resp_re, resp_im)
    back_re = along_rows(dft_cos, prod_re) - along_rows(dft_sin, prod_im)
    back_im = along_rows(dft_cos, prod_im) + along_rows(dft_sin, prod_re)
    back_re, back_im = complex_mul(back_re, back_im, twist_cos, twist_sin)
    state = jnp.stack([back_re, back_im])
    for level in range(bit_count):
        span = 1 << level
        partner = from_partner(state, "seq", level)
        is_upper = my_index >> level & 1
        turn_cos, turn_sin = angle_table(my_index % span, 2 * span)
        other_re, other_im = complex_mul(partner[0], partner[1], turn_cos, turn_sin)
        mine_re, mine_im = complex_mul(state[0], state[1], turn_cos, turn_sin)
        lower_new = jnp.stack([state[0] + other_re, state[1] + other_im])
        upper_new = jnp.stack([partner[0] - mine_re, partner[1] - mine_im])
        state = jnp.where(is_upper == 1, upper_new, lower_new)
    final_cos, final_sin = angle_table(my_index, 2 * seq_parts)
    response = (state[0, 0] + final_cos * state[0, 1] - final_sin * state[1, 1]) / fft_len
    gated = (filtered[0] * response).astype(jnp.bfloat16)
    partial_out = jnp.dot(
        gated, lax.all_gather(w_out, "seq", axis=1, tiled=True), preferred_element_type=jnp.float32
    )
    return lax.psum_scatter(partial_out.astype(jnp.bfloat16), "tp", scatter_dimension=1, tiled=True)


def solution(mesh):
    in_specs = (
        P("seq", None),
        P("seq", "tp"),
        P("seq", "tp"),
        P("seq", "tp"),
        P(None, None, "tp"),
        P(None, "tp"),
        P(None, "tp"),
        P("tp"),
        P("tp", "seq"),
    )
    out_specs = P("seq", "tp")
    return jax.shard_map(body, mesh=mesh, in_specs=in_specs, out_specs=out_specs, check_vma=False)
```

profile of v0, /device:TPU:0, one launch (start us, length us, event | category | flops | bytes accessed | tf_op | source)
XLA Modules:
  0.0 800.9 jit_solution(5146544282153188129)
XLA Ops:
  9.7 116.0 %all-gather.9.cloned.1.call-done = bf16[4096,1024]{1,0:T(8,128)(2,1)} async-done(((bf16[256,1024]{1,0:T(8,128)(2,1)}), bf16[4096,1024]{1,0:T(8,128)(2,1)}) %all-gather.9.cloned.1.call-update) | async-done | bytes 8388624 | tf_op jit(solution)/shard_map/all_gather | solution.py:47
  125.7 4.6 convolution_bitcast_fusion
  130.3 109.2 %all-gather.7.cloned.1.call-done = bf16[4096,1024]{1,0:T(8,128)(2,1)} async-done(((bf16[256,1024]{1,0:T(8,128)(2,1)}), bf16[4096,1024]{1,0:T(8,128)(2,1)}) %all-gather.7.cloned.1.call-update) | async-done | bytes 8388624 | tf_op jit(solution)/shard_map/all_gather | solution.py:46
  239.5 4.6 convolution_bitcast_fusion.1
  244.2 109.2 %all-gather.5.cloned.1.call-done = bf16[4096,1024]{1,0:T(8,128)(2,1)} async-done(((bf16[256,1024]{1,0:T(8,128)(2,1)}), bf16[4096,1024]{1,0:T(8,128)(2,1)}) %all-gather.5.cloned.1.call-update) | async-done | bytes 8388624 | tf_op jit(solution)/shard_map/all_gather | solution.py:45
  353.3 4.6 convolution_bitcast_fusion.2
  358.2 3.2 collective-permute-start
  367.0 4.3 collective-permute-start.1
  371.5 44.2 %collective-permute-done.1 = bf16[2,2,128,1024]{3,2,1,0:T(8,128)(2,1)} collective-permute-done((bf16[2,2,128,1024]{3,2,1,0:T(8,128)(2,1)}, bf16[2,2,128,1024]{3,2,1,0:T(8,128)(2,1)}, u32[]{:S(2)}, u32[]{:S(2)}) %collective-permute-start.1) | collective-permute-done | bytes 1048608 | tf_op jit(solution)/shard_map/ppermute | solution.py:23
  418.4 2.9 fusion.100
  421.8 24.2 %collective-permute-done.2 = bf16[2,2,128,1024]{3,2,1,0:T(8,128)(2,1)S(1)} collective-permute-done((bf16[2,2,128,1024]{3,2,1,0:T(8,128)(2,1)}, bf16[2,2,128,1024]{3,2,1,0:T(8,128)(2,1)S(1)}, u32[]{:S(2)}, u32[]{:S(2)}) %collective-permute-start.2) | collective-permute-done | bytes 1048608 | tf_op jit(solution)/shard_map/ppermute | solution.py:23
  446.7 3.3 fusion.99
  450.0 1.7 collective-permute-start.3
  452.5 24.8 %collective-permute-done.3 = bf16[2,2,128,1024]{3,2,1,0:T(8,128)(2,1)S(1)} collective-permute-done((bf16[2,2,128,1024]{3,2,1,0:T(8,128)(2,1)}, bf16[2,2,128,1024]{3,2,1,0:T(8,128)(2,1)S(1)}, u32[]{:S(2)}, u32[]{:S(2)}) %collective-permute-start.3) | collective-permute-done | bytes 1048608 | tf_op jit(solution)/shard_map/ppermute | solution.py:23
  478.0 3.3 fusion.98
  481.9 9.8 %multiply_reduce_fusion = (f32[2,128,1024]{2,1,0:T(8,128)}, f32[2,128,1024]{2,1,0:T(8,128)S(1)}) fusion(f32[2,128]{1,0:T(2,128)S(1)} %get-tuple-element.55, f32[16,1024]{1,0:T(8,128)S(1)} %get-tuple-element.44, f32[16,1024]{1,0:T(8,128)S(1)} %get-tuple-element.47, f32[2,128]{1,0:T(2,128)S(1)} %get-tuple-element.56, f32[16,1024]{1,0:T(8,128)S(1)} %get-tuple-element.46, ...), kind=kLoop, calls=%fused_computation.5 | loop fusion | flops 54001664 | bytes 2492672 | tf_op jit(solution)/shard_map/reduce_sum | solution.py:106
  491.6 2.5 copy.28
  495.5 20.6 %collective-permute-done.4 = bf16[2,2,128,1024]{3,2,1,0:T(8,128)(2,1)} collective-permute-done((bf16[2,2,128,1024]{3,2,1,0:T(8,128)(2,1)}, bf16[2,2,128,1024]{3,2,1,0:T(8,128)(2,1)}, u32[]{:S(2)}, u32[]{:S(2)}) %collective-permute-start.4) | collective-permute-done | bytes 1048608 | tf_op jit(solution)/shard_map/ppermute | solution.py:23
  517.9 1.8 maximum_select_fusion.3
  519.7 2.0 fusion.27
  521.8 2.0 fusion.28
  523.9 2.1 fusion.7
  526.0 2.5 multiply_subtract_fusion.1
  532.6 1.6 multiply_subtract_fusion
  535.4 54.8 %collective-permute-done.5 = f32[2,2,128,1024]{3,2,1,0:T(8,128)S(1)} collective-permute-done((f32[2,2,128,1024]{3,2,1,0:T(8,128)S(1)}, f32[2,2,128,1024]{3,2,1,0:T(8,128)S(1)}, u32[]{:S(2)}, u32[]{:S(2)}) %collective-permute-start.5) | collective-permute-done | bytes 2097184 | tf_op jit(solution)/shard_map/ppermute | solution.py:23
  593.1 45.1 %collective-permute-done.6 = f32[2,2,128,1024]{3,2,1,0:T(8,128)S(1)} collective-permute-done((f32[2,2,128,1024]{3,2,1,0:T(8,128)S(1)}, f32[2,2,128,1024]{3,2,1,0:T(8,128)S(1)}, u32[]{:S(2)}, u32[]{:S(2)}) %collective-permute-start.6) | collective-permute-done | bytes 2097184 | tf_op jit(solution)/shard_map/ppermute | solution.py:23
  641.0 44.2 %collective-permute-done.7 = f32[2,2,128,1024]{3,2,1,0:T(8,128)S(1)} collective-permute-done((f32[2,2,128,1024]{3,2,1,0:T(8,128)S(1)}, f32[2,2,128,1024]{3,2,1,0:T(8,128)S(1)}, u32[]{:S(2)}, u32[]{:S(2)}) %collective-permute-start.7) | collective-permute-done | bytes 2097184 | tf_op jit(solution)/shard_map/ppermute | solution.py:23
  686.5 2.3 collective-permute-start.8
  688.8 88.3 %collective-permute-done.8 = f32[2,2,128,1024]{3,2,1,0:T(8,128)S(1)} collective-permute-done((f32[2,2,128,1024]{3,2,1,0:T(8,128)S(1)}, f32[2,2,128,1024]{3,2,1,0:T(8,128)S(1)}, u32[]{:S(2)}, u32[]{:S(2)}) %collective-permute-start.8) | collective-permute-done | bytes 2097184 | tf_op jit(solution)/shard_map/ppermute | solution.py:23
  778.0 1.7 maximum_select_fusion.7
  779.8 6.2 convolution_convert_fusion
  786.0 8.4 %reduce-scatter.2.cloned.1.call-done = bf16[128,2048]{1,0:T(8,128)(2,1)} async-done(((bf16[128,4096]{1,0:T(8,128)(2,1)}), bf16[128,2048]{1,0:T(8,128)(2,1)}) %reduce-scatter.2.cloned.1.call-update) | async-done | bytes 524304 | tf_op jit(solution)/shard_map/reduce_scatter | solution.py:129
  (80 shorter events, 30.7 us)
Async XLA Ops:
  6.5 119.2 %copy-start = (bf16[128,4096]{1,0:T(8,128)(2,1)S(1)}, bf16[128,4096]{1,0:T(8,128)(2,1)}, u32[]{:S(2)}) copy-start(bf16[128,4096]{1,0:T(8,128)(2,1)} %param.9) | copy-start | bytes 3145732
  6.5 119.2 %all-gather.9.cloned.1.call-start = ((), (), s32[]{:S(2)}) async-start(), calls=%async_computation.3 | async-start | bytes 8912896 | tf_op jit(solution)/shard_map/all_gather | solution.py:47
  7.3 232.3 %all-gather.7.cloned.1.call-start = ((), (), s32[]{:S(2)}) async-start(), calls=%async_computation.2 | async-start | bytes 8912896 | tf_op jit(solution)/shard_map/all_gather | solution.py:46
  8.0 345.3 %all-gather.5.cloned.1.call-start = ((), (), s32[]{:S(2)}) async-start(), calls=%async_computation.1 | async-start | bytes 8912896 | tf_op jit(solution)/shard_map/all_gather | solution.py:45
  8.7 771.0 %all-gather.11.cloned.1.call-start = ((), (), s32[]{:S(2)}) async-start(), calls=%async_computation.4 | async-start | bytes 8912896 | tf_op jit(solution)/shard_map/all_gather | solution.py:127
  358.2 4.7 collective-permute-start
  363.5 1.2 copy-start.6
  364.8 1.0 copy-start.4
  367.0 48.7 %collective-permute-start.1 = (bf16[2,2,128,1024]{3,2,1,0:T(8,128)(2,1)}, bf16[2,2,128,1024]{3,2,1,0:T(8,128)(2,1)}, u32[]{:S(2)}, u32[]{:S(2)}) collective-permute-start(bf16[2,2,128,1024]{3,2,1,0:T(8,128)(2,1)} %fusion.3), channel_id=1, source_target_pairs={{0,16},{2,18},{4,20},{6,22},{8,24},{10,26},{12,28},{14,30},{16,0},... | collective-permute-start | bytes 3145736 | tf_op jit(solution)/shard_map/ppermute | solution.py:23
  417.2 1.2 copy-start.5
  421.3 25.4 %copy-start.3 = (f32[2,2,128,1024]{3,2,1,0:T(8,128)}, f32[2,2,128,1024]{3,2,1,0:T(8,128)S(1)}, u32[]{:S(2)}) copy-start(f32[2,2,128,1024]{3,2,1,0:T(8,128)S(1)} %get-tuple-element.12) | copy-start | bytes 6291460
  421.3 24.7 %collective-permute-start.2 = (bf16[2,2,128,1024]{3,2,1,0:T(8,128)(2,1)}, bf16[2,2,128,1024]{3,2,1,0:T(8,128)(2,1)S(1)}, u32[]{:S(2)}, u32[]{:S(2)}) collective-permute-start(bf16[2,2,128,1024]{3,2,1,0:T(8,128)(2,1)} %get-tuple-element.11), channel_id=1, source_target_pairs={{0,8},{2,10},{4,12},{6,14},{8,0},{10,2},{12,4},{14,6},{16,24},{18,... | collective-permute-start | bytes 3145736 | tf_op jit(solution)/shard_map/ppermute | solution.py:23
  446.7 5.7 copy-start.11
  450.0 27.9 %copy-start.2 = (f32[2,2,128,1024]{3,2,1,0:T(8,128)}, f32[2,2,128,1024]{3,2,1,0:T(8,128)S(1)}, u32[]{:S(2)}) copy-start(f32[2,2,128,1024]{3,2,1,0:T(8,128)S(1)} %get-tuple-element.10) | copy-start | bytes 6291460
  450.0 27.2 %collective-permute-start.3 = (bf16[2,2,128,1024]{3,2,1,0:T(8,128)(2,1)}, bf16[2,2,128,1024]{3,2,1,0:T(8,128)(2,1)S(1)}, u32[]{:S(2)}, u32[]{:S(2)}) collective-permute-start(bf16[2,2,128,1024]{3,2,1,0:T(8,128)(2,1)} %get-tuple-element.9), channel_id=1, source_target_pairs={{0,4},{2,6},{4,0},{6,2},{8,12},{10,14},{12,8},{14,10},{16,20},{18,... | collective-permute-start | bytes 3145736 | tf_op jit(solution)/shard_map/ppermute | solution.py:23
  451.7 342.7 %reduce-scatter.2.cloned.1.call-start = ((), (), s32[]{:S(2)}) async-start(), calls=%async_computation.5 | async-start | bytes 1572864 | tf_op jit(solution)/shard_map/reduce_scatter | solution.py:129
  477.9 3.9 copy-start.10
  481.2 34.8 %collective-permute-start.4 = (bf16[2,2,128,1024]{3,2,1,0:T(8,128)(2,1)}, bf16[2,2,128,1024]{3,2,1,0:T(8,128)(2,1)}, u32[]{:S(2)}, u32[]{:S(2)}) collective-permute-start(bf16[2,2,128,1024]{3,2,1,0:T(8,128)(2,1)} %get-tuple-element.7), channel_id=1, source_target_pairs={{0,2},{2,0},{4,6},{6,4},{8,10},{10,8},{12,14},{14,12},{16,18},{18,... | collective-permute-start | bytes 3145736 | tf_op jit(solution)/shard_map/ppermute | solution.py:23
  523.8 2.1 copy-start.8
  523.9 2.1 copy-start.9
  523.9 2.1 copy-start.12
  534.5 55.7 %collective-permute-start.5 = (f32[2,2,128,1024]{3,2,1,0:T(8,128)S(1)}, f32[2,2,128,1024]{3,2,1,0:T(8,128)S(1)}, u32[]{:S(2)}, u32[]{:S(2)}) collective-permute-start(f32[2,2,128,1024]{3,2,1,0:T(8,128)S(1)} %pad_maximum_fusion.1), channel_id=1, source_target_pairs={{0,2},{2,0},{4,6},{6,4},{8,10},{10,8},{12,14},{14,12},{16,18},{18,... | collective-permute-start | bytes 6291464 | tf_op jit(solution)/shard_map/ppermute | solution.py:23
  591.5 46.6 %collective-permute-start.6 = (f32[2,2,128,1024]{3,2,1,0:T(8,128)S(1)}, f32[2,2,128,1024]{3,2,1,0:T(8,128)S(1)}, u32[]{:S(2)}, u32[]{:S(2)}) collective-permute-start(f32[2,2,128,1024]{3,2,1,0:T(8,128)S(1)} %maximum_select_fusion.4), channel_id=1, source_target_pairs={{0,4},{2,6},{4,0},{6,2},{8,12},{10,14},{12,8},{14,10},{16,20},{18,... | collective-permute-start | bytes 6291464 | tf_op jit(solution)/shard_map/ppermute | solution.py:23
  639.5 45.7 %collective-permute-start.7 = (f32[2,2,128,1024]{3,2,1,0:T(8,128)S(1)}, f32[2,2,128,1024]{3,2,1,0:T(8,128)S(1)}, u32[]{:S(2)}, u32[]{:S(2)}) collective-permute-start(f32[2,2,128,1024]{3,2,1,0:T(8,128)S(1)} %maximum_select_fusion.5), channel_id=1, source_target_pairs={{0,8},{2,10},{4,12},{6,14},{8,0},{10,2},{12,4},{14,6},{16,24},{18,... | collective-permute-start | bytes 6291464 | tf_op jit(solution)/shard_map/ppermute | solution.py:23
  686.5 90.6 %collective-permute-start.8 = (f32[2,2,128,1024]{3,2,1,0:T(8,128)S(1)}, f32[2,2,128,1024]{3,2,1,0:T(8,128)S(1)}, u32[]{:S(2)}, u32[]{:S(2)}) collective-permute-start(f32[2,2,128,1024]{3,2,1,0:T(8,128)S(1)} %maximum_select_fusion.6), channel_id=1, source_target_pairs={{0,16},{2,18},{4,20},{6,22},{8,24},{10,26},{12,28},{14,30},{16,0},... | collective-permute-start | bytes 6291464 | tf_op jit(solution)/shard_map/ppermute | solution.py:23
  778.0 1.7 copy-start.7
  779.8 14.6 %copy-start.1 = (bf16[128,4096]{1,0:T(8,128)(2,1)S(1)}, bf16[128,4096]{1,0:T(8,128)(2,1)}, u32[]{:S(2)}) copy-start(bf16[128,4096]{1,0:T(8,128)(2,1)} %param.9) | copy-start | bytes 3145732
Sparse Core Ops, SparseCore 0:
  10.1 115.5 all-gather.8
  128.5 111.0 all-gather.6
  242.3 111.0 all-gather.4
  451.8 140.6 all-gather.10
  786.2 8.2 reduce-scatter.1
where the time goes:
time: 802 us; the launch traced here: 801 us
  waiting for transfers between devices  692 us (86%)
  other arithmetic  35.4 us (4%)
  matrix products  34.5 us (4%)
  starting transfers between devices  16.8 us (2%)
  between operations  14.3 us (2%)
    ppermute x8, waiting for transfers between devices, from_partner(): return lax.ppermute(value, axis, pairs)  346 us
    all_gather x1, waiting for transfers between devices, body(): lax.all_gather(w_value, 'seq', axis=0, tiled=True)  116 us
    all_gather x1, waiting for transfers between devices, body(): lax.all_gather(w_query, 'seq', axis=0, tiled=True)  109 us
    all_gather x1, waiting for transfers between devices, body(): lax.all_gather(w_key, 'seq', axis=0, tiled=True)  109 us
  transfers between devices with their start and end apart: 14, of which 13 were waited for; matrix products, arithmetic and copies ran while one was open for 7% of the time, Pallas kernels for 0%

commit v1 on v0

v1 whole, which is shorter than its diff:
```python
import functools

import jax
import jax.numpy as jnp
from jax import lax
from jax.experimental import pallas as pl
from jax.experimental.pallas import tpu as pltpu
from jax.sharding import PartitionSpec as P

SHORT = 3
HALO = 8
SEGMENTS = 8
BF16 = jnp.bfloat16
F32 = jnp.float32


def flipped(value, axis, mask):
    size = lax.axis_size(axis)
    return lax.ppermute(value, axis, [(i, i ^ mask) for i in range(size)])


def spread(value, axis, count):
    return [value] + [flipped(value, axis, off) for off in range(1, count)]


def dot(left, right):
    return jnp.dot(left, right, preferred_element_type=F32)


def load_projected(g, padded, own, recv, halo, groups, rows):
    padded[0:HALO, :] = halo[...]
    for block in range(groups):
        source = lax.bitwise_xor(g, jnp.int32(block))
        start = HALO + block * rows
        padded[start : start + rows, :] = own[source] + recv[source].astype(F32)


def short_filter(padded, taps, start, rows):
    total = taps[0:1, :] * padded[HALO + start : HALO + start + rows, :]
    for lag in range(1, SHORT):
        first = HALO + start - lag
        total = total + taps[lag : lag + 1, :] * padded[first : first + rows, :]
    return total


def drive_kernel(
    groups, rows, order,
    g_ref, k_own, k_recv, k_halo, v_own, v_recv, v_halo, k_taps, v_taps, rates,
    drive, entry, last, k_pad, v_pad, ends,
):
    g = g_ref[0]
    load_projected(g, k_pad, k_own, k_recv, k_halo, groups, rows)
    load_projected(g, v_pad, v_own, v_recv, v_halo, groups, rows)
    length = groups * rows
    step_rows = min(64, rows)
    for start in range(0, length, step_rows):
        drive[start : start + step_rows, :] = short_filter(
            k_pad, k_taps, start, step_rows
        ) * short_filter(v_pad, v_taps, start, step_rows)
    segment = length // SEGMENTS
    lanes = drive.shape[1]
    factors = jnp.exp(-rates[...])
    wide = [jnp.broadcast_to(factors[j : j + 1, :], (SEGMENTS, lanes)) for j in range(order)]

    def step(t, states):
        now = drive[pl.ds(t, SEGMENTS, stride=segment), :]
        return tuple(s * f + now for s, f in zip(states, wide))

    zero = jnp.zeros((SEGMENTS, lanes), F32)
    states = lax.fori_loop(0, segment, step, (zero,) * order, unroll=8)
    for j in range(order):
        ends[j] = states[j]
    whole = jnp.exp(-rates[...] * float(segment))
    running = jnp.zeros((order, lanes), F32)
    for i in range(SEGMENTS):
        entry[i] = running
        running = running * whole + ends[:, i, :]
    last[...] = running


def gate_kernel(
    groups, rows, order,
    g_ref, drive, entry, before, q_own, q_recv, q_halo, q_taps, rates, residues, skip,
    gated, q_pad, begin, response,
):
    g = g_ref[0]
    length = groups * rows
    segment = length // SEGMENTS
    lanes = drive.shape[1]
    decay = rates[...]
    for i in range(SEGMENTS):
        begin[i] = entry[i] + jnp.exp(-decay * float(segment * i)) * before[...]
    factors = jnp.exp(-decay)
    weights = residues[...]
    wide = [jnp.broadcast_to(factors[j : j + 1, :], (SEGMENTS, lanes)) for j in range(order)]
    heavy = [jnp.broadcast_to(weights[j : j + 1, :], (SEGMENTS, lanes)) for j in range(order)]
    direct = jnp.broadcast_to(skip[...], (SEGMENTS, lanes))

    def step(t, states):
        now = drive[pl.ds(t, SEGMENTS, stride=segment), :]
        states = tuple(s * f + now for s, f in zip(states, wide))
        terms = [s * w for s, w in zip(states, heavy)] + [direct * now]
        while len(terms) > 1:
            terms = [sum(terms[i : i + 2]) for i in range(0, len(terms), 2)]
        response[pl.ds(t, SEGMENTS, stride=segment), :] = terms[0]
        return states

    first = tuple(begin[:, j, :] for j in range(order))
    lax.fori_loop(0, segment, step, first, unroll=4)
    load_projected(g, q_pad, q_own, q_recv, q_halo, groups, rows)
    step_rows = min(64, rows)
    for start in range(0, length, step_rows):
        value = short_filter(q_pad, q_taps, start, step_rows) * response[start : start + step_rows, :]
        gated[start : start + step_rows, :] = value.astype(BF16)


def by_lanes(shape, lanes):
    lead = len(shape) - 1
    return pl.BlockSpec((*shape[:-1], lanes), lambda i: (0,) * lead + (i,))


def call_by_lanes(kernel, lanes, args, outs, scratch, flops):
    width = outs[0].shape[-1]
    specs = [pl.BlockSpec(memory_space=pltpu.SMEM)] + [by_lanes(a.shape, lanes) for a in args[1:]]
    moved = sum(a.size * a.dtype.itemsize for a in [*args, *outs])
    return pl.pallas_call(
        kernel,
        grid=(width // lanes,),
        in_specs=specs,
        out_specs=[by_lanes(o.shape, lanes) for o in outs],
        out_shape=outs,
        scratch_shapes=scratch,
        compiler_params=pltpu.CompilerParams(vmem_limit_bytes=32 * 1024 * 1024),
        cost_estimate=pl.CostEstimate(flops=flops, bytes_accessed=moved, transcendentals=0),
    )(*args)


def body(tokens, w_query, w_key, w_value, short_taps, decay_rates, residues, skip_gain, w_out):
    seq_parts, tp_parts = lax.axis_size("seq"), lax.axis_size("tp")
    me, core = lax.axis_index("seq"), lax.axis_index("tp")
    rows, depth = tokens.shape
    order = decay_rates.shape[0]
    groups = seq_parts // 4
    low, high = groups, 2 * groups
    h, l, g = me // high, me // low % 2, me % groups
    width = w_query.shape[1] // groups
    half = depth // 2
    share = half // tp_parts
    length = groups * rows

    def at(side):
        return lax.dynamic_slice(tokens, (0, side * half + core * share), (rows, share))

    got = flipped(at(1 - h), "seq", high)
    layers = [[h_ * high + l_ * low + i for i in range(groups)] for h_ in range(2) for l_ in range(2)]

    def weight_of(w):
        blocks = w.reshape(w.shape[0], groups, width).transpose(1, 0, 2)
        mine = lax.all_to_all(blocks, "seq", 0, 0, axis_index_groups=layers)
        mine = mine.reshape(half // 2, width)
        theirs = flipped(mine, "seq", low)
        if tp_parts == 2:
            return [jnp.where((core ^ off) == l, mine, theirs) for off in range(2)]
        both = jnp.where(
            l == 0, jnp.concatenate([mine, theirs]), jnp.concatenate([theirs, mine])
        )
        return [
            lax.dynamic_slice(both, ((core ^ off) * share, 0), (share, width))
            for off in range(tp_parts)
        ]

    weights = {name: weight_of(w) for name, w in (("v", w_value), ("k", w_key), ("q", w_query))}

    def gathered(block):
        whole = jnp.concatenate(spread(block, "seq", groups))
        return spread(whole, "tp", tp_parts)

    there, here = gathered(got), gathered(at(h))

    def projected(name):
        theirs = sum(dot(t, w) for t, w in zip(there, weights[name]))
        mine = sum(dot(t, w) for t, w in zip(here, weights[name]))
        recv = flipped(theirs.astype(BF16), "seq", high)
        shape = (groups, rows, width)
        return mine.reshape(shape), theirs.reshape(shape), recv.reshape(shape)

    parts = {name: projected(name) for name in ("v", "k", "q")}

    def halo_of(names):
        last = (groups - 1) ^ g

        def tail(which):
            return jnp.concatenate(
                [
                    lax.dynamic_index_in_dim(parts[n][which], last, 0, False)[rows - HALO :]
                    for n in names
                ],
                axis=1,
            )

        mine, theirs = tail(0), tail(1)
        near = flipped(jnp.where(l == 0, mine, theirs), "seq", low)
        far = flipped(jnp.where(l == 0, theirs, mine), "seq", low | high)
        return jnp.where((h == 0) & (l == 0), 0.0, near + far)

    kv_halo, q_halo = halo_of(("k", "v")), halo_of(("q",))
    k_halo, v_halo = kv_halo[:, :width], kv_halo[:, width:]
    first = g * width

    def channels(value):
        return lax.dynamic_slice_in_dim(value, first, width, value.ndim - 1)

    taps, rates, heights = channels(short_taps), channels(decay_rates), channels(residues)
    skip = channels(skip_gain[None, :])
    lanes = min(128, width)
    g_in = g.astype(jnp.int32).reshape(1)
    padded = pltpu.VMEM((HALO + length, lanes), F32)
    drive, entry, last = call_by_lanes(
        functools.partial(drive_kernel, groups, rows, order),
        lanes,
        (
            g_in,
            parts["k"][0], parts["k"][2], k_halo,
            parts["v"][0], parts["v"][2], v_halo,
            taps[1], taps[2], rates,
        ),
        (
            jax.ShapeDtypeStruct((length, width), F32),
            jax.ShapeDtypeStruct((SEGMENTS, order, width), F32),
            jax.ShapeDtypeStruct((order, width), F32),
        ),
        [padded, padded, pltpu.VMEM((order, SEGMENTS, lanes), F32)],
        length * width * (2 * order + 16),
    )
    layer = 2 * h + l
    before = jnp.zeros_like(last)
    for flip in range(1, 4):
        other = layer ^ flip
        sent = flipped(last, "seq", flip * low)
        gap = jnp.maximum(layer - other - 1, 0).astype(F32) * float(length)
        before = before + jnp.where(other < layer, jnp.exp(-rates * gap) * sent, 0.0)
    (gated,) = call_by_lanes(
        functools.partial(gate_kernel, groups, rows, order),
        lanes,
        (
            g_in, drive, entry, before,
            parts["q"][0], parts["q"][2], q_halo,
            taps[0], rates, heights, skip,
        ),
        (jax.ShapeDtypeStruct((length, width), BF16),),
        [
            padded,
            pltpu.VMEM((SEGMENTS, order, lanes), F32),
            pltpu.VMEM((length, lanes), F32),
        ],
        length * width * (4 * order + 16),
    )
    gated = gated.reshape(groups, rows, width)
    if tp_parts != 2:
        mine = lax.all_to_all(gated, "seq", 0, 0, axis_index_groups=layers)
        mine = mine.transpose(1, 0, 2).reshape(rows, groups * width)
        columns = lax.all_gather(w_out, "seq", axis=1, tiled=True)
        partial_out = dot(mine, columns).astype(BF16)
        return lax.psum_scatter(partial_out, "tp", scatter_dimension=1, tiled=True)
    halves = [[h_ * high + i for i in range(high)] for h_ in range(2)]
    both = lax.all_to_all(
        jnp.concatenate([gated, gated]), "seq", 0, 0, axis_index_groups=halves
    )
    both = both.reshape(2, groups, rows, width).transpose(0, 2, 1, 3)
    both = both.reshape(2 * rows, groups * width)

    def columns_of(block, masks):
        held = block[None]
        for mask in masks:
            held = jnp.concatenate([held, flipped(held, "seq", mask)])
        return held

    bits = [1 << i for i in range(groups.bit_length() - 1)]
    block = w_out.shape[1]
    outs = []
    for source, masks in ((w_out, bits), (flipped(w_out, "seq", high), bits[::-1])):
        held = columns_of(source, masks)
        offs = [0]
        for mask in masks:
            offs = offs + [off ^ mask for off in offs]
        held = held.transpose(1, 0, 2).reshape(w_out.shape[0], groups * block)
        outs.append((dot(both, held).reshape(2 * rows, groups, block), offs))

    def in_order(value, offs):
        return jnp.concatenate(
            [
                lax.dynamic_index_in_dim(
                    value, jnp.asarray(offs, jnp.int32).argsort()[n ^ g], 1, False
                )
                for n in range(groups)
            ],
            axis=1,
        )

    own_out, other_out = (in_order(value, offs) for value, offs in outs)
    keep = jnp.where(h == core, own_out, other_out)
    give = jnp.where(h == core, other_out, own_out)
    summed = (keep + flipped(give.astype(BF16), "tp", 1).astype(F32)).astype(BF16)
    summed = summed.reshape(2, rows, groups * block)
    mine = lax.dynamic_index_in_dim(summed, l, 0, False)
    theirs = flipped(lax.dynamic_index_in_dim(summed, 1 - l, 0, False), "seq", low)
    return jnp.where(
        l == 0,
        jnp.concatenate([mine, theirs], axis=1),
        jnp.concatenate([theirs, mine], axis=1),
    )


def solution(mesh):
    in_specs = (
        P("seq", None),
        P("seq", "tp"),
        P("seq", "tp"),
        P("seq", "tp"),
        P(None, None, "tp"),
        P(None, "tp"),
        P(None, "tp"),
        P("tp"),
        P("tp", "seq"),
    )
    out_specs = P("seq", "tp")
    return jax.shard_map(body, mesh=mesh, in_specs=in_specs, out_specs=out_specs, check_vma=False)
```

time: 802 us -> 204 us (0.25)
  waiting for transfers between devices: 692 us -> 83.8 us
  starting transfers between devices: 16.8 us -> 59.2 us
  other arithmetic: 35.4 us -> 9.06 us
  matrix products: 34.5 us -> 13.7 us
  local copies, waits for them, and re-layouts: 7.7 us -> 17.8 us
    all_gather x4 -> x0, waiting for transfers between devices: 334 us -> none  [the longest x1 116 us: body(): lax.all_gather(w_value, 'seq', axis=0, tiled=True)]
    ppermute x9 -> x29, waiting for transfers between devices: 347 us -> 71.6 us  [flipped(): return lax.ppermute(value, axis, [(i, i ^ mask) for i in range(size)])]
    ppermute x9 -> x29, starting transfers between devices: 16.4 us -> 41.8 us  [flipped(): return lax.ppermute(value, axis, [(i, i ^ mask) for i in range(size)])]
    dot_general x12 -> x14, matrix products: 34.5 us -> 13.7 us  [dot(): return jnp.dot(left, right, preferred_element_type=F32)]
    all_to_all x0 -> x4, starting transfers between devices: none -> 17.4 us  [the longest x3 13.7 us: weight_of(): mine = lax.all_to_all(blocks, 'seq', 0, 0, axis_index_groups=layers)]
    convert_element_type x8 -> x2, other arithmetic: 14 us -> 0.29 us  [the longest x1 0.17 us: body(): (keep + flipped(give.astype(BF16), 'tp', 1).astype(F32)).astype(BF16)]
    all_to_all x0 -> x4, waiting for transfers between devices: none -> 12.2 us  [the longest x3 12.2 us: weight_of(): mine = lax.all_to_all(blocks, 'seq', 0, 0, axis_index_groups=layers)]
    reduce_sum x1 -> x0, other arithmetic: 9.76 us -> none  [body(): resp_re = jnp.sum(weights * denom_re, axis=0) + skip_gain[None, None, :]]
  transfers between devices with their start and end apart: 14 -> 33, of which waited for: 13 -> 15; matrix products, arithmetic and copies ran while one was open for 7% -> 16% of each run, Pallas kernels for 0% -> 2%
where the time goes in v1:
time: 204 us; the launch traced here: 203 us
  waiting for transfers between devices  83.8 us (41%)
  starting transfers between devices  59.2 us (29%)
  local copies, waits for them, and re-layouts  17.8 us (9%)
  between operations  15.7 us (8%)
  matrix products  13.7 us (7%)
  other arithmetic  9.06 us (4%)
  Pallas kernels  3.78 us (2%)
    ppermute x29, waiting for transfers between devices, flipped(): return lax.ppermute(value, axis, [(i, i ^ mask) for i in range(size)])  71.6 us
    ppermute x29, starting transfers between devices, flipped(): return lax.ppermute(value, axis, [(i, i ^ mask) for i in range(size)])  41.8 us
    dot_general x14, matrix products, dot(): return jnp.dot(left, right, preferred_element_type=F32)  13.7 us
    all_to_all x3, starting transfers between devices, weight_of(): mine = lax.all_to_all(blocks, 'seq', 0, 0, axis_index_groups=layers)  13.7 us
    all_to_all x3, waiting for transfers between devices, weight_of(): mine = lax.all_to_all(blocks, 'seq', 0, 0, axis_index_groups=layers)  12.2 us
    unnamed x35, local copies, waits for them, and re-layouts  8.71 us
    concatenate x2, other arithmetic, columns_of(): held = jnp.concatenate([held, flipped(held, 'seq', mask)])  4.41 us
  transfers between devices with their start and end apart: 33, of which 15 were waited for; matrix products, arithmetic and copies ran while one was open for 16% of the time, Pallas kernels for 2%

profile of v1, /device:TPU:0, one launch (start us, length us, event | category | flops | bytes accessed | tf_op | source)
XLA Modules:
  0.0 203.0 jit_solution(17323741896161641888)
XLA Ops:
  0.0 2.1 %copy.22 = bf16[256,1024]{0,1:T(8,128)(2,1)} copy(bf16[256,1024]{1,0:T(8,128)(2,1)} %param.19) | data formatting | bytes 1048576 | tf_op args[2]
  2.1 5.3 %all-to-all-start = ((bf16[4,256,256]{1,2,0:T(8,128)(2,1)}), bf16[4,256,256]{1,2,0:T(8,128)(2,1)S(1)}, u32[]{:S(2)}, u32[]{:S(2)}) async-start(bf16[4,256,256]{1,2,0:T(8,128)(2,1)} %bitcast.2), calls=%async_computation | async-start | bytes 1048576 | tf_op jit(solution)/shard_map/all_to_all | solution.py:159
  8.2 2.9 %collective-permute-start.2 = (bf16[128,1024]{1,0:T(8,128)(2,1)S(1)}, bf16[128,1024]{1,0:T(8,128)(2,1)S(1)}, u32[]{:S(2)}, u32[]{:S(2)}) collective-permute-start(bf16[128,1024]{1,0:T(8,128)(2,1)S(1)} %get-tuple-element.38), channel_id=1, source_target_pairs={{0,6},{2,4},{4,2},{6,0},{8,14},{10,12},{12,10},{14,8},{16,22},{18,... | collective-permute-start | bytes 786440 | tf_op jit(solution)/shard_map/ppermute | solution.py:19
  12.7 8.0 %all-to-all-done = bf16[4,256,256]{1,2,0:T(8,128)(2,1)S(1)} async-done(((bf16[4,256,256]{1,2,0:T(8,128)(2,1)}), bf16[4,256,256]{1,2,0:T(8,128)(2,1)S(1)}, u32[]{:S(2)}, u32[]{:S(2)}) %all-to-all-start) | async-done | bytes 524320 | tf_op jit(solution)/shard_map/all_to_all | solution.py:159
  20.8 4.3 %all-to-all-start.1 = ((bf16[4,256,256]{1,2,0:T(8,128)(2,1)}), bf16[4,256,256]{1,2,0:T(8,128)(2,1)S(1)}, u32[]{:S(2)}, u32[]{:S(2)}) async-start(bf16[4,256,256]{1,2,0:T(8,128)(2,1)} %bitcast.8), calls=%async_computation.1 | async-start | bytes 1048576 | tf_op jit(solution)/shard_map/all_to_all | solution.py:159
  25.2 2.6 %collective-permute-start.24 = (bf16[1024,256]{0,1:T(8,128)(2,1)S(1)}, bf16[1024,256]{0,1:T(8,128)(2,1)}, u32[]{:S(2)}, u32[]{:S(2)}) collective-permute-start(bf16[1024,256]{0,1:T(8,128)(2,1)S(1)} %copy.29), channel_id=1, source_target_pairs={{0,16},{2,18},{4,20},{6,22},{8,24},{10,26},{12,28},{14,30},{16,0},... | collective-permute-start | bytes 1572872 | tf_op jit(solution)/shard_map/ppermute | solution.py:19
  32.6 22.6 %collective-permute-done.5 = bf16[128,1024]{1,0:T(8,128)(2,1)} collective-permute-done((bf16[128,1024]{1,0:T(8,128)(2,1)}, bf16[128,1024]{1,0:T(8,128)(2,1)}, u32[]{:S(2)}, u32[]{:S(2)}) %collective-permute-start.5) | collective-permute-done | bytes 262176 | tf_op jit(solution)/shard_map/ppermute | solution.py:19
  56.9 4.1 %all-to-all-start.2 = ((bf16[4,256,256]{1,2,0:T(8,128)(2,1)}), bf16[4,256,256]{1,2,0:T(8,128)(2,1)}, u32[]{:S(2)}, u32[]{:S(2)}) async-start(bf16[4,256,256]{1,2,0:T(8,128)(2,1)} %bitcast.20), calls=%async_computation.2 | async-start | bytes 1048576 | tf_op jit(solution)/shard_map/all_to_all | solution.py:159
  61.8 2.0 collective-permute-start.7
  65.3 2.8 %collective-permute-start.8 = (bf16[128,1024]{1,0:T(8,128)(2,1)}, bf16[128,1024]{1,0:T(8,128)(2,1)}, u32[]{:S(2)}, u32[]{:S(2)}) collective-permute-start(bf16[128,1024]{1,0:T(8,128)(2,1)} %collective-permute-done.5), channel_id=1, source_target_pairs={{0,6},{2,4},{4,2},{6,0},{8,14},{10,12},{12,10},{14,8},{16,22},{18,... | collective-permute-start | bytes 786440 | tf_op jit(solution)/shard_map/ppermute | solution.py:19
  71.0 4.2 %all-to-all-done.2 = bf16[4,256,256]{1,2,0:T(8,128)(2,1)} async-done(((bf16[4,256,256]{1,2,0:T(8,128)(2,1)}), bf16[4,256,256]{1,2,0:T(8,128)(2,1)}, u32[]{:S(2)}, u32[]{:S(2)}) %all-to-all-start.2) | async-done | bytes 524320 | tf_op jit(solution)/shard_map/all_to_all | solution.py:159
  77.4 3.4 %collective-permute-done.7 = bf16[128,1024]{1,0:T(8,128)(2,1)} collective-permute-done((bf16[128,1024]{1,0:T(8,128)(2,1)}, bf16[128,1024]{1,0:T(8,128)(2,1)}, u32[]{:S(2)}, u32[]{:S(2)}) %collective-permute-start.7) | collective-permute-done | bytes 262176 | tf_op jit(solution)/shard_map/ppermute | solution.py:19
  80.8 2.5 %collective-permute-start.22 = (bf16[1,1024,256]{1,2,0:T(8,128)(2,1)}, bf16[1,1024,256]{1,2,0:T(8,128)(2,1)}, u32[]{:S(2)}, u32[]{:S(2)}) collective-permute-start(bf16[1,1024,256]{1,2,0:T(8,128)(2,1)} %bitcast.138), channel_id=1, source_target_pairs={{0,2},{2,0},{4,6},{6,4},{8,10},{10,8},{12,14},{14,12},{16,18},{18,... | collective-permute-start | bytes 1572872 | tf_op jit(solution)/shard_map/ppermute | solution.py:19
  86.0 4.7 %collective-permute-done.25 = bf16[1,1024,256]{1,2,0:T(8,128)(2,1)} collective-permute-done((bf16[1,1024,256]{1,2,0:T(8,128)(2,1)}, bf16[1,1024,256]{1,2,0:T(8,128)(2,1)}, u32[]{:S(2)}, u32[]{:S(2)}) %collective-permute-start.25) | collective-permute-done | bytes 524320 | tf_op jit(solution)/shard_map/ppermute | solution.py:19
  92.3 2.3 %pad_maximum_fusion.3 = bf16[2,1024,256]{1,2,0:T(8,128)(2,1)} fusion(bf16[1,1024,256]{1,2,0:T(8,128)(2,1)} %collective-permute-done.25, bf16[1,1024,256]{1,2,0:T(8,128)(2,1)} %bitcast.45), kind=kLoop, calls=%fused_computation.21 | loop fusion | flops 524288 | bytes 2097152 | tf_op jit(solution)/shard_map/concatenate | solution.py:275
  98.8 6.7 %collective-permute-done.18 = bf16[1024,256]{1,0:T(8,128)(2,1)S(1)} collective-permute-done((bf16[1024,256]{1,0:T(8,128)(2,1)S(1)}, bf16[1024,256]{1,0:T(8,128)(2,1)S(1)}, u32[]{:S(2)}, u32[]{:S(2)}) %collective-permute-start.18) | collective-permute-done | bytes 524320 | tf_op jit(solution)/shard_map/ppermute | solution.py:19
  109.4 3.4 %collective-permute-start.10 = (bf16[512,256]{1,0:T(8,128)(2,1)S(1)}, bf16[512,256]{1,0:T(8,128)(2,1)S(1)}, u32[]{:S(2)}, u32[]{:S(2)}) collective-permute-start(bf16[512,256]{1,0:T(8,128)(2,1)S(1)} %get-tuple-element.56), channel_id=1, source_target_pairs={{0,16},{2,18},{4,20},{6,22},{8,24},{10,26},{12,28},{14,30},{16,0},... | collective-permute-start | bytes 786440 | tf_op jit(solution)/shard_map/ppermute | solution.py:19
  119.7 2.5 %collective-permute-start.20 = (f32[8,256]{1,0:T(8,128)S(1)}, f32[8,256]{1,0:T(8,128)S(1)}, u32[]{:S(2)}, u32[]{:S(2)}) collective-permute-start(f32[8,256]{1,0:T(8,128)S(1)} %get-tuple-element.36), channel_id=1, source_target_pairs={{0,8},{2,10},{4,12},{6,14},{8,0},{10,2},{12,4},{14,6},{16,24},{18,... | collective-permute-start | bytes 24584 | tf_op jit(solution)/shard_map/ppermute | solution.py:19
  122.2 2.1 %collective-permute-start.21 = (f32[8,256]{1,0:T(8,128)S(1)}, f32[8,256]{1,0:T(8,128)S(1)}, u32[]{:S(2)}, u32[]{:S(2)}) collective-permute-start(f32[8,256]{1,0:T(8,128)S(1)} %get-tuple-element.35), channel_id=1, source_target_pairs={{0,24},{2,26},{4,28},{6,30},{8,16},{10,18},{12,20},{14,22},{16,8},... | collective-permute-start | bytes 24584 | tf_op jit(solution)/shard_map/ppermute | solution.py:19
  124.3 6.2 %collective-permute-done.10 = bf16[512,256]{1,0:T(8,128)(2,1)S(1)} collective-permute-done((bf16[512,256]{1,0:T(8,128)(2,1)S(1)}, bf16[512,256]{1,0:T(8,128)(2,1)S(1)}, u32[]{:S(2)}, u32[]{:S(2)}) %collective-permute-start.10) | collective-permute-done | bytes 262176 | tf_op jit(solution)/shard_map/ppermute | solution.py:19
  130.5 2.5 %collective-permute-start.19 = (bf16[512,256]{1,0:T(8,128)(2,1)S(1)}, bf16[512,256]{1,0:T(8,128)(2,1)S(1)}, u32[]{:S(2)}, u32[]{:S(2)}) collective-permute-start(bf16[512,256]{1,0:T(8,128)(2,1)S(1)} %get-tuple-element.60), channel_id=1, source_target_pairs={{0,16},{2,18},{4,20},{6,22},{8,24},{10,26},{12,28},{14,30},{16,0},... | collective-permute-start | bytes 786440 | tf_op jit(solution)/shard_map/ppermute | solution.py:19
  133.0 9.1 %collective-permute-done.14 = bf16[512,256]{1,0:T(8,128)(2,1)S(1)} collective-permute-done((bf16[512,256]{1,0:T(8,128)(2,1)S(1)}, bf16[512,256]{1,0:T(8,128)(2,1)S(1)}, u32[]{:S(2)}, u32[]{:S(2)}) %collective-permute-start.14) | collective-permute-done | bytes 262176 | tf_op jit(solution)/shard_map/ppermute | solution.py:19
  143.5 2.5 %collective-permute-start.17 = (f32[16,256]{1,0:T(8,128)S(1)}, f32[16,256]{1,0:T(8,128)S(1)}, u32[]{:S(2)}, u32[]{:S(2)}) collective-permute-start(f32[16,256]{1,0:T(8,128)S(1)} %get-tuple-element.18), channel_id=1, source_target_pairs={{0,24},{2,26},{4,28},{6,30},{8,16},{10,18},{12,20},{14,22},{16,8},... | collective-permute-start | bytes 49160 | tf_op jit(solution)/shard_map/ppermute | solution.py:19
  146.0 2.0 collective-permute-start.15
  151.4 2.3 %shard_map.164 = bf16[512,256]{1,0:T(8,128)(2,1)S(1)} custom-call(s32[1]{0:T(128)} %bitcast.g_ref, f32[512,256]{1,0:T(8,128)S(1)} %get-tuple-element.16.drive, f32[8,16,256]{2,1,0:T(8,128)S(1)} %get-tuple-element.17.entry, f32[16,256]{1,0:T(8,128)S(1)} %select_add_fusion.before, f32[4,128,256]{2,1,0:T(8,128)S(1)} %bitcast.100, ...), custom_call_target="tpu_custom_call" | custom-call | flops 10485760 | bytes 1765380 | tf_op jit(solution)/shard_map/pallas_call | solution.py:126
  154.6 3.7 %all-to-all-start.3 = ((bf16[8,128,256]{2,1,0:T(8,128)(2,1)}), bf16[8,128,256]{2,1,0:T(8,128)(2,1)S(1)}, u32[]{:S(2)}, u32[]{:S(2)}) async-start(bf16[8,128,256]{2,1,0:T(8,128)(2,1)} %pad_maximum_fusion.5), calls=%async_computation.3 | async-start | bytes 1048576 | tf_op jit(solution)/shard_map/all_to_all | solution.py:266
  158.3 2.1 %pad_maximum_fusion.1 = bf16[2,1024,256]{1,2,0:T(8,128)(2,1)} fusion(bf16[1,1024,256]{1,2,0:T(8,128)(2,1)} %collective-permute-done.22, bf16[1,1024,256]{1,2,0:T(8,128)(2,1)S(1)} %bitcast.139), kind=kLoop, calls=%fused_computation.19 | loop fusion | flops 524288 | bytes 2097152 | tf_op jit(solution)/shard_map/concatenate | solution.py:275
  179.7 1.9 fusion.5
  182.3 6.4 %collective-permute-done.23 = bf16[2,1024,256]{1,2,0:T(8,128)(2,1)} collective-permute-done((bf16[2,1024,256]{1,2,0:T(8,128)(2,1)}, bf16[2,1024,256]{1,2,0:T(8,128)(2,1)}, u32[]{:S(2)}, u32[]{:S(2)}) %collective-permute-start.23) | collective-permute-done | bytes 1048608 | tf_op jit(solution)/shard_map/ppermute | solution.py:19
  188.6 2.1 %fusion = f32[256,4,256]{0,2,1:T(8,128)S(1)} fusion(bf16[256,1024,1]{1,0,2:T(8,128)(2,1)S(1)} %reshape.103, bf16[2,1024,256]{1,2,0:T(8,128)(2,1)} %collective-permute-done.23, bf16[1,1024,256]{1,2,0:T(8,128)(2,1)} %collective-permute-done.22, bf16[1,1024,256]{1,2,0:T(8,128)(2,1)S(1)} %bitcast.140), kind=kOutput, calls=%fused_computation.1 | convolution fusion | flops 543162368 | bytes 3670016 | tf_op jit(solution)/shard_map/dot_general | solution.py:27
  191.6 1.9 collective-permute-done.27
  195.2 6.9 %collective-permute-done.28 = bf16[128,1024]{1,0:T(8,128)(2,1)S(1)} collective-permute-done((bf16[128,1024]{1,0:T(8,128)(2,1)S(1)}, bf16[128,1024]{1,0:T(8,128)(2,1)S(1)}, u32[]{:S(2)}, u32[]{:S(2)}) %collective-permute-start.28) | collective-permute-done | bytes 262176 | tf_op jit(solution)/shard_map/ppermute | solution.py:19
  (125 shorter events, 49.3 us)
Async XLA Ops:
  2.1 18.6 %all-to-all-start = ((bf16[4,256,256]{1,2,0:T(8,128)(2,1)}), bf16[4,256,256]{1,2,0:T(8,128)(2,1)S(1)}, u32[]{:S(2)}, u32[]{:S(2)}) async-start(bf16[4,256,256]{1,2,0:T(8,128)(2,1)} %bitcast.2), calls=%async_computation | async-start | bytes 1048576 | tf_op jit(solution)/shard_map/all_to_all | solution.py:159
  8.2 20.0 %collective-permute-start.2 = (bf16[128,1024]{1,0:T(8,128)(2,1)S(1)}, bf16[128,1024]{1,0:T(8,128)(2,1)S(1)}, u32[]{:S(2)}, u32[]{:S(2)}) collective-permute-start(bf16[128,1024]{1,0:T(8,128)(2,1)S(1)} %get-tuple-element.38), channel_id=1, source_target_pairs={{0,6},{2,4},{4,2},{6,0},{8,14},{10,12},{12,10},{14,8},{16,22},{18,... | collective-permute-start | bytes 786440 | tf_op jit(solution)/shard_map/ppermute | solution.py:19
  11.1 18.0 %collective-permute-start.1 = (bf16[128,1024]{1,0:T(8,128)(2,1)S(1)}, bf16[128,1024]{1,0:T(8,128)(2,1)S(1)}, u32[]{:S(2)}, u32[]{:S(2)}) collective-permute-start(bf16[128,1024]{1,0:T(8,128)(2,1)S(1)} %get-tuple-element.38), channel_id=1, source_target_pairs={{0,4},{2,6},{4,0},{6,2},{8,12},{10,14},{12,8},{14,10},{16,20},{18,... | collective-permute-start | bytes 786440 | tf_op jit(solution)/shard_map/ppermute | solution.py:19
  11.7 17.4 %collective-permute-start = (bf16[128,1024]{1,0:T(8,128)(2,1)S(1)}, bf16[128,1024]{1,0:T(8,128)(2,1)S(1)}, u32[]{:S(2)}, u32[]{:S(2)}) collective-permute-start(bf16[128,1024]{1,0:T(8,128)(2,1)S(1)} %get-tuple-element.38), channel_id=1, source_target_pairs={{0,2},{2,0},{4,6},{6,4},{8,10},{10,8},{12,14},{14,12},{16,18},{18,... | collective-permute-start | bytes 786440 | tf_op jit(solution)/shard_map/ppermute | solution.py:19
  20.8 36.2 %all-to-all-start.1 = ((bf16[4,256,256]{1,2,0:T(8,128)(2,1)}), bf16[4,256,256]{1,2,0:T(8,128)(2,1)S(1)}, u32[]{:S(2)}, u32[]{:S(2)}) async-start(bf16[4,256,256]{1,2,0:T(8,128)(2,1)} %bitcast.8), calls=%async_computation.1 | async-start | bytes 1048576 | tf_op jit(solution)/shard_map/all_to_all | solution.py:159
  25.2 38.5 %collective-permute-start.24 = (bf16[1024,256]{0,1:T(8,128)(2,1)S(1)}, bf16[1024,256]{0,1:T(8,128)(2,1)}, u32[]{:S(2)}, u32[]{:S(2)}) collective-permute-start(bf16[1024,256]{0,1:T(8,128)(2,1)S(1)} %copy.29), channel_id=1, source_target_pairs={{0,16},{2,18},{4,20},{6,22},{8,24},{10,26},{12,28},{14,30},{16,0},... | collective-permute-start | bytes 1572872 | tf_op jit(solution)/shard_map/ppermute | solution.py:19
  27.8 27.4 %collective-permute-start.5 = (bf16[128,1024]{1,0:T(8,128)(2,1)}, bf16[128,1024]{1,0:T(8,128)(2,1)}, u32[]{:S(2)}, u32[]{:S(2)}) collective-permute-start(bf16[128,1024]{1,0:T(8,128)(2,1)} %get-tuple-element.37), channel_id=1, source_target_pairs={{0,16},{2,18},{4,20},{6,22},{8,24},{10,26},{12,28},{14,30},{16,0},... | collective-permute-start | bytes 786440 | tf_op jit(solution)/shard_map/ppermute | solution.py:19
  31.6 63.1 %collective-permute-start.4 = (bf16[512,1024]{1,0:T(8,128)(2,1)}, bf16[512,1024]{1,0:T(8,128)(2,1)S(1)}, u32[]{:S(2)}, u32[]{:S(2)}) collective-permute-start(bf16[512,1024]{1,0:T(8,128)(2,1)} %pad_maximum_fusion), channel_id=1, source_target_pairs={{0,1},{1,0},{2,3},{3,2},{4,5},{5,4},{6,7},{7,6},{8,9},{9,8},{10,11... | collective-permute-start | bytes 3145736 | tf_op jit(solution)/shard_map/ppermute | solution.py:19
  55.2 14.0 %collective-permute-start.6 = (bf16[128,1024]{1,0:T(8,128)(2,1)}, bf16[128,1024]{1,0:T(8,128)(2,1)}, u32[]{:S(2)}, u32[]{:S(2)}) collective-permute-start(bf16[128,1024]{1,0:T(8,128)(2,1)} %collective-permute-done.5), channel_id=1, source_target_pairs={{0,2},{2,0},{4,6},{6,4},{8,10},{10,8},{12,14},{14,12},{16,18},{18,... | collective-permute-start | bytes 786440 | tf_op jit(solution)/shard_map/ppermute | solution.py:19
  56.9 18.3 %all-to-all-start.2 = ((bf16[4,256,256]{1,2,0:T(8,128)(2,1)}), bf16[4,256,256]{1,2,0:T(8,128)(2,1)}, u32[]{:S(2)}, u32[]{:S(2)}) async-start(bf16[4,256,256]{1,2,0:T(8,128)(2,1)} %bitcast.20), calls=%async_computation.2 | async-start | bytes 1048576 | tf_op jit(solution)/shard_map/all_to_all | solution.py:159
  61.8 19.0 %collective-permute-start.7 = (bf16[128,1024]{1,0:T(8,128)(2,1)}, bf16[128,1024]{1,0:T(8,128)(2,1)}, u32[]{:S(2)}, u32[]{:S(2)}) collective-permute-start(bf16[128,1024]{1,0:T(8,128)(2,1)} %collective-permute-done.5), channel_id=1, source_target_pairs={{0,4},{2,6},{4,0},{6,2},{8,12},{10,14},{12,8},{14,10},{16,20},{18,... | collective-permute-start | bytes 786440 | tf_op jit(solution)/shard_map/ppermute | solution.py:19
  63.8 26.9 %collective-permute-start.25 = (bf16[1,1024,256]{1,2,0:T(8,128)(2,1)}, bf16[1,1024,256]{1,2,0:T(8,128)(2,1)}, u32[]{:S(2)}, u32[]{:S(2)}) collective-permute-start(bf16[1,1024,256]{1,2,0:T(8,128)(2,1)} %bitcast.45), channel_id=1, source_target_pairs={{0,4},{2,6},{4,0},{6,2},{8,12},{10,14},{12,8},{14,10},{16,20},{18,... | collective-permute-start | bytes 1572872 | tf_op jit(solution)/shard_map/ppermute | solution.py:19
  65.3 18.9 %collective-permute-start.8 = (bf16[128,1024]{1,0:T(8,128)(2,1)}, bf16[128,1024]{1,0:T(8,128)(2,1)}, u32[]{:S(2)}, u32[]{:S(2)}) collective-permute-start(bf16[128,1024]{1,0:T(8,128)(2,1)} %collective-permute-done.5), channel_id=1, source_target_pairs={{0,6},{2,4},{4,2},{6,0},{8,14},{10,12},{12,10},{14,8},{16,22},{18,... | collective-permute-start | bytes 786440 | tf_op jit(solution)/shard_map/ppermute | solution.py:19
  69.2 25.4 %collective-permute-start.3 = (bf16[1024,256]{1,0:T(8,128)(2,1)}, bf16[1024,256]{1,0:T(8,128)(2,1)}, u32[]{:S(2)}, u32[]{:S(2)}) collective-permute-start(bf16[1024,256]{1,0:T(8,128)(2,1)} %bitcast.3), channel_id=1, source_target_pairs={{0,8},{2,10},{4,12},{6,14},{8,0},{10,2},{12,4},{14,6},{16,24},{18,... | collective-permute-start | bytes 1572872 | tf_op jit(solution)/shard_map/ppermute | solution.py:19
  80.8 77.5 %collective-permute-start.22 = (bf16[1,1024,256]{1,2,0:T(8,128)(2,1)}, bf16[1,1024,256]{1,2,0:T(8,128)(2,1)}, u32[]{:S(2)}, u32[]{:S(2)}) collective-permute-start(bf16[1,1024,256]{1,2,0:T(8,128)(2,1)} %bitcast.138), channel_id=1, source_target_pairs={{0,2},{2,0},{4,6},{6,4},{8,10},{10,8},{12,14},{14,12},{16,18},{18,... | collective-permute-start | bytes 1572872 | tf_op jit(solution)/shard_map/ppermute | solution.py:19
  84.3 13.6 %collective-permute-start.11 = (bf16[1024,256]{1,0:T(8,128)(2,1)S(1)}, bf16[1024,256]{1,0:T(8,128)(2,1)S(1)}, u32[]{:S(2)}, u32[]{:S(2)}) collective-permute-start(bf16[1024,256]{1,0:T(8,128)(2,1)S(1)} %bitcast.114), channel_id=1, source_target_pairs={{0,8},{2,10},{4,12},{6,14},{8,0},{10,2},{12,4},{14,6},{16,24},{18,... | collective-permute-start | bytes 1572872 | tf_op jit(solution)/shard_map/ppermute | solution.py:19
  90.6 14.8 %collective-permute-start.18 = (bf16[1024,256]{1,0:T(8,128)(2,1)S(1)}, bf16[1024,256]{1,0:T(8,128)(2,1)S(1)}, u32[]{:S(2)}, u32[]{:S(2)}) collective-permute-start(bf16[1024,256]{1,0:T(8,128)(2,1)S(1)} %bitcast.109), channel_id=1, source_target_pairs={{0,8},{2,10},{4,12},{6,14},{8,0},{10,2},{12,4},{14,6},{16,24},{18,... | collective-permute-start | bytes 1572872 | tf_op jit(solution)/shard_map/ppermute | solution.py:19
  94.6 11.7 %collective-permute-start.9 = (bf16[512,1024]{1,0:T(8,128)(2,1)S(1)}, bf16[512,1024]{1,0:T(8,128)(2,1)S(1)}, u32[]{:S(2)}, u32[]{:S(2)}) collective-permute-start(bf16[512,1024]{1,0:T(8,128)(2,1)S(1)} %constant_dynamic-update-slice_fusion), channel_id=1, source_target_pairs={{0,1},{1,0},{2,3},{3,2},{4,5},{5,4},{6,7},{7,6},{8,9},{9,8},{10,11... | collective-permute-start | bytes 3145736 | tf_op jit(solution)/shard_map/ppermute | solution.py:19
  109.4 21.1 %collective-permute-start.10 = (bf16[512,256]{1,0:T(8,128)(2,1)S(1)}, bf16[512,256]{1,0:T(8,128)(2,1)S(1)}, u32[]{:S(2)}, u32[]{:S(2)}) collective-permute-start(bf16[512,256]{1,0:T(8,128)(2,1)S(1)} %get-tuple-element.56), channel_id=1, source_target_pairs={{0,16},{2,18},{4,20},{6,22},{8,24},{10,26},{12,28},{14,30},{16,0},... | collective-permute-start | bytes 786440 | tf_op jit(solution)/shard_map/ppermute | solution.py:19
  113.8 5.9 %collective-permute-start.12 = (f32[8,512]{1,0:T(8,128)S(1)}, f32[8,512]{1,0:T(8,128)S(1)}, u32[]{:S(2)}, u32[]{:S(2)}) collective-permute-start(f32[8,512]{1,0:T(8,128)S(1)} %get-tuple-element.45), channel_id=1, source_target_pairs={{0,8},{2,10},{4,12},{6,14},{8,0},{10,2},{12,4},{14,6},{16,24},{18,... | collective-permute-start | bytes 49160 | tf_op jit(solution)/shard_map/ppermute | solution.py:19
  115.6 6.6 %collective-permute-start.13 = (f32[8,512]{1,0:T(8,128)S(1)}, f32[8,512]{1,0:T(8,128)S(1)}, u32[]{:S(2)}, u32[]{:S(2)}) collective-permute-start(f32[8,512]{1,0:T(8,128)S(1)} %get-tuple-element.44), channel_id=1, source_target_pairs={{0,24},{2,26},{4,28},{6,30},{8,16},{10,18},{12,20},{14,22},{16,8},... | collective-permute-start | bytes 49160 | tf_op jit(solution)/shard_map/ppermute | solution.py:19
  115.6 26.5 %collective-permute-start.14 = (bf16[512,256]{1,0:T(8,128)(2,1)S(1)}, bf16[512,256]{1,0:T(8,128)(2,1)S(1)}, u32[]{:S(2)}, u32[]{:S(2)}) collective-permute-start(bf16[512,256]{1,0:T(8,128)(2,1)S(1)} %get-tuple-element.58), channel_id=1, source_target_pairs={{0,16},{2,18},{4,20},{6,22},{8,24},{10,26},{12,28},{14,30},{16,0},... | collective-permute-start | bytes 786440 | tf_op jit(solution)/shard_map/ppermute | solution.py:19
  119.7 26.3 %collective-permute-start.20 = (f32[8,256]{1,0:T(8,128)S(1)}, f32[8,256]{1,0:T(8,128)S(1)}, u32[]{:S(2)}, u32[]{:S(2)}) collective-permute-start(f32[8,256]{1,0:T(8,128)S(1)} %get-tuple-element.36), channel_id=1, source_target_pairs={{0,8},{2,10},{4,12},{6,14},{8,0},{10,2},{12,4},{14,6},{16,24},{18,... | collective-permute-start | bytes 24584 | tf_op jit(solution)/shard_map/ppermute | solution.py:19
  122.2 23.9 %collective-permute-start.21 = (f32[8,256]{1,0:T(8,128)S(1)}, f32[8,256]{1,0:T(8,128)S(1)}, u32[]{:S(2)}, u32[]{:S(2)}) collective-permute-start(f32[8,256]{1,0:T(8,128)S(1)} %get-tuple-element.35), channel_id=1, source_target_pairs={{0,24},{2,26},{4,28},{6,30},{8,16},{10,18},{12,20},{14,22},{16,8},... | collective-permute-start | bytes 24584 | tf_op jit(solution)/shard_map/ppermute | solution.py:19
  130.5 20.9 %collective-permute-start.19 = (bf16[512,256]{1,0:T(8,128)(2,1)S(1)}, bf16[512,256]{1,0:T(8,128)(2,1)S(1)}, u32[]{:S(2)}, u32[]{:S(2)}) collective-permute-start(bf16[512,256]{1,0:T(8,128)(2,1)S(1)} %get-tuple-element.60), channel_id=1, source_target_pairs={{0,16},{2,18},{4,20},{6,22},{8,24},{10,26},{12,28},{14,30},{16,0},... | collective-permute-start | bytes 786440 | tf_op jit(solution)/shard_map/ppermute | solution.py:19
  143.5 5.7 %collective-permute-start.17 = (f32[16,256]{1,0:T(8,128)S(1)}, f32[16,256]{1,0:T(8,128)S(1)}, u32[]{:S(2)}, u32[]{:S(2)}) collective-permute-start(f32[16,256]{1,0:T(8,128)S(1)} %get-tuple-element.18), channel_id=1, source_target_pairs={{0,24},{2,26},{4,28},{6,30},{8,16},{10,18},{12,20},{14,22},{16,8},... | collective-permute-start | bytes 49160 | tf_op jit(solution)/shard_map/ppermute | solution.py:19
  146.0 4.6 %collective-permute-start.16 = (f32[16,256]{1,0:T(8,128)S(1)}, f32[16,256]{1,0:T(8,128)S(1)}, u32[]{:S(2)}, u32[]{:S(2)}) collective-permute-start(f32[16,256]{1,0:T(8,128)S(1)} %get-tuple-element.18), channel_id=1, source_target_pairs={{0,16},{2,18},{4,20},{6,22},{8,24},{10,26},{12,28},{14,30},{16,0},... | collective-permute-start | bytes 49160 | tf_op jit(solution)/shard_map/ppermute | solution.py:19
  146.0 4.6 %collective-permute-start.15 = (f32[16,256]{1,0:T(8,128)S(1)}, f32[16,256]{1,0:T(8,128)S(1)}, u32[]{:S(2)}, u32[]{:S(2)}) collective-permute-start(f32[16,256]{1,0:T(8,128)S(1)} %get-tuple-element.18), channel_id=1, source_target_pairs={{0,8},{2,10},{4,12},{6,14},{8,0},{10,2},{12,4},{14,6},{16,24},{18,... | collective-permute-start | bytes 49160 | tf_op jit(solution)/shard_map/ppermute | solution.py:19
  149.2 30.4 %collective-permute-start.26 = (bf16[2,1024,256]{1,2,0:T(8,128)(2,1)}, bf16[2,1024,256]{1,2,0:T(8,128)(2,1)S(1)}, u32[]{:S(2)}, u32[]{:S(2)}) collective-permute-start(bf16[2,1024,256]{1,2,0:T(8,128)(2,1)} %pad_maximum_fusion.3), channel_id=1, source_target_pairs={{0,2},{2,0},{4,6},{6,4},{8,10},{10,8},{12,14},{14,12},{16,18},{18,... | collective-permute-start | bytes 3145736 | tf_op jit(solution)/shard_map/ppermute | solution.py:19
  154.6 24.3 %all-to-all-start.3 = ((bf16[8,128,256]{2,1,0:T(8,128)(2,1)}), bf16[8,128,256]{2,1,0:T(8,128)(2,1)S(1)}, u32[]{:S(2)}, u32[]{:S(2)}) async-start(bf16[8,128,256]{2,1,0:T(8,128)(2,1)} %pad_maximum_fusion.5), calls=%async_computation.3 | async-start | bytes 1048576 | tf_op jit(solution)/shard_map/all_to_all | solution.py:266
  160.4 28.2 %collective-permute-start.23 = (bf16[2,1024,256]{1,2,0:T(8,128)(2,1)}, bf16[2,1024,256]{1,2,0:T(8,128)(2,1)}, u32[]{:S(2)}, u32[]{:S(2)}) collective-permute-start(bf16[2,1024,256]{1,2,0:T(8,128)(2,1)} %pad_maximum_fusion.1), channel_id=1, source_target_pairs={{0,4},{2,6},{4,0},{6,2},{8,12},{10,14},{12,8},{14,10},{16,20},{18,... | collective-permute-start | bytes 3145736 | tf_op jit(solution)/shard_map/ppermute | solution.py:19
  193.7 8.4 %collective-permute-start.28 = (bf16[128,1024]{1,0:T(8,128)(2,1)S(1)}, bf16[128,1024]{1,0:T(8,128)(2,1)S(1)}, u32[]{:S(2)}, u32[]{:S(2)}) collective-permute-start(bf16[128,1024]{1,0:T(8,128)(2,1)S(1)} %get-tuple-element.40), channel_id=1, source_target_pairs={{0,8},{2,10},{4,12},{6,14},{8,0},{10,2},{12,4},{14,6},{16,24},{18,... | collective-permute-start | bytes 786440 | tf_op jit(solution)/shard_map/ppermute | solution.py:19
  (15 other events, 161.9 us)

commit v2 on v1

--- a/solution.py
+++ b/solution.py
@@ -21,6 +21,29 @@
 
 def spread(value, axis, count):
     return [value] + [flipped(value, axis, off) for off in range(1, count)]
+
+
+def swapped(blocks, groups):
+    return lax.all_to_all(blocks, "seq", 0, 0, axis_index_groups=groups)
+
+
+def after(value, *others):
+    return lax.optimization_barrier((value, *others))[0]
+
+
+def together(*values):
+    return lax.optimization_barrier(values)
+
+
+def in_order(blocks, g):
+    count = len(blocks)
+    ordered = []
+    for n in range(count):
+        block = blocks[n]
+        for value in range(1, count):
+            block = jnp.where(g == value, blocks[n ^ value], block)
+        ordered.append(block)
+    return ordered
 
 
 def dot(left, right):
@@ -147,68 +170,134 @@
     half = depth // 2
     share = half // tp_parts
     length = groups * rows
+    layers = [[layer * groups + i for i in range(groups)] for layer in range(4)]
+    halves = [[side * high + i for i in range(high)] for side in range(2)]
 
     def at(side):
         return lax.dynamic_slice(tokens, (0, side * half + core * share), (rows, share))
 
-    got = flipped(at(1 - h), "seq", high)
-    layers = [[h_ * high + l_ * low + i for i in range(groups)] for h_ in range(2) for l_ in range(2)]
-
-    def weight_of(w):
-        blocks = w.reshape(w.shape[0], groups, width).transpose(1, 0, 2)
-        mine = lax.all_to_all(blocks, "seq", 0, 0, axis_index_groups=layers)
-        mine = mine.reshape(half // 2, width)
-        theirs = flipped(mine, "seq", low)
+    def block_of(w, off):
+        return lax.dynamic_slice_in_dim(w, (g ^ off) * width, width, 1)
+
+    def weight_of(mine, theirs):
         if tp_parts == 2:
             return [jnp.where((core ^ off) == l, mine, theirs) for off in range(2)]
         both = jnp.where(
             l == 0, jnp.concatenate([mine, theirs]), jnp.concatenate([theirs, mine])
         )
         return [
-            lax.dynamic_slice(both, ((core ^ off) * share, 0), (share, width))
+            lax.dynamic_slice(both, ((core ^ off) * share, 0), (share, mine.shape[1]))
             for off in range(tp_parts)
         ]
 
-    weights = {name: weight_of(w) for name, w in (("v", w_value), ("k", w_key), ("q", w_query))}
-
-    def gathered(block):
-        whole = jnp.concatenate(spread(block, "seq", groups))
-        return spread(whole, "tp", tp_parts)
-
-    there, here = gathered(got), gathered(at(h))
-
-    def projected(name):
-        theirs = sum(dot(t, w) for t, w in zip(there, weights[name]))
-        mine = sum(dot(t, w) for t, w in zip(here, weights[name]))
-        recv = flipped(theirs.astype(BF16), "seq", high)
-        shape = (groups, rows, width)
-        return mine.reshape(shape), theirs.reshape(shape), recv.reshape(shape)
-
-    parts = {name: projected(name) for name in ("v", "k", "q")}
-
-    def halo_of(names):
+    def columns_of(block, masks):
+        held, offs = block[None], [0]
+        for mask in masks:
+            held = jnp.concatenate([held, flipped(held, "seq", mask)])
+            offs = offs + [off ^ mask for off in offs]
+        ordered = in_order([held[offs.index(off)] for off in range(groups)], g)
+        return jnp.concatenate(ordered, axis=1)
+
+    got = flipped(at(1 - h), "seq", high)
+    flat_vk = together(
+        *(
+            jnp.concatenate([block_of(w, off) for w in (w_value, w_key)], axis=1)
+            for off in range(groups)
+        )
+    )
+    flat_q = together(*(block_of(w_query, off) for off in range(groups)))
+
+    def round_layer(blocks):
+        return [blocks[0]] + [flipped(blocks[off], "seq", off) for off in range(1, groups)]
+
+    came_vk, came_q = round_layer(flat_vk), round_layer(flat_q)
+    out_depth = w_out.shape[0] // 2
+    far_first = flipped(w_out[:out_depth], "seq", high)
+    got, far_first, *came = together(got, far_first, *came_vk, *came_q)
+    mine_vk = jnp.concatenate(in_order(came[:groups], g))
+    mine_q = jnp.concatenate(in_order(came[groups:], g))
+
+    def weight_of(mine, theirs):
+        if tp_parts == 2:
+            return [jnp.where((core ^ off) == l, mine, theirs) for off in range(2)]
+        both = jnp.where(
+            l == 0, jnp.concatenate([mine, theirs]), jnp.concatenate([theirs, mine])
+        )
+        return [
+            lax.dynamic_slice(both, ((core ^ off) * share, 0), (share, mine.shape[1]))
+            for off in range(tp_parts)
+        ]
+
+    def columns_of(block, masks):
+        held, offs = block[None], [0]
+        for mask in masks:
+            held = jnp.concatenate([held, flipped(held, "seq", mask)])
+            offs = offs + [off ^ mask for off in offs]
+        ordered = in_order([held[offs.index(off)] for off in range(groups)], g)
+        return jnp.concatenate(ordered, axis=1)
+
+    got = flipped(at(1 - h), "seq", high)
+    flat = together(
+        *(
+            jnp.concatenate([block_of(w, off) for w in (w_value, w_key, w_query)], axis=1)
+            for off in range(groups)
+        )
+    )
+    came = [flat[0]] + [flipped(flat[off], "seq", off) for off in range(1, groups)]
+    out_depth = w_out.shape[0] // 2
+    far_first = flipped(w_out[:out_depth], "seq", high)
+
+    theirs_vk = flipped(mine_vk, "seq", low)
+    far_last = flipped(after(w_out[out_depth:], got), "seq", high)
+    *there, far_last = together(*spread(got, "seq", groups), far_last)
+    here = spread(after(at(h), there[0]), "seq", groups)
+    there = spread(jnp.concatenate(there), "tp", tp_parts)
+    theirs_vk, mine_q, *both = together(theirs_vk, mine_q, *there, *here)
+    there, here = both[:tp_parts], both[tp_parts:]
+
+    def partial_sums(shares, weights):
+        return sum(dot(t, w) for t, w in zip(shares, weights))
+
+    def sent_over(value):
+        return flipped(value.astype(BF16), "seq", high)
+
+    def rows_before(mine, theirs):
         last = (groups - 1) ^ g
 
-        def tail(which):
-            return jnp.concatenate(
-                [
-                    lax.dynamic_index_in_dim(parts[n][which], last, 0, False)[rows - HALO :]
-                    for n in names
-                ],
-                axis=1,
-            )
-
-        mine, theirs = tail(0), tail(1)
+        def tail(value):
+            value = value.reshape(groups, rows, -1)
+            return lax.dynamic_index_in_dim(value, last, 0, False)[rows - HALO :]
+
+        mine, theirs = tail(mine), tail(theirs)
         near = flipped(jnp.where(l == 0, mine, theirs), "seq", low)
         far = flipped(jnp.where(l == 0, theirs, mine), "seq", low | high)
         return jnp.where((h == 0) & (l == 0), 0.0, near + far)
 
-    kv_halo, q_halo = halo_of(("k", "v")), halo_of(("q",))
-    k_halo, v_halo = kv_halo[:, :width], kv_halo[:, width:]
-    first = g * width
+    weights_vk = weight_of(mine_vk, theirs_vk)
+    there_vk = partial_sums(there, weights_vk)
+    recv_vk = sent_over(there_vk)
+    here = spread(jnp.concatenate(here), "tp", tp_parts)
+    theirs_q = flipped(after(mine_q, there_vk), "seq", low)
+    here_vk = partial_sums(here, weights_vk)
+    vk_halo = rows_before(here_vk, there_vk)
+    recv_vk, theirs_q, vk_halo, *here = together(recv_vk, theirs_q, vk_halo, *here)
+
+    weights_q = weight_of(mine_q, theirs_q)
+    there_q = partial_sums(there, weights_q)
+    recv_q = sent_over(there_q)
+    here_q = partial_sums(here, weights_q)
+    q_halo = rows_before(here_q, there_q)
+
+    def named(vk, q):
+        shape = (groups, rows, width)
+        return {"v": vk[:, :width].reshape(shape), "k": vk[:, width:].reshape(shape), "q": q.reshape(shape)}
+
+    here_parts, recv_parts = named(here_vk, here_q), named(recv_vk, recv_q)
+    parts = {n: (here_parts[n], None, recv_parts[n]) for n in ("v", "k", "q")}
+    v_halo, k_halo = vk_halo[:, :width], vk_halo[:, width:]
 
     def channels(value):
-        return lax.dynamic_slice_in_dim(value, first, width, value.ndim - 1)
+        return lax.dynamic_slice_in_dim(value, g * width, width, value.ndim - 1)
 
     taps, rates, heights = channels(short_taps), channels(decay_rates), channels(residues)
     skip = channels(skip_gain[None, :])
@@ -232,6 +321,13 @@
         [padded, padded, pltpu.VMEM((order, SEGMENTS, lanes), F32)],
         length * width * (2 * order + 16),
     )
+    if tp_parts == 2:
+        bits = [1 << i for i in range(groups.bit_length() - 1)]
+        own_columns = columns_of(after(w_out, there_vk), bits)
+        far_columns = columns_of(after(jnp.concatenate([far_first, far_last]), there_vk), bits[::-1])
+        keep_columns = jnp.where(h == core, own_columns, far_columns)
+        give_columns = jnp.where(h == core, far_columns, own_columns)
+        before_gate = (keep_columns, give_columns)
     layer = 2 * h + l
     before = jnp.zeros_like(last)
     for flip in range(1, 4):
@@ -239,6 +335,8 @@
         sent = flipped(last, "seq", flip * low)
         gap = jnp.maximum(layer - other - 1, 0).astype(F32) * float(length)
         before = before + jnp.where(other < layer, jnp.exp(-rates * gap) * sent, 0.0)
+    if tp_parts == 2:
+        before, keep_columns, give_columns = together(before, *before_gate)
     (gated,) = call_by_lanes(
         functools.partial(gate_kernel, groups, rows, order),
         lanes,
@@ -257,57 +355,26 @@
     )
     gated = gated.reshape(groups, rows, width)
     if tp_parts != 2:
-        mine = lax.all_to_all(gated, "seq", 0, 0, axis_index_groups=layers)
-        mine = mine.transpose(1, 0, 2).reshape(rows, groups * width)
+        mine = swapped(gated, layers).transpose(1, 0, 2).reshape(rows, groups * width)
         columns = lax.all_gather(w_out, "seq", axis=1, tiled=True)
         partial_out = dot(mine, columns).astype(BF16)
         return lax.psum_scatter(partial_out, "tp", scatter_dimension=1, tiled=True)
-    halves = [[h_ * high + i for i in range(high)] for h_ in range(2)]
-    both = lax.all_to_all(
-        jnp.concatenate([gated, gated]), "seq", 0, 0, axis_index_groups=halves
+
+    both = swapped(
+        jnp.concatenate([gated, gated]), halves
     )
     both = both.reshape(2, groups, rows, width).transpose(0, 2, 1, 3)
     both = both.reshape(2 * rows, groups * width)
-
-    def columns_of(block, masks):
-        held = block[None]
-        for mask in masks:
-            held = jnp.concatenate([held, flipped(held, "seq", mask)])
-        return held
-
-    bits = [1 << i for i in range(groups.bit_length() - 1)]
-    block = w_out.shape[1]
-    outs = []
-    for source, masks in ((w_out, bits), (flipped(w_out, "seq", high), bits[::-1])):
-        held = columns_of(source, masks)
-        offs = [0]
-        for mask in masks:
-            offs = offs + [off ^ mask for off in offs]
-        held = held.transpose(1, 0, 2).reshape(w_out.shape[0], groups * block)
-        outs.append((dot(both, held).reshape(2 * rows, groups, block), offs))
-
-    def in_order(value, offs):
-        return jnp.concatenate(
-            [
-                lax.dynamic_index_in_dim(
-                    value, jnp.asarray(offs, jnp.int32).argsort()[n ^ g], 1, False
-                )
-                for n in range(groups)
-            ],
-            axis=1,
-        )
-
-    own_out, other_out = (in_order(value, offs) for value, offs in outs)
-    keep = jnp.where(h == core, own_out, other_out)
-    give = jnp.where(h == core, other_out, own_out)
-    summed = (keep + flipped(give.astype(BF16), "tp", 1).astype(F32)).astype(BF16)
-    summed = summed.reshape(2, rows, groups * block)
-    mine = lax.dynamic_index_in_dim(summed, l, 0, False)
+    give = dot(both, give_columns).astype(BF16)
+    keep = dot(both, keep_columns)
+    summed = (keep + flipped(give, "tp", 1).astype(F32)).astype(BF16)
+    summed = summed.reshape(2, rows, -1)
+    ours = lax.dynamic_index_in_dim(summed, l, 0, False)
     theirs = flipped(lax.dynamic_index_in_dim(summed, 1 - l, 0, False), "seq", low)
     return jnp.where(
         l == 0,
-        jnp.concatenate([mine, theirs], axis=1),
-        jnp.concatenate([theirs, mine], axis=1),
+        jnp.concatenate([ours, theirs], axis=1),
+        jnp.concatenate([theirs, ours], axis=1),
     )
 
 

time: 204 us -> 160 us (0.78)
  waiting for transfers between devices: 83.8 us -> 57.3 us
  between operations: 15.7 us -> 0.59 us
  blocking collectives: 0 us -> 12.2 us
  local copies, waits for them, and re-layouts: 17.8 us -> 10.1 us
  starting transfers between devices: 59.2 us -> 54.1 us
  other arithmetic: 9.06 us -> 6.39 us
    all_to_all x4 -> x0, starting transfers between devices: 17.4 us -> none  [the longest x3 13.7 us: weight_of(): mine = lax.all_to_all(blocks, 'seq', 0, 0, axis_index_groups=layers)]
    ppermute x29 -> x34, waiting for transfers between devices: 71.6 us -> 57.3 us  [flipped(): return lax.ppermute(value, axis, [(i, i ^ mask) for i in range(size)])]
    ppermute x29 -> x34, starting transfers between devices: 41.8 us -> 54.1 us  [flipped(): return lax.ppermute(value, axis, [(i, i ^ mask) for i in range(size)])]
    all_to_all x0 -> x1, blocking collectives: none -> 12.2 us  [swapped(): return lax.all_to_all(blocks, 'seq', 0, 0, axis_index_groups=groups)]
    all_to_all x4 -> x0, waiting for transfers between devices: 12.2 us -> none  [the longest x3 12.2 us: weight_of(): mine = lax.all_to_all(blocks, 'seq', 0, 0, axis_index_groups=layers)]
    unnamed x35 -> x59, local copies, waits for them, and re-layouts: 8.71 us -> 2.49 us
    concatenate x2, other arithmetic: 4.41 us -> 0.19 us  [columns_of(): held = jnp.concatenate([held, flipped(held, 'seq', mask)])]
    select_n x5 -> x10, other arithmetic: 0.95 us -> 4.22 us  [the longest x4 1.63 us: in_order(): block = jnp.where(g == value, blocks[n ^ value], block)]
  transfers between devices with their start and end apart: 33 -> 34, of which waited for: 15 -> 17; matrix products, arithmetic and copies ran while one was open for 16% -> 15% of each run, Pallas kernels for 2% -> 1%
where the time goes in v2:
time: 160 us; the launch traced here: 159 us
  waiting for transfers between devices  57.3 us (36%)
  starting transfers between devices  54.1 us (34%)
  matrix products  14.8 us (9%)
  blocking collectives  12.2 us (8%)
  local copies, waits for them, and re-layouts  10.1 us (6%)
  other arithmetic  6.39 us (4%)
  Pallas kernels  3.78 us (2%)
    ppermute x34, waiting for transfers between devices, flipped(): return lax.ppermute(value, axis, [(i, i ^ mask) for i in range(size)])  57.3 us
    ppermute x34, starting transfers between devices, flipped(): return lax.ppermute(value, axis, [(i, i ^ mask) for i in range(size)])  54.1 us
    dot_general x10, matrix products, dot(): return jnp.dot(left, right, preferred_element_type=F32)  14.8 us
    all_to_all x1, blocking collectives, swapped(): return lax.all_to_all(blocks, 'seq', 0, 0, axis_index_groups=groups)  12.2 us
    pallas_call x2, Pallas kernels, call_by_lanes(): pl.pallas_call(kernel, grid=(width // lanes,), in_specs=specs, out_specs=...  3.78 us
  transfers between devices with their start and end apart: 34, of which 17 were waited for; matrix products, arithmetic and copies ran while one was open for 15% of the time, Pallas kernels for 1%

profile of v2, /device:TPU:0, one launch (start us, length us, event | category | flops | bytes accessed | tf_op | source)
XLA Modules:
  0.0 159.2 jit_solution(11500046745663701935)
XLA Ops:
  1.1 4.1 %collective-permute-start = (bf16[128,1024]{1,0:T(8,128)(2,1)S(1)}, bf16[128,1024]{1,0:T(8,128)(2,1)S(1)}, u32[]{:S(2)}, u32[]{:S(2)}) collective-permute-start(bf16[128,1024]{1,0:T(8,128)(2,1)S(1)} %get-tuple-element.112), channel_id=1, source_target_pairs={{0,16},{2,18},{4,20},{6,22},{8,24},{10,26},{12,28},{14,30},{16,0},... | collective-permute-start | bytes 786440 | tf_op jit(solution)/shard_map/ppermute | solution.py:19
  5.2 2.0 %constant_dynamic-slice_fusion.6 = (bf16[256,256]{1,0:T(8,128)(2,1)}, bf16[256,256]{1,0:T(8,128)(2,1)S(1)}, bf16[256,256]{1,0:T(8,128)(2,1)S(1)}, bf16[256,256]{...) fusion(bf16[256,1024]{1,0:T(8,128)(2,1)} %param.10, ...), kind=kLoop, calls=%fused_computation.82 | loop fusion | bytes 2097168 | tf_op jit(solution)/shard_map/dynamic_slice | solution.py:180
  13.1 3.1 %collective-permute-start.4 = (bf16[256,512]{1,0:T(8,128)(2,1)S(1)}, bf16[256,512]{1,0:T(8,128)(2,1)S(1)}, u32[]{:S(2)}, u32[]{:S(2)}) collective-permute-start(bf16[256,512]{1,0:T(8,128)(2,1)S(1)} %pad_maximum_fusion.11), channel_id=1, source_target_pairs={{0,6},{2,4},{4,2},{6,0},{8,14},{10,12},{12,10},{14,8},{16,22},{18,... | collective-permute-start | bytes 786440 | tf_op jit(solution)/shard_map/ppermute | solution.py:19
  17.2 9.2 %collective-permute-start.7 = (bf16[256,256]{1,0:T(8,128)(2,1)}, bf16[256,256]{1,0:T(8,128)(2,1)S(1)}, u32[]{:S(2)}, u32[]{:S(2)}) collective-permute-start(bf16[256,256]{1,0:T(8,128)(2,1)} %get-tuple-element.57), channel_id=1, source_target_pairs={{0,6},{2,4},{4,2},{6,0},{8,14},{10,12},{12,10},{14,8},{16,22},{18,... | collective-permute-start | bytes 393224 | tf_op jit(solution)/shard_map/ppermute | solution.py:19
  26.4 3.2 %collective-permute-done.7 = bf16[256,256]{1,0:T(8,128)(2,1)S(1)} collective-permute-done((bf16[256,256]{1,0:T(8,128)(2,1)}, bf16[256,256]{1,0:T(8,128)(2,1)S(1)}, u32[]{:S(2)}, u32[]{:S(2)}) %collective-permute-start.7) | collective-permute-done | bytes 131104 | tf_op jit(solution)/shard_map/ppermute | solution.py:19
  30.0 2.7 %collective-permute-start.11 = (bf16[128,1024]{1,0:T(8,128)(2,1)S(1)}, bf16[128,1024]{1,0:T(8,128)(2,1)S(1)}, u32[]{:S(2)}, u32[]{:S(2)}) collective-permute-start(bf16[128,1024]{1,0:T(8,128)(2,1)S(1)} %collective-permute-done), channel_id=1, source_target_pairs={{0,6},{2,4},{4,2},{6,0},{8,14},{10,12},{12,10},{14,8},{16,22},{18,... | collective-permute-start | bytes 786440 | tf_op jit(solution)/shard_map/ppermute | solution.py:19
  34.5 4.7 %collective-permute-start.8 = (bf16[1024,512]{1,0:T(8,128)(2,1)}, bf16[1024,512]{1,0:T(8,128)(2,1)}, u32[]{:S(2)}, u32[]{:S(2)}) collective-permute-start(bf16[1024,512]{1,0:T(8,128)(2,1)} %pad_maximum_fusion.2), channel_id=1, source_target_pairs={{0,8},{2,10},{4,12},{6,14},{8,0},{10,2},{12,4},{14,6},{16,24},{18,... | collective-permute-start | bytes 3145736 | tf_op jit(solution)/shard_map/ppermute | solution.py:19
  39.2 2.3 %collective-permute-done.12 = bf16[512,256]{1,0:T(8,128)(2,1)S(1)} collective-permute-done((bf16[512,256]{1,0:T(8,128)(2,1)}, bf16[512,256]{1,0:T(8,128)(2,1)S(1)}, u32[]{:S(2)}, u32[]{:S(2)}) %collective-permute-start.12) | collective-permute-done | bytes 262176 | tf_op jit(solution)/shard_map/ppermute | solution.py:19
  42.9 1.8 %collective-permute-start.14 = (bf16[128,1024]{1,0:T(8,128)(2,1)S(1)}, bf16[128,1024]{1,0:T(8,128)(2,1)S(1)}, u32[]{:S(2)}, u32[]{:S(2)}) collective-permute-start(bf16[128,1024]{1,0:T(8,128)(2,1)S(1)} %get-tuple-element.72), channel_id=1, source_target_pairs={{0,2},{2,0},{4,6},{6,4},{8,10},{10,8},{12,14},{14,12},{16,18},{18,... | collective-permute-start | bytes 786440 | tf_op jit(solution)/shard_map/ppermute | solution.py:19
  47.5 4.6 %collective-permute-done.14 = bf16[128,1024]{1,0:T(8,128)(2,1)S(1)} collective-permute-done((bf16[128,1024]{1,0:T(8,128)(2,1)S(1)}, bf16[128,1024]{1,0:T(8,128)(2,1)S(1)}, u32[]{:S(2)}, u32[]{:S(2)}) %collective-permute-start.14) | collective-permute-done | bytes 262176 | tf_op jit(solution)/shard_map/ppermute | solution.py:19
  52.1 6.7 %collective-permute-done.15 = bf16[128,1024]{1,0:T(8,128)(2,1)S(1)} collective-permute-done((bf16[128,1024]{1,0:T(8,128)(2,1)S(1)}, bf16[128,1024]{1,0:T(8,128)(2,1)S(1)}, u32[]{:S(2)}, u32[]{:S(2)}) %collective-permute-start.15) | collective-permute-done | bytes 262176 | tf_op jit(solution)/shard_map/ppermute | solution.py:19
  58.8 5.2 %collective-permute-done.8 = bf16[1024,512]{1,0:T(8,128)(2,1)} collective-permute-done((bf16[1024,512]{1,0:T(8,128)(2,1)}, bf16[1024,512]{1,0:T(8,128)(2,1)}, u32[]{:S(2)}, u32[]{:S(2)}) %collective-permute-start.8) | collective-permute-done | bytes 1048608 | tf_op jit(solution)/shard_map/ppermute | solution.py:19
  67.0 2.0 %fusion.10 = f32[512,512]{1,0:T(8,128)S(1)} fusion(bf16[512,1024]{1,0:T(8,128)(2,1)S(1)} %collective-permute-done.13, bf16[1024,512]{1,0:T(8,128)(2,1)} %collective-permute-done.8, pred[]{:T(512)S(6)} %eq.24, bf16[256,512]{1,0:T(8,128)(2,1)S(1)} %copy-done.9, bf16[256,512]{1,0:T(8,128)(2,1)S(1)} %copy-done.12, bf16[256,512]{1,0:T(8,128)(2,1)S(1)} %copy-done.15, ...), kind=kOutput, calls=%fused_computation.43 | convolution fusion | flops 541589504 | bytes 4194305 | tf_op jit(solution)/shard_map/dot_general | solution.py:50
  69.0 1.9 %fusion.21 = (bf16[512,512]{1,0:T(8,128)(2,1)}, f32[512,512]{1,0:T(8,128)}) fusion(f32[512,512]{1,0:T(8,128)S(1)} %fusion.10, bf16[512,1024]{1,0:T(8,128)(2,1)S(1)} %constant_dynamic-update-slice_fusion, bf16[1024,512]{1,0:T(8,128)(2,1)} %collective-permute-done.8, pred[]{:T(512)S(6)} %eq.23, bf16[256,512]{1,0:T(8,128)(2,1)S(1)} %copy-done.9, ...), kind=kOutput, calls=%fused_computation.102 | convolution fusion | flops 542113792 | bytes 5767169 | tf_op jit(solution)/shard_map/dot_general | solution.py:50
  77.2 3.3 %collective-permute-start.18 = (bf16[512,512]{1,0:T(8,128)(2,1)}, bf16[512,512]{1,0:T(8,128)(2,1)S(1)}, u32[]{:S(2)}, u32[]{:S(2)}) collective-permute-start(bf16[512,512]{1,0:T(8,128)(2,1)} %get-tuple-element.144), channel_id=1, source_target_pairs={{0,16},{2,18},{4,20},{6,22},{8,24},{10,26},{12,28},{14,30},{16,0},... | collective-permute-start | bytes 1572872 | tf_op jit(solution)/shard_map/ppermute | solution.py:19
  80.5 4.8 %collective-permute-done.25 = bf16[1,1024,256]{2,1,0:T(8,128)(2,1)S(1)} collective-permute-done((bf16[1,1024,256]{2,1,0:T(8,128)(2,1)S(1)}, bf16[1,1024,256]{2,1,0:T(8,128)(2,1)S(1)}, u32[]{:S(2)}, u32[]{:S(2)}) %collective-permute-start.25) | collective-permute-done | bytes 524320 | tf_op jit(solution)/shard_map/ppermute | solution.py:19
  87.0 2.3 %fusion.11 = f32[512,512]{1,0:T(8,128)S(1)} fusion(bf16[512,1024]{1,0:T(8,128)(2,1)} %collective-permute-done.17, bf16[1024,512]{1,0:T(8,128)(2,1)} %collective-permute-done.8, pred[]{:T(512)S(6)} %eq.24, bf16[256,512]{1,0:T(8,128)(2,1)S(1)} %copy-done.10, bf16[256,512]{1,0:T(8,128)(2,1)S(1)} %copy-done.13, bf16[256,512]{1,0:T(8,128)(2,1)S(1)} %copy-done.16, ...), kind=kOutput, calls=%fused_computation.44 | convolution fusion | flops 541589504 | bytes 4194305 | tf_op jit(solution)/shard_map/dot_general | solution.py:50
  89.3 2.0 %convolution_add_fusion.1 = f32[512,512]{1,0:T(8,128)S(1)} fusion(f32[512,512]{1,0:T(8,128)S(1)} %fusion.11, bf16[512,1024]{1,0:T(8,128)(2,1)} %constant_dynamic-update-slice_fusion.4, bf16[1024,512]{1,0:T(8,128)(2,1)} %collective-permute-done.8, pred[]{:T(512)S(6)} %eq.23, bf16[256,512]{1,0:T(8,128)(2,1)S(1)} %copy-done.10, ...), kind=kOutput, calls=%fused_computation.5 | convolution fusion | flops 541851648 | bytes 5242881 | tf_op jit(solution)/shard_map/dot_general | solution.py:50
  92.9 2.8 %collective-permute-start.21 = (f32[8,512]{1,0:T(8,128)S(1)}, f32[8,512]{1,0:T(8,128)S(1)}, u32[]{:S(2)}, u32[]{:S(2)}) collective-permute-start(f32[8,512]{1,0:T(8,128)S(1)} %get-tuple-element.105), channel_id=1, source_target_pairs={{0,24},{2,26},{4,28},{6,30},{8,16},{10,18},{12,20},{14,22},{16,8},... | collective-permute-start | bytes 49160 | tf_op jit(solution)/shard_map/ppermute | solution.py:19
  95.8 5.4 %collective-permute-done.20 = f32[8,512]{1,0:T(8,128)S(1)} collective-permute-done((f32[8,512]{1,0:T(8,128)S(1)}, f32[8,512]{1,0:T(8,128)S(1)}, u32[]{:S(2)}, u32[]{:S(2)}) %collective-permute-start.20) | collective-permute-done | bytes 16416 | tf_op jit(solution)/shard_map/ppermute | solution.py:19
  101.5 2.3 %collective-permute-done.21 = f32[8,512]{1,0:T(8,128)S(1)} collective-permute-done((f32[8,512]{1,0:T(8,128)S(1)}, f32[8,512]{1,0:T(8,128)S(1)}, u32[]{:S(2)}, u32[]{:S(2)}) %collective-permute-start.21) | collective-permute-done | bytes 16416 | tf_op jit(solution)/shard_map/ppermute | solution.py:19
  105.2 1.7 %fusion.13 = f32[512,256]{1,0:T(8,128)S(1)} fusion(bf16[512,1024]{1,0:T(8,128)(2,1)} %collective-permute-done.17, bf16[1024,256]{1,0:T(8,128)(2,1)S(1)} %pad_maximum_fusion.5, bf16[1024,256]{1,0:T(8,128)(2,1)S(1)} %collective-permute-done.19, pred[]{:T(512)S(6)} %eq.24), kind=kOutput, calls=%fused_computation.56 | convolution fusion | flops 268697600 | bytes 2621441 | tf_op jit(solution)/shard_map/dot_general | solution.py:50
  106.9 1.7 %convolution_add_fusion.3 = f32[512,256]{1,0:T(8,128)S(1)} fusion(f32[512,256]{1,0:T(8,128)S(1)} %fusion.13, bf16[512,1024]{1,0:T(8,128)(2,1)} %constant_dynamic-update-slice_fusion.4, bf16[1024,256]{1,0:T(8,128)(2,1)S(1)} %pad_maximum_fusion.5, bf16[1024,256]{1,0:T(8,128)(2,1)S(1)} %collective-permute-done.19, pred[]{:T(512)S(6)} %eq.23), kind=kOutput, calls=%fused_computation.8 | convolution fusion | flops 268828672 | bytes 3145729 | tf_op jit(solution)/shard_map/dot_general | solution.py:50
  109.5 2.4 %collective-permute-start.31 = (f32[8,256]{1,0:T(8,128)S(1)}, f32[8,256]{1,0:T(8,128)S(1)}, u32[]{:S(2)}, u32[]{:S(2)}) collective-permute-start(f32[8,256]{1,0:T(8,128)S(1)} %get-tuple-element.107), channel_id=1, source_target_pairs={{0,24},{2,26},{4,28},{6,30},{8,16},{10,18},{12,20},{14,22},{16,8},... | collective-permute-start | bytes 24584 | tf_op jit(solution)/shard_map/ppermute | solution.py:19
  115.4 2.4 %collective-permute-start.24 = (f32[16,256]{1,0:T(8,128)S(1)}, f32[16,256]{1,0:T(8,128)S(1)}, u32[]{:S(2)}, u32[]{:S(2)}) collective-permute-start(f32[16,256]{1,0:T(8,128)S(1)} %get-tuple-element.85), channel_id=1, source_target_pairs={{0,24},{2,26},{4,28},{6,30},{8,16},{10,18},{12,20},{14,22},{16,8},... | collective-permute-start | bytes 49160 | tf_op jit(solution)/shard_map/ppermute | solution.py:19
  118.4 2.8 %collective-permute-done.24 = f32[16,256]{1,0:T(8,128)S(1)} collective-permute-done((f32[16,256]{1,0:T(8,128)S(1)}, f32[16,256]{1,0:T(8,128)S(1)}, u32[]{:S(2)}, u32[]{:S(2)}) %collective-permute-start.24) | collective-permute-done | bytes 16416 | tf_op jit(solution)/shard_map/ppermute | solution.py:19
  121.6 3.7 %collective-permute-done.28 = bf16[2,1024,256]{2,1,0:T(8,128)(2,1)S(1)} collective-permute-done((bf16[2,1024,256]{2,1,0:T(8,128)(2,1)S(1)}, bf16[2,1024,256]{2,1,0:T(8,128)(2,1)S(1)}, u32[]{:S(2)}, u32[]{:S(2)}) %collective-permute-start.28) | collective-permute-done | bytes 1048608 | tf_op jit(solution)/shard_map/ppermute | solution.py:19
  126.4 3.9 %collective-permute-done.29 = bf16[512,256]{1,0:T(8,128)(2,1)S(1)} collective-permute-done((bf16[512,256]{1,0:T(8,128)(2,1)S(1)}, bf16[512,256]{1,0:T(8,128)(2,1)S(1)}, u32[]{:S(2)}, u32[]{:S(2)}) %collective-permute-start.29) | collective-permute-done | bytes 262176 | tf_op jit(solution)/shard_map/ppermute | solution.py:19
  130.4 2.3 %shard_map.92 = bf16[512,256]{1,0:T(8,128)(2,1)S(1)} custom-call(s32[1]{0:T(128)} %bitcast.g_ref, f32[512,256]{1,0:T(8,128)S(1)} %get-tuple-element.83.drive, f32[8,16,256]{2,1,0:T(8,128)S(1)} %get-tuple-element.84.entry, f32[16,256]{1,0:T(8,128)S(1)} %select_add_fusion.before, f32[4,128,256]{2,1,0:T(8,128)S(1)} %bitcast.122, ...), custom_call_target="tpu_custom_call" | custom-call | flops 10485760 | bytes 1765380 | tf_op jit(solution)/shard_map/pallas_call | solution.py:149
  132.7 12.2 %all_to_all.5 = bf16[8,128,256]{2,1,0:T(8,128)(2,1)S(1)} all-to-all(bf16[8,128,256]{2,1,0:T(8,128)(2,1)S(1)} %pad_maximum_fusion.7), channel_id=1, replica_groups={{0,2,4,6,8,10,12,14},{16,18,20,22,24,26,28,30},{1,3,5,7,9,11,13,15},{17..., dimensions={0} | all-to-all | bytes 1048576 | tf_op jit(solution)/shard_map/all_to_all | solution.py:27
  147.0 2.1 %collective-permute-done.32 = bf16[256,1024]{1,0:T(8,128)(2,1)S(1)} collective-permute-done((bf16[256,1024]{1,0:T(8,128)(2,1)}, bf16[256,1024]{1,0:T(8,128)(2,1)S(1)}, u32[]{:S(2)}, u32[]{:S(2)}) %collective-permute-start.32) | collective-permute-done | bytes 524320 | tf_op jit(solution)/shard_map/ppermute | solution.py:19
  150.9 7.4 %collective-permute-done.33 = bf16[128,1024]{1,0:T(8,128)(2,1)S(1)} collective-permute-done((bf16[128,1024]{1,0:T(8,128)(2,1)S(1)}, bf16[128,1024]{1,0:T(8,128)(2,1)S(1)}, u32[]{:S(2)}, u32[]{:S(2)}) %collective-permute-start.33) | collective-permute-done | bytes 262176 | tf_op jit(solution)/shard_map/ppermute | solution.py:19
  (143 shorter events, 39.5 us)
Async XLA Ops:
  1.1 16.0 %collective-permute-start = (bf16[128,1024]{1,0:T(8,128)(2,1)S(1)}, bf16[128,1024]{1,0:T(8,128)(2,1)S(1)}, u32[]{:S(2)}, u32[]{:S(2)}) collective-permute-start(bf16[128,1024]{1,0:T(8,128)(2,1)S(1)} %get-tuple-element.112), channel_id=1, source_target_pairs={{0,16},{2,18},{4,20},{6,22},{8,24},{10,26},{12,28},{14,30},{16,0},... | collective-permute-start | bytes 786440 | tf_op jit(solution)/shard_map/ppermute | solution.py:19
  7.2 5.8 %collective-permute-start.5 = (bf16[256,256]{1,0:T(8,128)(2,1)S(1)}, bf16[256,256]{1,0:T(8,128)(2,1)}, u32[]{:S(2)}, u32[]{:S(2)}) collective-permute-start(bf16[256,256]{1,0:T(8,128)(2,1)S(1)} %get-tuple-element.55), channel_id=1, source_target_pairs={{0,2},{2,0},{4,6},{6,4},{8,10},{10,8},{12,14},{14,12},{16,18},{18,... | collective-permute-start | bytes 393224 | tf_op jit(solution)/shard_map/ppermute | solution.py:19
  8.7 7.4 %collective-permute-start.6 = (bf16[256,256]{1,0:T(8,128)(2,1)S(1)}, bf16[256,256]{1,0:T(8,128)(2,1)S(1)}, u32[]{:S(2)}, u32[]{:S(2)}) collective-permute-start(bf16[256,256]{1,0:T(8,128)(2,1)S(1)} %get-tuple-element.56), channel_id=1, source_target_pairs={{0,4},{2,6},{4,0},{6,2},{8,12},{10,14},{12,8},{14,10},{16,20},{18,... | collective-permute-start | bytes 393224 | tf_op jit(solution)/shard_map/ppermute | solution.py:19
  11.1 18.4 %collective-permute-start.2 = (bf16[256,512]{1,0:T(8,128)(2,1)S(1)}, bf16[256,512]{1,0:T(8,128)(2,1)S(1)}, u32[]{:S(2)}, u32[]{:S(2)}) collective-permute-start(bf16[256,512]{1,0:T(8,128)(2,1)S(1)} %pad_maximum_fusion.9), channel_id=1, source_target_pairs={{0,2},{2,0},{4,6},{6,4},{8,10},{10,8},{12,14},{14,12},{16,18},{18,... | collective-permute-start | bytes 786440 | tf_op jit(solution)/shard_map/ppermute | solution.py:19
  11.7 17.8 %collective-permute-start.3 = (bf16[256,512]{1,0:T(8,128)(2,1)}, bf16[256,512]{1,0:T(8,128)(2,1)S(1)}, u32[]{:S(2)}, u32[]{:S(2)}) collective-permute-start(bf16[256,512]{1,0:T(8,128)(2,1)} %pad_maximum_fusion.10), channel_id=1, source_target_pairs={{0,4},{2,6},{4,0},{6,2},{8,12},{10,14},{12,8},{14,10},{16,20},{18,... | collective-permute-start | bytes 786440 | tf_op jit(solution)/shard_map/ppermute | solution.py:19
  13.1 16.5 %collective-permute-start.4 = (bf16[256,512]{1,0:T(8,128)(2,1)S(1)}, bf16[256,512]{1,0:T(8,128)(2,1)S(1)}, u32[]{:S(2)}, u32[]{:S(2)}) collective-permute-start(bf16[256,512]{1,0:T(8,128)(2,1)S(1)} %pad_maximum_fusion.11), channel_id=1, source_target_pairs={{0,6},{2,4},{4,2},{6,0},{8,14},{10,12},{12,10},{14,8},{16,22},{18,... | collective-permute-start | bytes 786440 | tf_op jit(solution)/shard_map/ppermute | solution.py:19
  16.2 13.4 %collective-permute-start.1 = (bf16[512,256]{1,0:T(8,128)(2,1)}, bf16[512,256]{1,0:T(8,128)(2,1)S(1)}, u32[]{:S(2)}, u32[]{:S(2)}) collective-permute-start(bf16[512,256]{1,0:T(8,128)(2,1)} %get-tuple-element.122), channel_id=1, source_target_pairs={{0,16},{2,18},{4,20},{6,22},{8,24},{10,26},{12,28},{14,30},{16,0},... | collective-permute-start | bytes 786440 | tf_op jit(solution)/shard_map/ppermute | solution.py:19
  17.2 12.4 %collective-permute-start.7 = (bf16[256,256]{1,0:T(8,128)(2,1)}, bf16[256,256]{1,0:T(8,128)(2,1)S(1)}, u32[]{:S(2)}, u32[]{:S(2)}) collective-permute-start(bf16[256,256]{1,0:T(8,128)(2,1)} %get-tuple-element.57), channel_id=1, source_target_pairs={{0,6},{2,4},{4,2},{6,0},{8,14},{10,12},{12,10},{14,8},{16,22},{18,... | collective-permute-start | bytes 393224 | tf_op jit(solution)/shard_map/ppermute | solution.py:19
  29.6 11.9 %collective-permute-start.12 = (bf16[512,256]{1,0:T(8,128)(2,1)}, bf16[512,256]{1,0:T(8,128)(2,1)S(1)}, u32[]{:S(2)}, u32[]{:S(2)}) collective-permute-start(bf16[512,256]{1,0:T(8,128)(2,1)} %get-tuple-element.66), channel_id=1, source_target_pairs={{0,16},{2,18},{4,20},{6,22},{8,24},{10,26},{12,28},{14,30},{16,0},... | collective-permute-start | bytes 786440 | tf_op jit(solution)/shard_map/ppermute | solution.py:19
  29.6 11.9 %collective-permute-start.10 = (bf16[128,1024]{1,0:T(8,128)(2,1)S(1)}, bf16[128,1024]{1,0:T(8,128)(2,1)S(1)}, u32[]{:S(2)}, u32[]{:S(2)}) collective-permute-start(bf16[128,1024]{1,0:T(8,128)(2,1)S(1)} %collective-permute-done), channel_id=1, source_target_pairs={{0,4},{2,6},{4,0},{6,2},{8,12},{10,14},{12,8},{14,10},{16,20},{18,... | collective-permute-start | bytes 786440 | tf_op jit(solution)/shard_map/ppermute | solution.py:19
  30.0 11.5 %collective-permute-start.11 = (bf16[128,1024]{1,0:T(8,128)(2,1)S(1)}, bf16[128,1024]{1,0:T(8,128)(2,1)S(1)}, u32[]{:S(2)}, u32[]{:S(2)}) collective-permute-start(bf16[128,1024]{1,0:T(8,128)(2,1)S(1)} %collective-permute-done), channel_id=1, source_target_pairs={{0,6},{2,4},{4,2},{6,0},{8,14},{10,12},{12,10},{14,8},{16,22},{18,... | collective-permute-start | bytes 786440 | tf_op jit(solution)/shard_map/ppermute | solution.py:19
  32.7 10.0 %collective-permute-start.9 = (bf16[128,1024]{1,0:T(8,128)(2,1)S(1)}, bf16[128,1024]{1,0:T(8,128)(2,1)S(1)}, u32[]{:S(2)}, u32[]{:S(2)}) collective-permute-start(bf16[128,1024]{1,0:T(8,128)(2,1)S(1)} %collective-permute-done), channel_id=1, source_target_pairs={{0,2},{2,0},{4,6},{6,4},{8,10},{10,8},{12,14},{14,12},{16,18},{18,... | collective-permute-start | bytes 786440 | tf_op jit(solution)/shard_map/ppermute | solution.py:19
  34.5 29.5 %collective-permute-start.8 = (bf16[1024,512]{1,0:T(8,128)(2,1)}, bf16[1024,512]{1,0:T(8,128)(2,1)}, u32[]{:S(2)}, u32[]{:S(2)}) collective-permute-start(bf16[1024,512]{1,0:T(8,128)(2,1)} %pad_maximum_fusion.2), channel_id=1, source_target_pairs={{0,8},{2,10},{4,12},{6,14},{8,0},{10,2},{12,4},{14,6},{16,24},{18,... | collective-permute-start | bytes 3145736 | tf_op jit(solution)/shard_map/ppermute | solution.py:19
  42.8 21.2 %collective-permute-start.13 = (bf16[512,1024]{1,0:T(8,128)(2,1)S(1)}, bf16[512,1024]{1,0:T(8,128)(2,1)S(1)}, u32[]{:S(2)}, u32[]{:S(2)}) collective-permute-start(bf16[512,1024]{1,0:T(8,128)(2,1)S(1)} %constant_dynamic-update-slice_fusion), channel_id=1, source_target_pairs={{0,1},{1,0},{2,3},{3,2},{4,5},{5,4},{6,7},{7,6},{8,9},{9,8},{10,11... | collective-permute-start | bytes 3145736 | tf_op jit(solution)/shard_map/ppermute | solution.py:19
  42.9 9.2 %collective-permute-start.14 = (bf16[128,1024]{1,0:T(8,128)(2,1)S(1)}, bf16[128,1024]{1,0:T(8,128)(2,1)S(1)}, u32[]{:S(2)}, u32[]{:S(2)}) collective-permute-start(bf16[128,1024]{1,0:T(8,128)(2,1)S(1)} %get-tuple-element.72), channel_id=1, source_target_pairs={{0,2},{2,0},{4,6},{6,4},{8,10},{10,8},{12,14},{14,12},{16,18},{18,... | collective-permute-start | bytes 786440 | tf_op jit(solution)/shard_map/ppermute | solution.py:19
  44.8 14.0 %collective-permute-start.15 = (bf16[128,1024]{1,0:T(8,128)(2,1)S(1)}, bf16[128,1024]{1,0:T(8,128)(2,1)S(1)}, u32[]{:S(2)}, u32[]{:S(2)}) collective-permute-start(bf16[128,1024]{1,0:T(8,128)(2,1)S(1)} %get-tuple-element.72), channel_id=1, source_target_pairs={{0,4},{2,6},{4,0},{6,2},{8,12},{10,14},{12,8},{14,10},{16,20},{18,... | collective-permute-start | bytes 786440 | tf_op jit(solution)/shard_map/ppermute | solution.py:19
  45.9 12.9 %collective-permute-start.16 = (bf16[128,1024]{1,0:T(8,128)(2,1)S(1)}, bf16[128,1024]{1,0:T(8,128)(2,1)S(1)}, u32[]{:S(2)}, u32[]{:S(2)}) collective-permute-start(bf16[128,1024]{1,0:T(8,128)(2,1)S(1)} %get-tuple-element.72), channel_id=1, source_target_pairs={{0,6},{2,4},{4,2},{6,0},{8,14},{10,12},{12,10},{14,8},{16,22},{18,... | collective-permute-start | bytes 786440 | tf_op jit(solution)/shard_map/ppermute | solution.py:19
  66.9 20.0 %collective-permute-start.17 = (bf16[512,1024]{1,0:T(8,128)(2,1)}, bf16[512,1024]{1,0:T(8,128)(2,1)}, u32[]{:S(2)}, u32[]{:S(2)}) collective-permute-start(bf16[512,1024]{1,0:T(8,128)(2,1)} %constant_dynamic-update-slice_fusion.4), channel_id=1, source_target_pairs={{0,1},{1,0},{2,3},{3,2},{4,5},{5,4},{6,7},{7,6},{8,9},{9,8},{10,11... | collective-permute-start | bytes 3145736 | tf_op jit(solution)/shard_map/ppermute | solution.py:19
  70.9 14.4 %collective-permute-start.25 = (bf16[1,1024,256]{2,1,0:T(8,128)(2,1)S(1)}, bf16[1,1024,256]{2,1,0:T(8,128)(2,1)S(1)}, u32[]{:S(2)}, u32[]{:S(2)}) collective-permute-start(bf16[1,1024,256]{2,1,0:T(8,128)(2,1)S(1)} %bitcast.130), channel_id=1, source_target_pairs={{0,2},{2,0},{4,6},{6,4},{8,10},{10,8},{12,14},{14,12},{16,18},{18,... | collective-permute-start | bytes 1572872 | tf_op jit(solution)/shard_map/ppermute | solution.py:19
  72.5 14.3 %collective-permute-start.27 = (bf16[1,1024,256]{2,1,0:T(8,128)(2,1)S(1)}, bf16[1,1024,256]{2,1,0:T(8,128)(2,1)S(1)}, u32[]{:S(2)}, u32[]{:S(2)}) collective-permute-start(bf16[1,1024,256]{2,1,0:T(8,128)(2,1)S(1)} %bitcast.132), channel_id=1, source_target_pairs={{0,4},{2,6},{4,0},{6,2},{8,12},{10,14},{12,8},{14,10},{16,20},{18,... | collective-permute-start | bytes 1572872 | tf_op jit(solution)/shard_map/ppermute | solution.py:19
  76.2 27.6 %collective-permute-start.19 = (bf16[1024,256]{1,0:T(8,128)(2,1)S(1)}, bf16[1024,256]{1,0:T(8,128)(2,1)S(1)}, u32[]{:S(2)}, u32[]{:S(2)}) collective-permute-start(bf16[1024,256]{1,0:T(8,128)(2,1)S(1)} %pad_maximum_fusion.5), channel_id=1, source_target_pairs={{0,8},{2,10},{4,12},{6,14},{8,0},{10,2},{12,4},{14,6},{16,24},{18,... | collective-permute-start | bytes 1572872 | tf_op jit(solution)/shard_map/ppermute | solution.py:19
  77.2 27.0 %collective-permute-start.18 = (bf16[512,512]{1,0:T(8,128)(2,1)}, bf16[512,512]{1,0:T(8,128)(2,1)S(1)}, u32[]{:S(2)}, u32[]{:S(2)}) collective-permute-start(bf16[512,512]{1,0:T(8,128)(2,1)} %get-tuple-element.144), channel_id=1, source_target_pairs={{0,16},{2,18},{4,20},{6,22},{8,24},{10,26},{12,28},{14,30},{16,0},... | collective-permute-start | bytes 1572872 | tf_op jit(solution)/shard_map/ppermute | solution.py:19
  85.4 35.9 %collective-permute-start.26 = (bf16[2,1024,256]{2,1,0:T(8,128)(2,1)S(1)}, bf16[2,1024,256]{2,1,0:T(8,128)(2,1)S(1)}, u32[]{:S(2)}, u32[]{:S(2)}) collective-permute-start(bf16[2,1024,256]{2,1,0:T(8,128)(2,1)S(1)} %pad_maximum_fusion.3), channel_id=1, source_target_pairs={{0,4},{2,6},{4,0},{6,2},{8,12},{10,14},{12,8},{14,10},{16,20},{18,... | collective-permute-start | bytes 3145736 | tf_op jit(solution)/shard_map/ppermute | solution.py:19
  92.1 9.0 %collective-permute-start.20 = (f32[8,512]{1,0:T(8,128)S(1)}, f32[8,512]{1,0:T(8,128)S(1)}, u32[]{:S(2)}, u32[]{:S(2)}) collective-permute-start(f32[8,512]{1,0:T(8,128)S(1)} %get-tuple-element.106), channel_id=1, source_target_pairs={{0,8},{2,10},{4,12},{6,14},{8,0},{10,2},{12,4},{14,6},{16,24},{18,... | collective-permute-start | bytes 49160 | tf_op jit(solution)/shard_map/ppermute | solution.py:19
  92.9 11.0 %collective-permute-start.21 = (f32[8,512]{1,0:T(8,128)S(1)}, f32[8,512]{1,0:T(8,128)S(1)}, u32[]{:S(2)}, u32[]{:S(2)}) collective-permute-start(f32[8,512]{1,0:T(8,128)S(1)} %get-tuple-element.105), channel_id=1, source_target_pairs={{0,24},{2,26},{4,28},{6,30},{8,16},{10,18},{12,20},{14,22},{16,8},... | collective-permute-start | bytes 49160 | tf_op jit(solution)/shard_map/ppermute | solution.py:19
  101.1 24.2 %collective-permute-start.28 = (bf16[2,1024,256]{2,1,0:T(8,128)(2,1)S(1)}, bf16[2,1024,256]{2,1,0:T(8,128)(2,1)S(1)}, u32[]{:S(2)}, u32[]{:S(2)}) collective-permute-start(bf16[2,1024,256]{2,1,0:T(8,128)(2,1)S(1)} %pad_maximum_fusion.4), channel_id=1, source_target_pairs={{0,2},{2,0},{4,6},{6,4},{8,10},{10,8},{12,14},{14,12},{16,18},{18,... | collective-permute-start | bytes 3145736 | tf_op jit(solution)/shard_map/ppermute | solution.py:19
  108.6 5.2 %collective-permute-start.30 = (f32[8,256]{1,0:T(8,128)S(1)}, f32[8,256]{1,0:T(8,128)S(1)}, u32[]{:S(2)}, u32[]{:S(2)}) collective-permute-start(f32[8,256]{1,0:T(8,128)S(1)} %get-tuple-element.108), channel_id=1, source_target_pairs={{0,8},{2,10},{4,12},{6,14},{8,0},{10,2},{12,4},{14,6},{16,24},{18,... | collective-permute-start | bytes 24584 | tf_op jit(solution)/shard_map/ppermute | solution.py:19
  109.5 6.0 %collective-permute-start.31 = (f32[8,256]{1,0:T(8,128)S(1)}, f32[8,256]{1,0:T(8,128)S(1)}, u32[]{:S(2)}, u32[]{:S(2)}) collective-permute-start(f32[8,256]{1,0:T(8,128)S(1)} %get-tuple-element.107), channel_id=1, source_target_pairs={{0,24},{2,26},{4,28},{6,30},{8,16},{10,18},{12,20},{14,22},{16,8},... | collective-permute-start | bytes 24584 | tf_op jit(solution)/shard_map/ppermute | solution.py:19
  113.8 4.6 %collective-permute-start.23 = (f32[16,256]{1,0:T(8,128)S(1)}, f32[16,256]{1,0:T(8,128)S(1)}, u32[]{:S(2)}, u32[]{:S(2)}) collective-permute-start(f32[16,256]{1,0:T(8,128)S(1)} %get-tuple-element.85), channel_id=1, source_target_pairs={{0,16},{2,18},{4,20},{6,22},{8,24},{10,26},{12,28},{14,30},{16,0},... | collective-permute-start | bytes 49160 | tf_op jit(solution)/shard_map/ppermute | solution.py:19
  115.4 5.8 %collective-permute-start.24 = (f32[16,256]{1,0:T(8,128)S(1)}, f32[16,256]{1,0:T(8,128)S(1)}, u32[]{:S(2)}, u32[]{:S(2)}) collective-permute-start(f32[16,256]{1,0:T(8,128)S(1)} %get-tuple-element.85), channel_id=1, source_target_pairs={{0,24},{2,26},{4,28},{6,30},{8,16},{10,18},{12,20},{14,22},{16,8},... | collective-permute-start | bytes 49160 | tf_op jit(solution)/shard_map/ppermute | solution.py:19
  117.8 12.5 %collective-permute-start.29 = (bf16[512,256]{1,0:T(8,128)(2,1)S(1)}, bf16[512,256]{1,0:T(8,128)(2,1)S(1)}, u32[]{:S(2)}, u32[]{:S(2)}) collective-permute-start(bf16[512,256]{1,0:T(8,128)(2,1)S(1)} %get-tuple-element.146), channel_id=1, source_target_pairs={{0,16},{2,18},{4,20},{6,22},{8,24},{10,26},{12,28},{14,30},{16,0},... | collective-permute-start | bytes 786440 | tf_op jit(solution)/shard_map/ppermute | solution.py:19
  149.9 8.4 %collective-permute-start.33 = (bf16[128,1024]{1,0:T(8,128)(2,1)S(1)}, bf16[128,1024]{1,0:T(8,128)(2,1)S(1)}, u32[]{:S(2)}, u32[]{:S(2)}) collective-permute-start(bf16[128,1024]{1,0:T(8,128)(2,1)S(1)} %get-tuple-element.118), channel_id=1, source_target_pairs={{0,8},{2,10},{4,12},{6,14},{8,0},{10,2},{12,4},{14,6},{16,24},{18,... | collective-permute-start | bytes 786440 | tf_op jit(solution)/shard_map/ppermute | solution.py:19
  (28 other events, 288.3 us)

commit v3 on v2

--- a/solution.py
+++ b/solution.py
@@ -137,6 +137,30 @@
         gated[start : start + step_rows, :] = value.astype(BF16)
 
 
+def assemble_kernel(depth, cuts, place, *refs):
+    count = len(refs) - len(cuts)
+    for off in range(count):
+        start = pl.multiple_of(lax.bitwise_xor(place[0], jnp.int32(off)) * depth, depth)
+        for (first, last), out in zip(cuts, refs[count:]):
+            out[pl.ds(start, depth), :] = refs[off][:, first:last]
+
+
+def assemble(place, blocks, cuts):
+    depth = blocks[0].shape[0]
+    outs = [jax.ShapeDtypeStruct((len(blocks) * depth, last - first), BF16) for first, last in cuts]
+    return pl.pallas_call(
+        functools.partial(assemble_kernel, depth, cuts),
+        in_specs=[pl.BlockSpec(memory_space=pltpu.SMEM)]
+        + [pl.BlockSpec(memory_space=pltpu.VMEM)] * len(blocks),
+        out_specs=[pl.BlockSpec(memory_space=pltpu.VMEM)] * len(outs),
+        out_shape=outs,
+        compiler_params=pltpu.CompilerParams(vmem_limit_bytes=32 * 1024 * 1024),
+        cost_estimate=pl.CostEstimate(
+            flops=0, bytes_accessed=sum(a.size * 2 for a in [*blocks, *outs]), transcendentals=0
+        ),
+    )(place, *blocks)
+
+
 def by_lanes(shape, lanes):
     lead = len(shape) - 1
     return pl.BlockSpec((*shape[:-1], lanes), lambda i: (0,) * lead + (i,))
@@ -172,12 +196,16 @@
     length = groups * rows
     layers = [[layer * groups + i for i in range(groups)] for layer in range(4)]
     halves = [[side * high + i for i in range(high)] for side in range(2)]
+    g_in = g.astype(jnp.int32).reshape(1)
 
     def at(side):
         return lax.dynamic_slice(tokens, (0, side * half + core * share), (rows, share))
 
     def block_of(w, off):
         return lax.dynamic_slice_in_dim(w, (g ^ off) * width, width, 1)
+
+    def channels(value):
+        return lax.dynamic_slice_in_dim(value, g * width, width, value.ndim - 1)
 
     def weight_of(mine, theirs):
         if tp_parts == 2:
@@ -190,129 +218,98 @@
             for off in range(tp_parts)
         ]
 
-    def columns_of(block, masks):
-        held, offs = block[None], [0]
-        for mask in masks:
-            held = jnp.concatenate([held, flipped(held, "seq", mask)])
-            offs = offs + [off ^ mask for off in offs]
-        ordered = in_order([held[offs.index(off)] for off in range(groups)], g)
-        return jnp.concatenate(ordered, axis=1)
-
-    got = flipped(at(1 - h), "seq", high)
-    flat_vk = together(
-        *(
-            jnp.concatenate([block_of(w, off) for w in (w_value, w_key)], axis=1)
-            for off in range(groups)
-        )
-    )
-    flat_q = together(*(block_of(w_query, off) for off in range(groups)))
-
-    def round_layer(blocks):
-        return [blocks[0]] + [flipped(blocks[off], "seq", off) for off in range(1, groups)]
-
-    came_vk, came_q = round_layer(flat_vk), round_layer(flat_q)
-    out_depth = w_out.shape[0] // 2
-    far_first = flipped(w_out[:out_depth], "seq", high)
-    got, far_first, *came = together(got, far_first, *came_vk, *came_q)
-    mine_vk = jnp.concatenate(in_order(came[:groups], g))
-    mine_q = jnp.concatenate(in_order(came[groups:], g))
-
-    def weight_of(mine, theirs):
-        if tp_parts == 2:
-            return [jnp.where((core ^ off) == l, mine, theirs) for off in range(2)]
-        both = jnp.where(
-            l == 0, jnp.concatenate([mine, theirs]), jnp.concatenate([theirs, mine])
-        )
-        return [
-            lax.dynamic_slice(both, ((core ^ off) * share, 0), (share, mine.shape[1]))
-            for off in range(tp_parts)
-        ]
-
-    def columns_of(block, masks):
-        held, offs = block[None], [0]
-        for mask in masks:
-            held = jnp.concatenate([held, flipped(held, "seq", mask)])
-            offs = offs + [off ^ mask for off in offs]
-        ordered = in_order([held[offs.index(off)] for off in range(groups)], g)
-        return jnp.concatenate(ordered, axis=1)
-
-    got = flipped(at(1 - h), "seq", high)
+    def partial_sums(shares, weights):
+        return sum(dot(t, w) for t, w in zip(shares, weights))
+
+    def sent_over(value):
+        return flipped(value.astype(BF16), "seq", high)
+
+    def rows_before(mine, theirs):
+        last = (groups - 1) ^ g
+
+        def tail(value):
+            value = value.reshape(groups, rows, -1)
+            return lax.dynamic_index_in_dim(value, last, 0, False)[rows - HALO :]
+
+        mine, theirs = tail(mine), tail(theirs)
+        return jnp.where(l == 0, mine, theirs), jnp.where(l == 0, theirs, mine)
+
+    def halo_of(near, far):
+        return jnp.where((h == 0) & (l == 0), 0.0, near + far)
+
+    given = at(1 - h)
+    got = flipped(given, "seq", high)
+    all_weights = [after(w, given) for w in (w_value, w_key, w_query)]
     flat = together(
         *(
-            jnp.concatenate([block_of(w, off) for w in (w_value, w_key, w_query)], axis=1)
+            jnp.concatenate([block_of(w, off) for w in all_weights], axis=1)
             for off in range(groups)
         )
     )
     came = [flat[0]] + [flipped(flat[off], "seq", off) for off in range(1, groups)]
     out_depth = w_out.shape[0] // 2
     far_first = flipped(w_out[:out_depth], "seq", high)
+    got, far_first, taps, rates, heights, skip, *came = together(
+        got, far_first, channels(short_taps), channels(decay_rates), channels(residues),
+        channels(skip_gain[None, :]), *came,
+    )
+    cuts = ((0, 2 * width), (2 * width, 3 * width))
+    if width % 128 == 0 and w_query.shape[0] % 16 == 0:
+        mine_vk, mine_q = assemble(g_in, came, cuts)
+    else:
+        whole = jnp.concatenate(in_order(came, g))
+        mine_vk, mine_q = (whole[:, first:last] for first, last in cuts)
 
     theirs_vk = flipped(mine_vk, "seq", low)
     far_last = flipped(after(w_out[out_depth:], got), "seq", high)
-    *there, far_last = together(*spread(got, "seq", groups), far_last)
-    here = spread(after(at(h), there[0]), "seq", groups)
+    there = spread(got, "seq", groups)
+    *there, far_last = together(*there, far_last)
+
+    here = [jnp.concatenate(spread(after(at(h), there[-1]), "seq", groups))]
     there = spread(jnp.concatenate(there), "tp", tp_parts)
-    theirs_vk, mine_q, *both = together(theirs_vk, mine_q, *there, *here)
+    out_pair = jnp.stack([w_out, jnp.concatenate([far_first, far_last])])
+    theirs_vk, mine_q, out_pair, *both = together(theirs_vk, mine_q, out_pair, *there, *here)
     there, here = both[:tp_parts], both[tp_parts:]
-
-    def partial_sums(shares, weights):
-        return sum(dot(t, w) for t, w in zip(shares, weights))
-
-    def sent_over(value):
-        return flipped(value.astype(BF16), "seq", high)
-
-    def rows_before(mine, theirs):
-        last = (groups - 1) ^ g
-
-        def tail(value):
-            value = value.reshape(groups, rows, -1)
-            return lax.dynamic_index_in_dim(value, last, 0, False)[rows - HALO :]
-
-        mine, theirs = tail(mine), tail(theirs)
-        near = flipped(jnp.where(l == 0, mine, theirs), "seq", low)
-        far = flipped(jnp.where(l == 0, theirs, mine), "seq", low | high)
-        return jnp.where((h == 0) & (l == 0), 0.0, near + far)
 
     weights_vk = weight_of(mine_vk, theirs_vk)
     there_vk = partial_sums(there, weights_vk)
     recv_vk = sent_over(there_vk)
-    here = spread(jnp.concatenate(here), "tp", tp_parts)
+    here = spread(here[0], "tp", tp_parts)
     theirs_q = flipped(after(mine_q, there_vk), "seq", low)
     here_vk = partial_sums(here, weights_vk)
-    vk_halo = rows_before(here_vk, there_vk)
-    recv_vk, theirs_q, vk_halo, *here = together(recv_vk, theirs_q, vk_halo, *here)
+    fast = tp_parts == 2 and groups == 4
+    columns = []
+    if fast:
+        columns = [after(out_pair, here[-1])]
+        columns = columns + [flipped(columns[0], "seq", off) for off in (1, 2)]
+    recv_vk, theirs_q, here_vk, *columns = together(recv_vk, theirs_q, here_vk, *columns)
+
+    def last_rows(value):
+        end = ((groups - 1) ^ g) * rows + rows - HALO
+        return lax.dynamic_slice_in_dim(value, end, HALO, 0).astype(F32)
+
+    vk_halo = lax.ppermute(
+        last_rows(here_vk) + last_rows(recv_vk), "seq", [(i, i + low) for i in range(seq_parts - low)]
+    )
 
     weights_q = weight_of(mine_q, theirs_q)
     there_q = partial_sums(there, weights_q)
     recv_q = sent_over(there_q)
     here_q = partial_sums(here, weights_q)
-    q_halo = rows_before(here_q, there_q)
+    near_q, far_q = rows_before(here_q, there_q)
 
     def named(vk, q):
         shape = (groups, rows, width)
-        return {"v": vk[:, :width].reshape(shape), "k": vk[:, width:].reshape(shape), "q": q.reshape(shape)}
-
-    here_parts, recv_parts = named(here_vk, here_q), named(recv_vk, recv_q)
-    parts = {n: (here_parts[n], None, recv_parts[n]) for n in ("v", "k", "q")}
+        return (vk[:, :width].reshape(shape), vk[:, width:].reshape(shape), q.reshape(shape))
+
+    (here_v, here_k, here_q), (recv_v, recv_k, recv_q) = named(here_vk, here_q), named(recv_vk, recv_q)
     v_halo, k_halo = vk_halo[:, :width], vk_halo[:, width:]
-
-    def channels(value):
-        return lax.dynamic_slice_in_dim(value, g * width, width, value.ndim - 1)
-
-    taps, rates, heights = channels(short_taps), channels(decay_rates), channels(residues)
-    skip = channels(skip_gain[None, :])
     lanes = min(128, width)
-    g_in = g.astype(jnp.int32).reshape(1)
     padded = pltpu.VMEM((HALO + length, lanes), F32)
     drive, entry, last = call_by_lanes(
         functools.partial(drive_kernel, groups, rows, order),
         lanes,
-        (
-            g_in,
-            parts["k"][0], parts["k"][2], k_halo,
-            parts["v"][0], parts["v"][2], v_halo,
-            taps[1], taps[2], rates,
-        ),
+        (g_in, here_k, recv_k, k_halo, here_v, recv_v, v_halo, taps[1], taps[2], rates),
         (
             jax.ShapeDtypeStruct((length, width), F32),
             jax.ShapeDtypeStruct((SEGMENTS, order, width), F32),
@@ -321,30 +318,29 @@
         [padded, padded, pltpu.VMEM((order, SEGMENTS, lanes), F32)],
         length * width * (2 * order + 16),
     )
-    if tp_parts == 2:
-        bits = [1 << i for i in range(groups.bit_length() - 1)]
-        own_columns = columns_of(after(w_out, there_vk), bits)
-        far_columns = columns_of(after(jnp.concatenate([far_first, far_last]), there_vk), bits[::-1])
+    fade = jnp.exp(-rates * float(length))
+    beside = flipped(jnp.concatenate([last, near_q, far_q]), "seq", low)
+    beside, near_q, far_q = beside[:order], beside[order : order + HALO], beside[order + HALO :]
+    ended = jnp.where(l == 0, last * fade + beside, beside * fade + last)
+    across = flipped(jnp.concatenate([ended, far_q]), "seq", high)
+    across, far_q = across[:order], across[order:]
+    before = jnp.where(h == 1, across * jnp.where(l == 1, fade, 1.0), 0.0)
+    before = before + jnp.where(l == 1, beside, 0.0)
+    q_halo = halo_of(near_q, far_q)
+    if fast:
+        across_own = flipped(columns[1][0], "seq", 2)
+        across_far = flipped(columns[2][1], "seq", 1)
+        own_columns, far_columns = (
+            jnp.concatenate(in_order([columns[0][i], columns[1][i], columns[2][i], last_block], g), axis=1)
+            for i, last_block in enumerate((across_own, across_far))
+        )
         keep_columns = jnp.where(h == core, own_columns, far_columns)
         give_columns = jnp.where(h == core, far_columns, own_columns)
-        before_gate = (keep_columns, give_columns)
-    layer = 2 * h + l
-    before = jnp.zeros_like(last)
-    for flip in range(1, 4):
-        other = layer ^ flip
-        sent = flipped(last, "seq", flip * low)
-        gap = jnp.maximum(layer - other - 1, 0).astype(F32) * float(length)
-        before = before + jnp.where(other < layer, jnp.exp(-rates * gap) * sent, 0.0)
-    if tp_parts == 2:
-        before, keep_columns, give_columns = together(before, *before_gate)
+        before, keep_columns, give_columns = together(before, keep_columns, give_columns)
     (gated,) = call_by_lanes(
         functools.partial(gate_kernel, groups, rows, order),
         lanes,
-        (
-            g_in, drive, entry, before,
-            parts["q"][0], parts["q"][2], q_halo,
-            taps[0], rates, heights, skip,
-        ),
+        (g_in, drive, entry, before, here_q, recv_q, q_halo, taps[0], rates, heights, skip),
         (jax.ShapeDtypeStruct((length, width), BF16),),
         [
             padded,
@@ -354,15 +350,12 @@
         length * width * (4 * order + 16),
     )
     gated = gated.reshape(groups, rows, width)
-    if tp_parts != 2:
+    if not fast:
         mine = swapped(gated, layers).transpose(1, 0, 2).reshape(rows, groups * width)
         columns = lax.all_gather(w_out, "seq", axis=1, tiled=True)
         partial_out = dot(mine, columns).astype(BF16)
         return lax.psum_scatter(partial_out, "tp", scatter_dimension=1, tiled=True)
-
-    both = swapped(
-        jnp.concatenate([gated, gated]), halves
-    )
+    both = swapped(jnp.concatenate([gated, gated]), halves)
     both = both.reshape(2, groups, rows, width).transpose(0, 2, 1, 3)
     both = both.reshape(2 * rows, groups * width)
     give = dot(both, give_columns).astype(BF16)

time: 160 us -> 155 us (0.969)
  waiting for transfers between devices: 57.3 us -> 82.4 us
  starting transfers between devices: 54.1 us -> 36.3 us
  local copies, waits for them, and re-layouts: 10.1 us -> 6.15 us
  matrix products: 14.8 us -> 11.1 us
  other arithmetic: 6.39 us -> 3.61 us
  blocking collectives: 12.2 us -> 10.4 us
    ppermute x34 -> x26, waiting for transfers between devices: 57.3 us -> 82.4 us  [flipped(): return lax.ppermute(value, axis, [(i, i ^ mask) for i in range(size)])]
    ppermute x34 -> x26, starting transfers between devices: 54.1 us -> 33.8 us  [flipped(): return lax.ppermute(value, axis, [(i, i ^ mask) for i in range(size)])]
    dot_general x10, matrix products: 14.8 us -> 11.1 us  [dot(): return jnp.dot(left, right, preferred_element_type=F32)]
    ppermute x0 -> x1, starting transfers between devices: none -> 2.49 us  [body(): lax.ppermute(last_rows(here_vk) + last_rows(recv_vk), 'seq', [(i, i + low...]
    concatenate x9 -> x7, other arithmetic: 2.11 us -> 0.19 us  [the longest x4 0.11 us: body(): jnp.concatenate([block_of(w, off) for w in all_weights], axis=1)]
    all_to_all x1, blocking collectives: 12.2 us -> 10.4 us  [swapped(): return lax.all_to_all(blocks, 'seq', 0, 0, axis_index_groups=groups)]
  transfers between devices with their start and end apart: 34 -> 27, of which waited for: 17 -> 14; matrix products, arithmetic and copies ran while one was open for 15% -> 7% of each run, Pallas kernels for 1% -> 1%
where the time goes in v3:
time: 155 us; the launch traced here: 154 us
  waiting for transfers between devices  82.4 us (53%)
  starting transfers between devices  36.3 us (23%)
  matrix products  11.1 us (7%)
  blocking collectives  10.4 us (7%)
  local copies, waits for them, and re-layouts  6.15 us (4%)
  Pallas kernels  3.89 us (3%)
  other arithmetic  3.61 us (2%)
    ppermute x26, waiting for transfers between devices, flipped(): return lax.ppermute(value, axis, [(i, i ^ mask) for i in range(size)])  82.4 us
    ppermute x26, starting transfers between devices, flipped(): return lax.ppermute(value, axis, [(i, i ^ mask) for i in range(size)])  33.8 us
    dot_general x10, matrix products, dot(): return jnp.dot(left, right, preferred_element_type=F32)  11.1 us
    all_to_all x1, blocking collectives, swapped(): return lax.all_to_all(blocks, 'seq', 0, 0, axis_index_groups=groups)  10.4 us
    pallas_call x2, Pallas kernels, call_by_lanes(): pl.pallas_call(kernel, grid=(width // lanes,), in_specs=specs, out_specs=...  3.79 us
  transfers between devices with their start and end apart: 27, of which 14 were waited for; matrix products, arithmetic and copies ran while one was open for 7% of the time, Pallas kernels for 1%

profile of v3, /device:TPU:0, one launch (start us, length us, event | category | flops | bytes accessed | tf_op | source)
XLA Modules:
  0.0 154.4 jit_solution(33606790899224679)
XLA Ops:
  1.2 4.1 %collective-permute-start = (bf16[128,1024]{1,0:T(8,128)(2,1)S(1)}, bf16[128,1024]{1,0:T(8,128)(2,1)S(1)}, u32[]{:S(2)}, u32[]{:S(2)}) collective-permute-start(bf16[128,1024]{1,0:T(8,128)(2,1)S(1)} %get-tuple-element.112), channel_id=1, source_target_pairs={{0,16},{2,18},{4,20},{6,22},{8,24},{10,26},{12,28},{14,30},{16,0},... | collective-permute-start | bytes 786440 | tf_op jit(solution)/shard_map/ppermute | solution.py:19
  6.8 1.6 %collective-permute-start.2 = (bf16[256,768]{1,0:T(8,128)(2,1)S(1)}, bf16[256,768]{1,0:T(8,128)(2,1)S(1)}, u32[]{:S(2)}, u32[]{:S(2)}) collective-permute-start(bf16[256,768]{1,0:T(8,128)(2,1)S(1)} %pad_maximum_fusion.6), channel_id=1, source_target_pairs={{0,2},{2,0},{4,6},{6,4},{8,10},{10,8},{12,14},{14,12},{16,18},{18,... | collective-permute-start | bytes 1179656 | tf_op jit(solution)/shard_map/ppermute | solution.py:19
  8.3 1.5 collective-permute-start.3
  12.0 11.7 %collective-permute-done = bf16[128,1024]{1,0:T(8,128)(2,1)S(1)} collective-permute-done((bf16[128,1024]{1,0:T(8,128)(2,1)S(1)}, bf16[128,1024]{1,0:T(8,128)(2,1)S(1)}, u32[]{:S(2)}, u32[]{:S(2)}) %collective-permute-start) | collective-permute-done | bytes 262176 | tf_op jit(solution)/shard_map/ppermute | solution.py:19
  23.7 4.8 %collective-permute-done.1 = bf16[512,256]{1,0:T(8,128)(2,1)S(1)} collective-permute-done((bf16[512,256]{1,0:T(8,128)(2,1)S(1)}, bf16[512,256]{1,0:T(8,128)(2,1)S(1)}, u32[]{:S(2)}, u32[]{:S(2)}) %collective-permute-start.1) | collective-permute-done | bytes 262176 | tf_op jit(solution)/shard_map/ppermute | solution.py:19
  28.6 2.6 %collective-permute-start.8 = (bf16[128,1024]{1,0:T(8,128)(2,1)S(1)}, bf16[128,1024]{1,0:T(8,128)(2,1)S(1)}, u32[]{:S(2)}, u32[]{:S(2)}) collective-permute-start(bf16[128,1024]{1,0:T(8,128)(2,1)S(1)} %collective-permute-done), channel_id=1, source_target_pairs={{0,6},{2,4},{4,2},{6,0},{8,14},{10,12},{12,10},{14,8},{16,22},{18,... | collective-permute-start | bytes 786440 | tf_op jit(solution)/shard_map/ppermute | solution.py:19
  32.2 4.1 %collective-permute-start.5 = (bf16[1024,512]{1,0:T(8,128)(2,1)S(1)}, bf16[1024,512]{1,0:T(8,128)(2,1)S(1)}, u32[]{:S(2)}, u32[]{:S(2)}) collective-permute-start(bf16[1024,512]{1,0:T(8,128)(2,1)S(1)} %get-tuple-element.62), channel_id=1, source_target_pairs={{0,8},{2,10},{4,12},{6,14},{8,0},{10,2},{12,4},{14,6},{16,24},{18,... | collective-permute-start | bytes 3145736 | tf_op jit(solution)/shard_map/ppermute | solution.py:19
  36.3 6.3 %collective-permute-done.9 = bf16[512,256]{1,0:T(8,128)(2,1)S(1)} collective-permute-done((bf16[512,256]{1,0:T(8,128)(2,1)S(1)}, bf16[512,256]{1,0:T(8,128)(2,1)S(1)}, u32[]{:S(2)}, u32[]{:S(2)}) %collective-permute-start.9) | collective-permute-done | bytes 262176 | tf_op jit(solution)/shard_map/ppermute | solution.py:19
  42.9 2.3 %collective-permute-start.13 = (bf16[128,1024]{1,0:T(8,128)(2,1)S(1)}, bf16[128,1024]{1,0:T(8,128)(2,1)S(1)}, u32[]{:S(2)}, u32[]{:S(2)}) collective-permute-start(bf16[128,1024]{1,0:T(8,128)(2,1)S(1)} %get-tuple-element.72), channel_id=1, source_target_pairs={{0,6},{2,4},{4,2},{6,0},{8,14},{10,12},{12,10},{14,8},{16,22},{18,... | collective-permute-start | bytes 786440 | tf_op jit(solution)/shard_map/ppermute | solution.py:19
  47.5 5.4 %collective-permute-done.13 = bf16[128,1024]{1,0:T(8,128)(2,1)S(1)} collective-permute-done((bf16[128,1024]{1,0:T(8,128)(2,1)S(1)}, bf16[128,1024]{1,0:T(8,128)(2,1)S(1)}, u32[]{:S(2)}, u32[]{:S(2)}) %collective-permute-start.13) | collective-permute-done | bytes 262176 | tf_op jit(solution)/shard_map/ppermute | solution.py:19
  53.0 5.1 %collective-permute-done.12 = bf16[128,1024]{1,0:T(8,128)(2,1)S(1)} collective-permute-done((bf16[128,1024]{1,0:T(8,128)(2,1)S(1)}, bf16[128,1024]{1,0:T(8,128)(2,1)S(1)}, u32[]{:S(2)}, u32[]{:S(2)}) %collective-permute-start.12) | collective-permute-done | bytes 262176 | tf_op jit(solution)/shard_map/ppermute | solution.py:19
  58.2 4.2 %collective-permute-done.5 = bf16[1024,512]{1,0:T(8,128)(2,1)S(1)} collective-permute-done((bf16[1024,512]{1,0:T(8,128)(2,1)S(1)}, bf16[1024,512]{1,0:T(8,128)(2,1)S(1)}, u32[]{:S(2)}, u32[]{:S(2)}) %collective-permute-start.5) | collective-permute-done | bytes 1048608 | tf_op jit(solution)/shard_map/ppermute | solution.py:19
  63.8 2.8 %collective-permute-done.16 = bf16[512,1024]{1,0:T(8,128)(2,1)} collective-permute-done((bf16[512,1024]{1,0:T(8,128)(2,1)S(1)}, bf16[512,1024]{1,0:T(8,128)(2,1)}, u32[]{:S(2)}, u32[]{:S(2)}) %collective-permute-start.16) | collective-permute-done | bytes 1048608 | tf_op jit(solution)/shard_map/ppermute | solution.py:19
  67.8 1.5 collective-permute-start.17
  69.3 2.3 %fusion.12 = f32[512,512]{1,0:T(8,128)S(1)} fusion(bf16[512,1024]{1,0:T(8,128)(2,1)} %copy-done.5, bf16[1024,512]{1,0:T(8,128)(2,1)S(1)} %get-tuple-element.62, bf16[1024,512]{1,0:T(8,128)(2,1)} %copy-done.7, pred[]{:T(512)S(6)} %eq.25), kind=kOutput, calls=%fused_computation.44 | convolution fusion | flops 537395200 | bytes 4194305 | tf_op jit(solution)/shard_map/dot_general | solution.py:50
  72.4 1.6 %collective-permute-start.14 = (bf16[512,512]{1,0:T(8,128)(2,1)S(1)}, bf16[512,512]{1,0:T(8,128)(2,1)S(1)}, u32[]{:S(2)}, u32[]{:S(2)}) collective-permute-start(bf16[512,512]{1,0:T(8,128)(2,1)S(1)} %convolution_add_fusion.1), channel_id=1, source_target_pairs={{0,16},{2,18},{4,20},{6,22},{8,24},{10,26},{12,28},{14,30},{16,0},... | collective-permute-start | bytes 1572872 | tf_op jit(solution)/shard_map/ppermute | solution.py:19
  73.9 2.2 %collective-permute-start.15 = (bf16[1024,256]{1,0:T(8,128)(2,1)S(1)}, bf16[1024,256]{1,0:T(8,128)(2,1)S(1)}, u32[]{:S(2)}, u32[]{:S(2)}) collective-permute-start(bf16[1024,256]{1,0:T(8,128)(2,1)S(1)} %get-tuple-element.77), channel_id=1, source_target_pairs={{0,8},{2,10},{4,12},{6,14},{8,0},{10,2},{12,4},{14,6},{16,24},{18,... | collective-permute-start | bytes 1572872 | tf_op jit(solution)/shard_map/ppermute | solution.py:19
  76.1 2.0 %fusion.11 = f32[512,512]{1,0:T(8,128)S(1)} fusion(bf16[512,1024]{1,0:T(8,128)(2,1)} %collective-permute-done.16, bf16[1024,512]{1,0:T(8,128)(2,1)S(1)} %get-tuple-element.62, bf16[1024,512]{1,0:T(8,128)(2,1)S(1)} %copy-done.8, pred[]{:T(512)S(6)} %eq.25), kind=kOutput, calls=%fused_computation.43 | convolution fusion | flops 537395200 | bytes 4194305 | tf_op jit(solution)/shard_map/dot_general | solution.py:50
  78.8 19.0 %collective-permute-done.15 = bf16[1024,256]{1,0:T(8,128)(2,1)S(1)} collective-permute-done((bf16[1024,256]{1,0:T(8,128)(2,1)S(1)}, bf16[1024,256]{1,0:T(8,128)(2,1)S(1)}, u32[]{:S(2)}, u32[]{:S(2)}) %collective-permute-start.15) | collective-permute-done | bytes 524320 | tf_op jit(solution)/shard_map/ppermute | solution.py:19
  98.8 1.7 %fusion.14 = f32[512,256]{1,0:T(8,128)S(1)} fusion(bf16[512,1024]{1,0:T(8,128)(2,1)} %collective-permute-done.16, bf16[1024,256]{1,0:T(8,128)(2,1)S(1)} %get-tuple-element.77, bf16[1024,256]{1,0:T(8,128)(2,1)S(1)} %collective-permute-done.15, pred[]{:T(512)S(6)} %eq.25), kind=kOutput, calls=%fused_computation.52 | convolution fusion | flops 268697600 | bytes 2621441 | tf_op jit(solution)/shard_map/dot_general | solution.py:50
  101.1 2.5 %collective-permute-start.19 = (f32[8,512]{1,0:T(8,128)S(1)}, f32[8,512]{1,0:T(8,128)S(1)}, u32[]{:S(2)}, u32[]{:S(2)}) collective-permute-start(f32[8,512]{1,0:T(8,128)S(1)} %convert_add_fusion), channel_id=1, source_target_pairs={{0,8},{2,10},{4,12},{6,14},{8,16},{10,18},{12,20},{14,22},{16,24},... | collective-permute-start | bytes 49160 | tf_op jit(solution)/shard_map/ppermute | solution.py:291
  103.6 2.9 %collective-permute-start.24 = (bf16[512,256]{1,0:T(8,128)(2,1)S(1)}, bf16[512,256]{1,0:T(8,128)(2,1)S(1)}, u32[]{:S(2)}, u32[]{:S(2)}) collective-permute-start(bf16[512,256]{1,0:T(8,128)(2,1)S(1)} %get-tuple-element.136), channel_id=1, source_target_pairs={{0,16},{2,18},{4,20},{6,22},{8,24},{10,26},{12,28},{14,30},{16,0},... | collective-permute-start | bytes 786440 | tf_op jit(solution)/shard_map/ppermute | solution.py:19
  109.5 2.8 %collective-permute-done.20 = f32[32,256]{1,0:T(8,128)S(1)} collective-permute-done((f32[32,256]{1,0:T(8,128)S(1)}, f32[32,256]{1,0:T(8,128)S(1)}, u32[]{:S(2)}, u32[]{:S(2)}) %collective-permute-start.20) | collective-permute-done | bytes 32800 | tf_op jit(solution)/shard_map/ppermute | solution.py:19
  112.3 2.2 %collective-permute-start.21 = (f32[24,256]{1,0:T(8,128)S(1)}, f32[24,256]{1,0:T(8,128)S(1)}, u32[]{:S(2)}, u32[]{:S(2)}) collective-permute-start(f32[24,256]{1,0:T(8,128)S(1)} %pad_maximum_fusion.10), channel_id=1, source_target_pairs={{0,16},{2,18},{4,20},{6,22},{8,24},{10,26},{12,28},{14,30},{16,0},... | collective-permute-start | bytes 73736 | tf_op jit(solution)/shard_map/ppermute | solution.py:19
  115.2 3.5 %collective-permute-done.21 = f32[24,256]{1,0:T(8,128)S(1)} collective-permute-done((f32[24,256]{1,0:T(8,128)S(1)}, f32[24,256]{1,0:T(8,128)S(1)}, u32[]{:S(2)}, u32[]{:S(2)}) %collective-permute-start.21) | collective-permute-done | bytes 24608 | tf_op jit(solution)/shard_map/ppermute | solution.py:19
  118.7 2.3 %collective-permute-done.22 = bf16[1024,256]{1,0:T(8,128)(2,1)S(1)} collective-permute-done((bf16[1024,256]{1,0:T(8,128)(2,1)S(1)}, bf16[1024,256]{1,0:T(8,128)(2,1)S(1)}, u32[]{:S(2)}, u32[]{:S(2)}) %collective-permute-start.22) | collective-permute-done | bytes 524320 | tf_op jit(solution)/shard_map/ppermute | solution.py:19
  121.3 4.9 %collective-permute-done.23 = bf16[1024,256]{1,0:T(8,128)(2,1)S(1)} collective-permute-done((bf16[1024,256]{1,0:T(8,128)(2,1)S(1)}, bf16[1024,256]{1,0:T(8,128)(2,1)S(1)}, u32[]{:S(2)}, u32[]{:S(2)}) %collective-permute-start.23) | collective-permute-done | bytes 524320 | tf_op jit(solution)/shard_map/ppermute | solution.py:19
  127.3 2.3 %shard_map.93 = bf16[512,256]{1,0:T(8,128)(2,1)S(1)} custom-call(s32[1]{0:T(128)} %bitcast.place.g_ref, f32[512,256]{1,0:T(8,128)S(1)} %get-tuple-element.85.drive, f32[8,16,256]{2,1,0:T(8,128)S(1)} %get-tuple-element.86.entry, f32[16,256]{1,0:T(8,128)S(1)} %fusion.16.before, f32[4,128,256]{2,1,0:T(8,128)S(1)} %bitcast.115, ...), custom_call_target="tpu_custom_call" | custom-call | flops 10485760 | bytes 1765380 | tf_op jit(solution)/shard_map/pallas_call | solution.py:173
  129.6 10.4 %all_to_all.5 = bf16[8,128,256]{2,1,0:T(8,128)(2,1)S(1)} all-to-all(bf16[8,128,256]{2,1,0:T(8,128)(2,1)S(1)} %pad_maximum_fusion.4), channel_id=1, replica_groups={{0,2,4,6,8,10,12,14},{16,18,20,22,24,26,28,30},{1,3,5,7,9,11,13,15},{17..., dimensions={0} | all-to-all | bytes 1048576 | tf_op jit(solution)/shard_map/all_to_all | solution.py:27
  140.6 1.5 convolution_convert_fusion
  142.1 2.1 %collective-permute-done.25 = bf16[256,1024]{1,0:T(8,128)(2,1)S(1)} collective-permute-done((bf16[256,1024]{1,0:T(8,128)(2,1)}, bf16[256,1024]{1,0:T(8,128)(2,1)S(1)}, u32[]{:S(2)}, u32[]{:S(2)}) %collective-permute-start.25) | collective-permute-done | bytes 524320 | tf_op jit(solution)/shard_map/ppermute | solution.py:19
  146.0 7.4 %collective-permute-done.26 = bf16[128,1024]{1,0:T(8,128)(2,1)S(1)} collective-permute-done((bf16[128,1024]{1,0:T(8,128)(2,1)S(1)}, bf16[128,1024]{1,0:T(8,128)(2,1)S(1)}, u32[]{:S(2)}, u32[]{:S(2)}) %collective-permute-start.26) | collective-permute-done | bytes 262176 | tf_op jit(solution)/shard_map/ppermute | solution.py:19
  (98 shorter events, 22.3 us)
Async XLA Ops:
  0.0 11.3 %copy-start = (f32[3,3,1024]{2,1,0:T(4,128)S(1)}, f32[3,3,1024]{2,1,0:T(4,128)}, u32[]{:S(2)}) copy-start(f32[3,3,1024]{2,1,0:T(4,128)} %param.13) | copy-start | bytes 110596
  1.2 22.5 %collective-permute-start = (bf16[128,1024]{1,0:T(8,128)(2,1)S(1)}, bf16[128,1024]{1,0:T(8,128)(2,1)S(1)}, u32[]{:S(2)}, u32[]{:S(2)}) collective-permute-start(bf16[128,1024]{1,0:T(8,128)(2,1)S(1)} %get-tuple-element.112), channel_id=1, source_target_pairs={{0,16},{2,18},{4,20},{6,22},{8,24},{10,26},{12,28},{14,30},{16,0},... | collective-permute-start | bytes 786440 | tf_op jit(solution)/shard_map/ppermute | solution.py:19
  6.8 21.7 %collective-permute-start.2 = (bf16[256,768]{1,0:T(8,128)(2,1)S(1)}, bf16[256,768]{1,0:T(8,128)(2,1)S(1)}, u32[]{:S(2)}, u32[]{:S(2)}) collective-permute-start(bf16[256,768]{1,0:T(8,128)(2,1)S(1)} %pad_maximum_fusion.6), channel_id=1, source_target_pairs={{0,2},{2,0},{4,6},{6,4},{8,10},{10,8},{12,14},{14,12},{16,18},{18,... | collective-permute-start | bytes 1179656 | tf_op jit(solution)/shard_map/ppermute | solution.py:19
  8.3 20.1 %collective-permute-start.3 = (bf16[256,768]{1,0:T(8,128)(2,1)S(1)}, bf16[256,768]{1,0:T(8,128)(2,1)S(1)}, u32[]{:S(2)}, u32[]{:S(2)}) collective-permute-start(bf16[256,768]{1,0:T(8,128)(2,1)S(1)} %pad_maximum_fusion.7), channel_id=1, source_target_pairs={{0,4},{2,6},{4,0},{6,2},{8,12},{10,14},{12,8},{14,10},{16,20},{18,... | collective-permute-start | bytes 1179656 | tf_op jit(solution)/shard_map/ppermute | solution.py:19
  9.8 18.6 %collective-permute-start.4 = (bf16[256,768]{1,0:T(8,128)(2,1)S(1)}, bf16[256,768]{1,0:T(8,128)(2,1)S(1)}, u32[]{:S(2)}, u32[]{:S(2)}) collective-permute-start(bf16[256,768]{1,0:T(8,128)(2,1)S(1)} %pad_maximum_fusion.8), channel_id=1, source_target_pairs={{0,6},{2,4},{4,2},{6,0},{8,14},{10,12},{12,10},{14,8},{16,22},{18,... | collective-permute-start | bytes 1179656 | tf_op jit(solution)/shard_map/ppermute | solution.py:19
  10.4 18.1 %collective-permute-start.1 = (bf16[512,256]{1,0:T(8,128)(2,1)S(1)}, bf16[512,256]{1,0:T(8,128)(2,1)S(1)}, u32[]{:S(2)}, u32[]{:S(2)}) collective-permute-start(bf16[512,256]{1,0:T(8,128)(2,1)S(1)} %get-tuple-element.118), channel_id=1, source_target_pairs={{0,16},{2,18},{4,20},{6,22},{8,24},{10,26},{12,28},{14,30},{16,0},... | collective-permute-start | bytes 786440 | tf_op jit(solution)/shard_map/ppermute | solution.py:19
  28.5 14.2 %collective-permute-start.9 = (bf16[512,256]{1,0:T(8,128)(2,1)S(1)}, bf16[512,256]{1,0:T(8,128)(2,1)S(1)}, u32[]{:S(2)}, u32[]{:S(2)}) collective-permute-start(bf16[512,256]{1,0:T(8,128)(2,1)S(1)} %get-tuple-element.66), channel_id=1, source_target_pairs={{0,16},{2,18},{4,20},{6,22},{8,24},{10,26},{12,28},{14,30},{16,0},... | collective-permute-start | bytes 786440 | tf_op jit(solution)/shard_map/ppermute | solution.py:19
  28.6 14.1 %collective-permute-start.8 = (bf16[128,1024]{1,0:T(8,128)(2,1)S(1)}, bf16[128,1024]{1,0:T(8,128)(2,1)S(1)}, u32[]{:S(2)}, u32[]{:S(2)}) collective-permute-start(bf16[128,1024]{1,0:T(8,128)(2,1)S(1)} %collective-permute-done), channel_id=1, source_target_pairs={{0,6},{2,4},{4,2},{6,0},{8,14},{10,12},{12,10},{14,8},{16,22},{18,... | collective-permute-start | bytes 786440 | tf_op jit(solution)/shard_map/ppermute | solution.py:19
  31.1 11.5 %collective-permute-start.7 = (bf16[128,1024]{1,0:T(8,128)(2,1)S(1)}, bf16[128,1024]{1,0:T(8,128)(2,1)S(1)}, u32[]{:S(2)}, u32[]{:S(2)}) collective-permute-start(bf16[128,1024]{1,0:T(8,128)(2,1)S(1)} %collective-permute-done), channel_id=1, source_target_pairs={{0,4},{2,6},{4,0},{6,2},{8,12},{10,14},{12,8},{14,10},{16,20},{18,... | collective-permute-start | bytes 786440 | tf_op jit(solution)/shard_map/ppermute | solution.py:19
  31.6 11.0 %collective-permute-start.6 = (bf16[128,1024]{1,0:T(8,128)(2,1)S(1)}, bf16[128,1024]{1,0:T(8,128)(2,1)S(1)}, u32[]{:S(2)}, u32[]{:S(2)}) collective-permute-start(bf16[128,1024]{1,0:T(8,128)(2,1)S(1)} %collective-permute-done), channel_id=1, source_target_pairs={{0,2},{2,0},{4,6},{6,4},{8,10},{10,8},{12,14},{14,12},{16,18},{18,... | collective-permute-start | bytes 786440 | tf_op jit(solution)/shard_map/ppermute | solution.py:19
  32.2 30.2 %collective-permute-start.5 = (bf16[1024,512]{1,0:T(8,128)(2,1)S(1)}, bf16[1024,512]{1,0:T(8,128)(2,1)S(1)}, u32[]{:S(2)}, u32[]{:S(2)}) collective-permute-start(bf16[1024,512]{1,0:T(8,128)(2,1)S(1)} %get-tuple-element.62), channel_id=1, source_target_pairs={{0,8},{2,10},{4,12},{6,14},{8,0},{10,2},{12,4},{14,6},{16,24},{18,... | collective-permute-start | bytes 3145736 | tf_op jit(solution)/shard_map/ppermute | solution.py:19
  42.8 15.4 %copy-start.3 = (bf16[512,1024]{1,0:T(8,128)(2,1)}, bf16[512,1024]{1,0:T(8,128)(2,1)S(1)}, u32[]{:S(2)}) copy-start(bf16[512,1024]{1,0:T(8,128)(2,1)S(1)} %constant_dynamic-update-slice_fusion) | copy-start | bytes 3145732
  42.8 19.6 %collective-permute-start.10 = (bf16[512,1024]{1,0:T(8,128)(2,1)S(1)}, bf16[512,1024]{1,0:T(8,128)(2,1)S(1)}, u32[]{:S(2)}, u32[]{:S(2)}) collective-permute-start(bf16[512,1024]{1,0:T(8,128)(2,1)S(1)} %constant_dynamic-update-slice_fusion), channel_id=1, source_target_pairs={{0,1},{1,0},{2,3},{3,2},{4,5},{5,4},{6,7},{7,6},{8,9},{9,8},{10,11... | collective-permute-start | bytes 3145736 | tf_op jit(solution)/shard_map/ppermute | solution.py:19
  42.9 10.1 %collective-permute-start.13 = (bf16[128,1024]{1,0:T(8,128)(2,1)S(1)}, bf16[128,1024]{1,0:T(8,128)(2,1)S(1)}, u32[]{:S(2)}, u32[]{:S(2)}) collective-permute-start(bf16[128,1024]{1,0:T(8,128)(2,1)S(1)} %get-tuple-element.72), channel_id=1, source_target_pairs={{0,6},{2,4},{4,2},{6,0},{8,14},{10,12},{12,10},{14,8},{16,22},{18,... | collective-permute-start | bytes 786440 | tf_op jit(solution)/shard_map/ppermute | solution.py:19
  45.1 13.0 %collective-permute-start.12 = (bf16[128,1024]{1,0:T(8,128)(2,1)S(1)}, bf16[128,1024]{1,0:T(8,128)(2,1)S(1)}, u32[]{:S(2)}, u32[]{:S(2)}) collective-permute-start(bf16[128,1024]{1,0:T(8,128)(2,1)S(1)} %get-tuple-element.72), channel_id=1, source_target_pairs={{0,4},{2,6},{4,0},{6,2},{8,12},{10,14},{12,8},{14,10},{16,20},{18,... | collective-permute-start | bytes 786440 | tf_op jit(solution)/shard_map/ppermute | solution.py:19
  45.7 12.4 %collective-permute-start.11 = (bf16[128,1024]{1,0:T(8,128)(2,1)S(1)}, bf16[128,1024]{1,0:T(8,128)(2,1)S(1)}, u32[]{:S(2)}, u32[]{:S(2)}) collective-permute-start(bf16[128,1024]{1,0:T(8,128)(2,1)S(1)} %get-tuple-element.72), channel_id=1, source_target_pairs={{0,2},{2,0},{4,6},{6,4},{8,10},{10,8},{12,14},{14,12},{16,18},{18,... | collective-permute-start | bytes 786440 | tf_op jit(solution)/shard_map/ppermute | solution.py:19
  63.7 2.8 %collective-permute-start.16 = (bf16[512,1024]{1,0:T(8,128)(2,1)S(1)}, bf16[512,1024]{1,0:T(8,128)(2,1)}, u32[]{:S(2)}, u32[]{:S(2)}) collective-permute-start(bf16[512,1024]{1,0:T(8,128)(2,1)S(1)} %pad_maximum_fusion.3), channel_id=1, source_target_pairs={{0,1},{1,0},{2,3},{3,2},{4,5},{5,4},{6,7},{7,6},{8,9},{9,8},{10,11... | collective-permute-start | bytes 3145736 | tf_op jit(solution)/shard_map/ppermute | solution.py:19
  63.7 7.9 %copy-start.8 = (bf16[1024,512]{1,0:T(8,128)(2,1)S(1)}, bf16[1024,512]{1,0:T(8,128)(2,1)}, u32[]{:S(2)}) copy-start(bf16[1024,512]{1,0:T(8,128)(2,1)} %copy-done.7) | copy-start | bytes 3145732
  66.5 31.3 %collective-permute-start.18 = (bf16[2,1024,256]{2,1,0:T(8,128)(2,1)}, bf16[2,1024,256]{2,1,0:T(8,128)(2,1)S(1)}, u32[]{:S(2)}, u32[]{:S(2)}) collective-permute-start(bf16[2,1024,256]{2,1,0:T(8,128)(2,1)} %pad_maximum_fusion.2), channel_id=1, source_target_pairs={{0,4},{2,6},{4,0},{6,2},{8,12},{10,14},{12,8},{14,10},{16,20},{18,... | collective-permute-start | bytes 3145736 | tf_op jit(solution)/shard_map/ppermute | solution.py:19
  67.8 30.0 %collective-permute-start.17 = (bf16[2,1024,256]{2,1,0:T(8,128)(2,1)}, bf16[2,1024,256]{2,1,0:T(8,128)(2,1)S(1)}, u32[]{:S(2)}, u32[]{:S(2)}) collective-permute-start(bf16[2,1024,256]{2,1,0:T(8,128)(2,1)} %pad_maximum_fusion.2), channel_id=1, source_target_pairs={{0,2},{2,0},{4,6},{6,4},{8,10},{10,8},{12,14},{14,12},{16,18},{18,... | collective-permute-start | bytes 3145736 | tf_op jit(solution)/shard_map/ppermute | solution.py:19
  72.4 25.5 %collective-permute-start.14 = (bf16[512,512]{1,0:T(8,128)(2,1)S(1)}, bf16[512,512]{1,0:T(8,128)(2,1)S(1)}, u32[]{:S(2)}, u32[]{:S(2)}) collective-permute-start(bf16[512,512]{1,0:T(8,128)(2,1)S(1)} %convolution_add_fusion.1), channel_id=1, source_target_pairs={{0,16},{2,18},{4,20},{6,22},{8,24},{10,26},{12,28},{14,30},{16,0},... | collective-permute-start | bytes 1572872 | tf_op jit(solution)/shard_map/ppermute | solution.py:19
  73.9 23.9 %collective-permute-start.15 = (bf16[1024,256]{1,0:T(8,128)(2,1)S(1)}, bf16[1024,256]{1,0:T(8,128)(2,1)S(1)}, u32[]{:S(2)}, u32[]{:S(2)}) collective-permute-start(bf16[1024,256]{1,0:T(8,128)(2,1)S(1)} %get-tuple-element.77), channel_id=1, source_target_pairs={{0,8},{2,10},{4,12},{6,14},{8,0},{10,2},{12,4},{14,6},{16,24},{18,... | collective-permute-start | bytes 1572872 | tf_op jit(solution)/shard_map/ppermute | solution.py:19
  78.1 19.8 %copy-start.6 = (bf16[512,1024]{1,0:T(8,128)(2,1)S(1)}, bf16[512,1024]{1,0:T(8,128)(2,1)}, u32[]{:S(2)}) copy-start(bf16[512,1024]{1,0:T(8,128)(2,1)} %copy-done.5) | copy-start | bytes 3145732
  101.1 19.9 %copy-start.1 = (bf16[2,1024,256]{2,1,0:T(8,128)(2,1)S(1)}, bf16[2,1024,256]{2,1,0:T(8,128)(2,1)}, u32[]{:S(2)}) copy-start(bf16[2,1024,256]{2,1,0:T(8,128)(2,1)} %pad_maximum_fusion.2) | copy-start | bytes 3145732
  101.1 5.4 %collective-permute-start.19 = (f32[8,512]{1,0:T(8,128)S(1)}, f32[8,512]{1,0:T(8,128)S(1)}, u32[]{:S(2)}, u32[]{:S(2)}) collective-permute-start(f32[8,512]{1,0:T(8,128)S(1)} %convert_add_fusion), channel_id=1, source_target_pairs={{0,8},{2,10},{4,12},{6,14},{8,16},{10,18},{12,20},{14,22},{16,24},... | collective-permute-start | bytes 49160 | tf_op jit(solution)/shard_map/ppermute | solution.py:291
  103.6 23.6 %collective-permute-start.24 = (bf16[512,256]{1,0:T(8,128)(2,1)S(1)}, bf16[512,256]{1,0:T(8,128)(2,1)S(1)}, u32[]{:S(2)}, u32[]{:S(2)}) collective-permute-start(bf16[512,256]{1,0:T(8,128)(2,1)S(1)} %get-tuple-element.136), channel_id=1, source_target_pairs={{0,16},{2,18},{4,20},{6,22},{8,24},{10,26},{12,28},{14,30},{16,0},... | collective-permute-start | bytes 786440 | tf_op jit(solution)/shard_map/ppermute | solution.py:19
  108.0 4.2 %collective-permute-start.20 = (f32[32,256]{1,0:T(8,128)S(1)}, f32[32,256]{1,0:T(8,128)S(1)}, u32[]{:S(2)}, u32[]{:S(2)}) collective-permute-start(f32[32,256]{1,0:T(8,128)S(1)} %pad_maximum_fusion.9), channel_id=1, source_target_pairs={{0,8},{2,10},{4,12},{6,14},{8,0},{10,2},{12,4},{14,6},{16,24},{18,... | collective-permute-start | bytes 98312 | tf_op jit(solution)/shard_map/ppermute | solution.py:19
  108.9 12.1 %collective-permute-start.22 = (bf16[1024,256]{1,0:T(8,128)(2,1)S(1)}, bf16[1024,256]{1,0:T(8,128)(2,1)S(1)}, u32[]{:S(2)}, u32[]{:S(2)}) collective-permute-start(bf16[1024,256]{1,0:T(8,128)(2,1)S(1)} %slice_bitcast_fusion.1), channel_id=1, source_target_pairs={{0,4},{2,6},{4,0},{6,2},{8,12},{10,14},{12,8},{14,10},{16,20},{18,... | collective-permute-start | bytes 1572872 | tf_op jit(solution)/shard_map/ppermute | solution.py:19
  112.3 6.4 %collective-permute-start.21 = (f32[24,256]{1,0:T(8,128)S(1)}, f32[24,256]{1,0:T(8,128)S(1)}, u32[]{:S(2)}, u32[]{:S(2)}) collective-permute-start(f32[24,256]{1,0:T(8,128)S(1)} %pad_maximum_fusion.10), channel_id=1, source_target_pairs={{0,16},{2,18},{4,20},{6,22},{8,24},{10,26},{12,28},{14,30},{16,0},... | collective-permute-start | bytes 73736 | tf_op jit(solution)/shard_map/ppermute | solution.py:19
  114.6 11.6 %collective-permute-start.23 = (bf16[1024,256]{1,0:T(8,128)(2,1)S(1)}, bf16[1024,256]{1,0:T(8,128)(2,1)S(1)}, u32[]{:S(2)}, u32[]{:S(2)}) collective-permute-start(bf16[1024,256]{1,0:T(8,128)(2,1)S(1)} %slice_bitcast_fusion), channel_id=1, source_target_pairs={{0,2},{2,0},{4,6},{6,4},{8,10},{10,8},{12,14},{14,12},{16,18},{18,... | collective-permute-start | bytes 1572872 | tf_op jit(solution)/shard_map/ppermute | solution.py:19
  142.1 2.1 %collective-permute-start.25 = (bf16[256,1024]{1,0:T(8,128)(2,1)}, bf16[256,1024]{1,0:T(8,128)(2,1)S(1)}, u32[]{:S(2)}, u32[]{:S(2)}) collective-permute-start(bf16[256,1024]{1,0:T(8,128)(2,1)} %convolution_convert_fusion), channel_id=1, source_target_pairs={{0,1},{1,0},{2,3},{3,2},{4,5},{5,4},{6,7},{7,6},{8,9},{9,8},{10,11... | collective-permute-start | bytes 1572872 | tf_op jit(solution)/shard_map/ppermute | solution.py:19
  145.0 8.4 %collective-permute-start.26 = (bf16[128,1024]{1,0:T(8,128)(2,1)S(1)}, bf16[128,1024]{1,0:T(8,128)(2,1)S(1)}, u32[]{:S(2)}, u32[]{:S(2)}) collective-permute-start(bf16[128,1024]{1,0:T(8,128)(2,1)S(1)} %get-tuple-element.114), channel_id=1, source_target_pairs={{0,8},{2,10},{4,12},{6,14},{8,0},{10,2},{12,4},{14,6},{16,24},{18,... | collective-permute-start | bytes 786440 | tf_op jit(solution)/shard_map/ppermute | solution.py:19
  (6 other events, 26.8 us)

commit v4 on v3

--- a/solution.py
+++ b/solution.py
@@ -280,7 +280,7 @@
     fast = tp_parts == 2 and groups == 4
     columns = []
     if fast:
-        columns = [after(out_pair, here[-1])]
+        columns = [out_pair]
         columns = columns + [flipped(columns[0], "seq", off) for off in (1, 2)]
     recv_vk, theirs_q, here_vk, *columns = together(recv_vk, theirs_q, here_vk, *columns)
 

time: 155 us -> 153 us (0.987)
  waiting for transfers between devices: 82.4 us -> 79.9 us
    ppermute x26, waiting for transfers between devices: 82.4 us -> 78.5 us  [flipped(): return lax.ppermute(value, axis, [(i, i ^ mask) for i in range(size)])]
  transfers between devices with their start and end apart: 27 -> 27, of which waited for: 14 -> 16; matrix products, arithmetic and copies ran while one was open for 7% -> 7% of each run, Pallas kernels for 1% -> 0%
where the time goes in v4:
time: 153 us; the launch traced here: 152 us
  waiting for transfers between devices  79.9 us (52%)
  starting transfers between devices  35.9 us (23%)
  blocking collectives  11.4 us (7%)
  matrix products  11.1 us (7%)
  local copies, waits for them, and re-layouts  6.15 us (4%)
  Pallas kernels  3.85 us (3%)
  other arithmetic  3.62 us (2%)
    ppermute x26, waiting for transfers between devices, flipped(): return lax.ppermute(value, axis, [(i, i ^ mask) for i in range(size)])  78.5 us
    ppermute x26, starting transfers between devices, flipped(): return lax.ppermute(value, axis, [(i, i ^ mask) for i in range(size)])  33.4 us
    all_to_all x1, blocking collectives, swapped(): return lax.all_to_all(blocks, 'seq', 0, 0, axis_index_groups=groups)  11.4 us
    dot_general x10, matrix products, dot(): return jnp.dot(left, right, preferred_element_type=F32)  11.1 us
    pallas_call x2, Pallas kernels, call_by_lanes(): pl.pallas_call(kernel, grid=(width // lanes,), in_specs=specs, out_specs=...  3.75 us
  transfers between devices with their start and end apart: 27, of which 16 were waited for; matrix products, arithmetic and copies ran while one was open for 7% of the time, Pallas kernels for 0%

profile of v4, /device:TPU:0, one launch (start us, length us, event | category | flops | bytes accessed | tf_op | source)
XLA Modules:
  0.0 152.3 jit_solution(13270415901331748932)
XLA Ops:
  1.2 4.1 %collective-permute-start = (bf16[128,1024]{1,0:T(8,128)(2,1)S(1)}, bf16[128,1024]{1,0:T(8,128)(2,1)S(1)}, u32[]{:S(2)}, u32[]{:S(2)}) collective-permute-start(bf16[128,1024]{1,0:T(8,128)(2,1)S(1)} %get-tuple-element.110), channel_id=1, source_target_pairs={{0,16},{2,18},{4,20},{6,22},{8,24},{10,26},{12,28},{14,30},{16,0},... | collective-permute-start | bytes 786440 | tf_op jit(solution)/shard_map/ppermute | solution.py:19
  6.8 1.6 %collective-permute-start.2 = (bf16[256,768]{1,0:T(8,128)(2,1)S(1)}, bf16[256,768]{1,0:T(8,128)(2,1)S(1)}, u32[]{:S(2)}, u32[]{:S(2)}) collective-permute-start(bf16[256,768]{1,0:T(8,128)(2,1)S(1)} %pad_maximum_fusion.6), channel_id=1, source_target_pairs={{0,2},{2,0},{4,6},{6,4},{8,10},{10,8},{12,14},{14,12},{16,18},{18,... | collective-permute-start | bytes 1179656 | tf_op jit(solution)/shard_map/ppermute | solution.py:19
  8.3 1.5 collective-permute-start.3
  12.0 11.7 %collective-permute-done = bf16[128,1024]{1,0:T(8,128)(2,1)S(1)} collective-permute-done((bf16[128,1024]{1,0:T(8,128)(2,1)S(1)}, bf16[128,1024]{1,0:T(8,128)(2,1)S(1)}, u32[]{:S(2)}, u32[]{:S(2)}) %collective-permute-start) | collective-permute-done | bytes 262176 | tf_op jit(solution)/shard_map/ppermute | solution.py:19
  23.7 4.8 %collective-permute-done.1 = bf16[512,256]{1,0:T(8,128)(2,1)S(1)} collective-permute-done((bf16[512,256]{1,0:T(8,128)(2,1)S(1)}, bf16[512,256]{1,0:T(8,128)(2,1)S(1)}, u32[]{:S(2)}, u32[]{:S(2)}) %collective-permute-start.1) | collective-permute-done | bytes 262176 | tf_op jit(solution)/shard_map/ppermute | solution.py:19
  28.6 1.6 %collective-permute-start.6 = (bf16[128,1024]{1,0:T(8,128)(2,1)S(1)}, bf16[128,1024]{1,0:T(8,128)(2,1)S(1)}, u32[]{:S(2)}, u32[]{:S(2)}) collective-permute-start(bf16[128,1024]{1,0:T(8,128)(2,1)S(1)} %collective-permute-done), channel_id=1, source_target_pairs={{0,2},{2,0},{4,6},{6,4},{8,10},{10,8},{12,14},{14,12},{16,18},{18,... | collective-permute-start | bytes 786440 | tf_op jit(solution)/shard_map/ppermute | solution.py:19
  30.2 1.5 collective-permute-start.7
  32.2 4.1 %collective-permute-start.5 = (bf16[1024,512]{1,0:T(8,128)(2,1)S(1)}, bf16[1024,512]{1,0:T(8,128)(2,1)S(1)}, u32[]{:S(2)}, u32[]{:S(2)}) collective-permute-start(bf16[1024,512]{1,0:T(8,128)(2,1)S(1)} %get-tuple-element.61), channel_id=1, source_target_pairs={{0,8},{2,10},{4,12},{6,14},{8,0},{10,2},{12,4},{14,6},{16,24},{18,... | collective-permute-start | bytes 3145736 | tf_op jit(solution)/shard_map/ppermute | solution.py:19
  36.3 6.4 %collective-permute-done.9 = bf16[512,256]{1,0:T(8,128)(2,1)S(1)} collective-permute-done((bf16[512,256]{1,0:T(8,128)(2,1)S(1)}, bf16[512,256]{1,0:T(8,128)(2,1)S(1)}, u32[]{:S(2)}, u32[]{:S(2)}) %collective-permute-start.9) | collective-permute-done | bytes 262176 | tf_op jit(solution)/shard_map/ppermute | solution.py:19
  44.2 1.5 collective-permute-start.12
  47.6 4.5 %collective-permute-done.11 = bf16[128,1024]{1,0:T(8,128)(2,1)S(1)} collective-permute-done((bf16[128,1024]{1,0:T(8,128)(2,1)S(1)}, bf16[128,1024]{1,0:T(8,128)(2,1)S(1)}, u32[]{:S(2)}, u32[]{:S(2)}) %collective-permute-start.11) | collective-permute-done | bytes 262176 | tf_op jit(solution)/shard_map/ppermute | solution.py:19
  52.1 5.1 %collective-permute-done.12 = bf16[128,1024]{1,0:T(8,128)(2,1)S(1)} collective-permute-done((bf16[128,1024]{1,0:T(8,128)(2,1)S(1)}, bf16[128,1024]{1,0:T(8,128)(2,1)S(1)}, u32[]{:S(2)}, u32[]{:S(2)}) %collective-permute-start.12) | collective-permute-done | bytes 262176 | tf_op jit(solution)/shard_map/ppermute | solution.py:19
  58.3 4.1 %collective-permute-done.5 = bf16[1024,512]{1,0:T(8,128)(2,1)S(1)} collective-permute-done((bf16[1024,512]{1,0:T(8,128)(2,1)S(1)}, bf16[1024,512]{1,0:T(8,128)(2,1)S(1)}, u32[]{:S(2)}, u32[]{:S(2)}) %collective-permute-start.5) | collective-permute-done | bytes 1048608 | tf_op jit(solution)/shard_map/ppermute | solution.py:19
  65.1 1.5 collective-permute-start.18
  66.6 2.3 %fusion.12 = f32[512,512]{1,0:T(8,128)S(1)} fusion(bf16[512,1024]{1,0:T(8,128)(2,1)} %copy-done.5, bf16[1024,512]{1,0:T(8,128)(2,1)S(1)} %get-tuple-element.61, bf16[1024,512]{1,0:T(8,128)(2,1)} %copy-done.7, pred[]{:T(512)S(6)} %eq.25), kind=kOutput, calls=%fused_computation.44 | convolution fusion | flops 537395200 | bytes 4194305 | tf_op jit(solution)/shard_map/dot_general | solution.py:50
  69.7 1.6 %collective-permute-start.14 = (bf16[512,512]{1,0:T(8,128)(2,1)S(1)}, bf16[512,512]{1,0:T(8,128)(2,1)S(1)}, u32[]{:S(2)}, u32[]{:S(2)}) collective-permute-start(bf16[512,512]{1,0:T(8,128)(2,1)S(1)} %convolution_add_fusion.1), channel_id=1, source_target_pairs={{0,16},{2,18},{4,20},{6,22},{8,24},{10,26},{12,28},{14,30},{16,0},... | collective-permute-start | bytes 1572872 | tf_op jit(solution)/shard_map/ppermute | solution.py:19
  71.2 2.2 %collective-permute-start.15 = (bf16[1024,256]{1,0:T(8,128)(2,1)S(1)}, bf16[1024,256]{1,0:T(8,128)(2,1)S(1)}, u32[]{:S(2)}, u32[]{:S(2)}) collective-permute-start(bf16[1024,256]{1,0:T(8,128)(2,1)S(1)} %get-tuple-element.76), channel_id=1, source_target_pairs={{0,8},{2,10},{4,12},{6,14},{8,0},{10,2},{12,4},{14,6},{16,24},{18,... | collective-permute-start | bytes 1572872 | tf_op jit(solution)/shard_map/ppermute | solution.py:19
  73.4 2.0 %fusion.11 = f32[512,512]{1,0:T(8,128)S(1)} fusion(bf16[512,1024]{1,0:T(8,128)(2,1)} %collective-permute-done.16, bf16[1024,512]{1,0:T(8,128)(2,1)S(1)} %get-tuple-element.61, bf16[1024,512]{1,0:T(8,128)(2,1)S(1)} %copy-done.8, pred[]{:T(512)S(6)} %eq.25), kind=kOutput, calls=%fused_computation.43 | convolution fusion | flops 537395200 | bytes 4194305 | tf_op jit(solution)/shard_map/dot_general | solution.py:50
  76.1 19.3 %collective-permute-done.15 = bf16[1024,256]{1,0:T(8,128)(2,1)S(1)} collective-permute-done((bf16[1024,256]{1,0:T(8,128)(2,1)S(1)}, bf16[1024,256]{1,0:T(8,128)(2,1)S(1)}, u32[]{:S(2)}, u32[]{:S(2)}) %collective-permute-start.15) | collective-permute-done | bytes 524320 | tf_op jit(solution)/shard_map/ppermute | solution.py:19
  95.9 1.7 %fusion.14 = f32[512,256]{1,0:T(8,128)S(1)} fusion(bf16[512,1024]{1,0:T(8,128)(2,1)} %collective-permute-done.16, bf16[1024,256]{1,0:T(8,128)(2,1)S(1)} %get-tuple-element.76, bf16[1024,256]{1,0:T(8,128)(2,1)S(1)} %collective-permute-done.15, pred[]{:T(512)S(6)} %eq.25), kind=kOutput, calls=%fused_computation.52 | convolution fusion | flops 268697600 | bytes 2621441 | tf_op jit(solution)/shard_map/dot_general | solution.py:50
  98.7 2.5 %collective-permute-start.19 = (f32[8,512]{1,0:T(8,128)S(1)}, f32[8,512]{1,0:T(8,128)S(1)}, u32[]{:S(2)}, u32[]{:S(2)}) collective-permute-start(f32[8,512]{1,0:T(8,128)S(1)} %convert_add_fusion), channel_id=1, source_target_pairs={{0,8},{2,10},{4,12},{6,14},{8,16},{10,18},{12,20},{14,22},{16,24},... | collective-permute-start | bytes 49160 | tf_op jit(solution)/shard_map/ppermute | solution.py:291
  101.3 1.4 collective-permute-done.19
  102.7 1.4 shard_map.92
  104.1 2.4 %collective-permute-start.20 = (f32[32,256]{1,0:T(8,128)S(1)}, f32[32,256]{1,0:T(8,128)S(1)}, u32[]{:S(2)}, u32[]{:S(2)}) collective-permute-start(f32[32,256]{1,0:T(8,128)S(1)} %pad_maximum_fusion.9), channel_id=1, source_target_pairs={{0,8},{2,10},{4,12},{6,14},{8,0},{10,2},{12,4},{14,6},{16,24},{18,... | collective-permute-start | bytes 98312 | tf_op jit(solution)/shard_map/ppermute | solution.py:19
  108.4 3.1 %collective-permute-start.21 = (f32[24,256]{1,0:T(8,128)S(1)}, f32[24,256]{1,0:T(8,128)S(1)}, u32[]{:S(2)}, u32[]{:S(2)}) collective-permute-start(f32[24,256]{1,0:T(8,128)S(1)} %pad_maximum_fusion.10), channel_id=1, source_target_pairs={{0,16},{2,18},{4,20},{6,22},{8,24},{10,26},{12,28},{14,30},{16,0},... | collective-permute-start | bytes 73736 | tf_op jit(solution)/shard_map/ppermute | solution.py:19
  113.6 4.7 %collective-permute-done.22 = bf16[1024,256]{1,0:T(8,128)(2,1)S(1)} collective-permute-done((bf16[1024,256]{1,0:T(8,128)(2,1)S(1)}, bf16[1024,256]{1,0:T(8,128)(2,1)S(1)}, u32[]{:S(2)}, u32[]{:S(2)}) %collective-permute-start.22) | collective-permute-done | bytes 524320 | tf_op jit(solution)/shard_map/ppermute | solution.py:19
  118.5 4.1 %collective-permute-done.23 = bf16[1024,256]{1,0:T(8,128)(2,1)S(1)} collective-permute-done((bf16[1024,256]{1,0:T(8,128)(2,1)S(1)}, bf16[1024,256]{1,0:T(8,128)(2,1)S(1)}, u32[]{:S(2)}, u32[]{:S(2)}) %collective-permute-start.23) | collective-permute-done | bytes 524320 | tf_op jit(solution)/shard_map/ppermute | solution.py:19
  124.3 2.3 %shard_map.93 = bf16[512,256]{1,0:T(8,128)(2,1)S(1)} custom-call(s32[1]{0:T(128)} %bitcast.place.g_ref, f32[512,256]{1,0:T(8,128)S(1)} %get-tuple-element.83.drive, f32[8,16,256]{2,1,0:T(8,128)S(1)} %get-tuple-element.84.entry, f32[16,256]{1,0:T(8,128)S(1)} %fusion.16.before, f32[4,128,256]{2,1,0:T(8,128)S(1)} %bitcast.115, ...), custom_call_target="tpu_custom_call" | custom-call | flops 10485760 | bytes 1765380 | tf_op jit(solution)/shard_map/pallas_call | solution.py:173
  126.7 11.4 %all_to_all.5 = bf16[8,128,256]{2,1,0:T(8,128)(2,1)S(1)} all-to-all(bf16[8,128,256]{2,1,0:T(8,128)(2,1)S(1)} %pad_maximum_fusion.4), channel_id=1, replica_groups={{0,2,4,6,8,10,12,14},{16,18,20,22,24,26,28,30},{1,3,5,7,9,11,13,15},{17..., dimensions={0} | all-to-all | bytes 1048576 | tf_op jit(solution)/shard_map/all_to_all | solution.py:27
  138.6 1.5 %convolution_convert_fusion = bf16[256,1024]{1,0:T(8,128)(2,1)} fusion(bf16[256,1024]{1,0:T(8,128)(2,1)S(1)} %bitcast.128, bf16[1024,1024]{1,0:T(8,128)(2,1)S(1)} %get-tuple-element.94), kind=kOutput, calls=%fused_computation.6 | convolution fusion | flops 537133056 | bytes 3145728 | tf_op jit(solution)/shard_map/dot_general | solution.py:50
  140.1 2.1 %collective-permute-done.25 = bf16[256,1024]{1,0:T(8,128)(2,1)S(1)} collective-permute-done((bf16[256,1024]{1,0:T(8,128)(2,1)}, bf16[256,1024]{1,0:T(8,128)(2,1)S(1)}, u32[]{:S(2)}, u32[]{:S(2)}) %collective-permute-start.25) | collective-permute-done | bytes 524320 | tf_op jit(solution)/shard_map/ppermute | solution.py:19
  144.0 7.4 %collective-permute-done.26 = bf16[128,1024]{1,0:T(8,128)(2,1)S(1)} collective-permute-done((bf16[128,1024]{1,0:T(8,128)(2,1)S(1)}, bf16[128,1024]{1,0:T(8,128)(2,1)S(1)}, u32[]{:S(2)}, u32[]{:S(2)}) %collective-permute-start.26) | collective-permute-done | bytes 262176 | tf_op jit(solution)/shard_map/ppermute | solution.py:19
  (98 shorter events, 24.4 us)
Async XLA Ops:
  0.0 11.3 %copy-start = (f32[3,3,1024]{2,1,0:T(4,128)S(1)}, f32[3,3,1024]{2,1,0:T(4,128)}, u32[]{:S(2)}) copy-start(f32[3,3,1024]{2,1,0:T(4,128)} %param.13) | copy-start | bytes 110596
  0.0 6.4 %copy-start.9 = (bf16[256,1024]{1,0:T(8,128)(2,1)S(1)}, bf16[256,1024]{1,0:T(8,128)(2,1)}, u32[]{:S(2)}) copy-start(bf16[256,1024]{1,0:T(8,128)(2,1)} %param.10) | copy-start | bytes 1572868
  1.2 22.5 %collective-permute-start = (bf16[128,1024]{1,0:T(8,128)(2,1)S(1)}, bf16[128,1024]{1,0:T(8,128)(2,1)S(1)}, u32[]{:S(2)}, u32[]{:S(2)}) collective-permute-start(bf16[128,1024]{1,0:T(8,128)(2,1)S(1)} %get-tuple-element.110), channel_id=1, source_target_pairs={{0,16},{2,18},{4,20},{6,22},{8,24},{10,26},{12,28},{14,30},{16,0},... | collective-permute-start | bytes 786440 | tf_op jit(solution)/shard_map/ppermute | solution.py:19
  6.8 21.7 %collective-permute-start.2 = (bf16[256,768]{1,0:T(8,128)(2,1)S(1)}, bf16[256,768]{1,0:T(8,128)(2,1)S(1)}, u32[]{:S(2)}, u32[]{:S(2)}) collective-permute-start(bf16[256,768]{1,0:T(8,128)(2,1)S(1)} %pad_maximum_fusion.6), channel_id=1, source_target_pairs={{0,2},{2,0},{4,6},{6,4},{8,10},{10,8},{12,14},{14,12},{16,18},{18,... | collective-permute-start | bytes 1179656 | tf_op jit(solution)/shard_map/ppermute | solution.py:19
  8.3 20.1 %collective-permute-start.3 = (bf16[256,768]{1,0:T(8,128)(2,1)S(1)}, bf16[256,768]{1,0:T(8,128)(2,1)S(1)}, u32[]{:S(2)}, u32[]{:S(2)}) collective-permute-start(bf16[256,768]{1,0:T(8,128)(2,1)S(1)} %pad_maximum_fusion.7), channel_id=1, source_target_pairs={{0,4},{2,6},{4,0},{6,2},{8,12},{10,14},{12,8},{14,10},{16,20},{18,... | collective-permute-start | bytes 1179656 | tf_op jit(solution)/shard_map/ppermute | solution.py:19
  9.8 18.6 %collective-permute-start.4 = (bf16[256,768]{1,0:T(8,128)(2,1)S(1)}, bf16[256,768]{1,0:T(8,128)(2,1)S(1)}, u32[]{:S(2)}, u32[]{:S(2)}) collective-permute-start(bf16[256,768]{1,0:T(8,128)(2,1)S(1)} %pad_maximum_fusion.8), channel_id=1, source_target_pairs={{0,6},{2,4},{4,2},{6,0},{8,14},{10,12},{12,10},{14,8},{16,22},{18,... | collective-permute-start | bytes 1179656 | tf_op jit(solution)/shard_map/ppermute | solution.py:19
  10.4 18.1 %collective-permute-start.1 = (bf16[512,256]{1,0:T(8,128)(2,1)S(1)}, bf16[512,256]{1,0:T(8,128)(2,1)S(1)}, u32[]{:S(2)}, u32[]{:S(2)}) collective-permute-start(bf16[512,256]{1,0:T(8,128)(2,1)S(1)} %get-tuple-element.116), channel_id=1, source_target_pairs={{0,16},{2,18},{4,20},{6,22},{8,24},{10,26},{12,28},{14,30},{16,0},... | collective-permute-start | bytes 786440 | tf_op jit(solution)/shard_map/ppermute | solution.py:19
  28.5 14.2 %collective-permute-start.9 = (bf16[512,256]{1,0:T(8,128)(2,1)S(1)}, bf16[512,256]{1,0:T(8,128)(2,1)S(1)}, u32[]{:S(2)}, u32[]{:S(2)}) collective-permute-start(bf16[512,256]{1,0:T(8,128)(2,1)S(1)} %get-tuple-element.65), channel_id=1, source_target_pairs={{0,16},{2,18},{4,20},{6,22},{8,24},{10,26},{12,28},{14,30},{16,0},... | collective-permute-start | bytes 786440 | tf_op jit(solution)/shard_map/ppermute | solution.py:19
  28.6 14.1 %collective-permute-start.6 = (bf16[128,1024]{1,0:T(8,128)(2,1)S(1)}, bf16[128,1024]{1,0:T(8,128)(2,1)S(1)}, u32[]{:S(2)}, u32[]{:S(2)}) collective-permute-start(bf16[128,1024]{1,0:T(8,128)(2,1)S(1)} %collective-permute-done), channel_id=1, source_target_pairs={{0,2},{2,0},{4,6},{6,4},{8,10},{10,8},{12,14},{14,12},{16,18},{18,... | collective-permute-start | bytes 786440 | tf_op jit(solution)/shard_map/ppermute | solution.py:19
  30.2 12.5 %collective-permute-start.7 = (bf16[128,1024]{1,0:T(8,128)(2,1)S(1)}, bf16[128,1024]{1,0:T(8,128)(2,1)S(1)}, u32[]{:S(2)}, u32[]{:S(2)}) collective-permute-start(bf16[128,1024]{1,0:T(8,128)(2,1)S(1)} %collective-permute-done), channel_id=1, source_target_pairs={{0,4},{2,6},{4,0},{6,2},{8,12},{10,14},{12,8},{14,10},{16,20},{18,... | collective-permute-start | bytes 786440 | tf_op jit(solution)/shard_map/ppermute | solution.py:19
  31.7 11.0 %collective-permute-start.8 = (bf16[128,1024]{1,0:T(8,128)(2,1)S(1)}, bf16[128,1024]{1,0:T(8,128)(2,1)S(1)}, u32[]{:S(2)}, u32[]{:S(2)}) collective-permute-start(bf16[128,1024]{1,0:T(8,128)(2,1)S(1)} %collective-permute-done), channel_id=1, source_target_pairs={{0,6},{2,4},{4,2},{6,0},{8,14},{10,12},{12,10},{14,8},{16,22},{18,... | collective-permute-start | bytes 786440 | tf_op jit(solution)/shard_map/ppermute | solution.py:19
  32.2 30.2 %collective-permute-start.5 = (bf16[1024,512]{1,0:T(8,128)(2,1)S(1)}, bf16[1024,512]{1,0:T(8,128)(2,1)S(1)}, u32[]{:S(2)}, u32[]{:S(2)}) collective-permute-start(bf16[1024,512]{1,0:T(8,128)(2,1)S(1)} %get-tuple-element.61), channel_id=1, source_target_pairs={{0,8},{2,10},{4,12},{6,14},{8,0},{10,2},{12,4},{14,6},{16,24},{18,... | collective-permute-start | bytes 3145736 | tf_op jit(solution)/shard_map/ppermute | solution.py:19
  42.8 15.5 %copy-start.3 = (bf16[512,1024]{1,0:T(8,128)(2,1)}, bf16[512,1024]{1,0:T(8,128)(2,1)S(1)}, u32[]{:S(2)}) copy-start(bf16[512,1024]{1,0:T(8,128)(2,1)S(1)} %constant_dynamic-update-slice_fusion) | copy-start | bytes 3145732
  42.8 19.6 %collective-permute-start.10 = (bf16[512,1024]{1,0:T(8,128)(2,1)S(1)}, bf16[512,1024]{1,0:T(8,128)(2,1)S(1)}, u32[]{:S(2)}, u32[]{:S(2)}) collective-permute-start(bf16[512,1024]{1,0:T(8,128)(2,1)S(1)} %constant_dynamic-update-slice_fusion), channel_id=1, source_target_pairs={{0,1},{1,0},{2,3},{3,2},{4,5},{5,4},{6,7},{7,6},{8,9},{9,8},{10,11... | collective-permute-start | bytes 3145736 | tf_op jit(solution)/shard_map/ppermute | solution.py:19
  42.9 9.2 %collective-permute-start.11 = (bf16[128,1024]{1,0:T(8,128)(2,1)S(1)}, bf16[128,1024]{1,0:T(8,128)(2,1)S(1)}, u32[]{:S(2)}, u32[]{:S(2)}) collective-permute-start(bf16[128,1024]{1,0:T(8,128)(2,1)S(1)} %get-tuple-element.71), channel_id=1, source_target_pairs={{0,2},{2,0},{4,6},{6,4},{8,10},{10,8},{12,14},{14,12},{16,18},{18,... | collective-permute-start | bytes 786440 | tf_op jit(solution)/shard_map/ppermute | solution.py:19
  44.2 13.0 %collective-permute-start.12 = (bf16[128,1024]{1,0:T(8,128)(2,1)S(1)}, bf16[128,1024]{1,0:T(8,128)(2,1)S(1)}, u32[]{:S(2)}, u32[]{:S(2)}) collective-permute-start(bf16[128,1024]{1,0:T(8,128)(2,1)S(1)} %get-tuple-element.71), channel_id=1, source_target_pairs={{0,4},{2,6},{4,0},{6,2},{8,12},{10,14},{12,8},{14,10},{16,20},{18,... | collective-permute-start | bytes 786440 | tf_op jit(solution)/shard_map/ppermute | solution.py:19
  45.7 12.5 %collective-permute-start.13 = (bf16[128,1024]{1,0:T(8,128)(2,1)S(1)}, bf16[128,1024]{1,0:T(8,128)(2,1)S(1)}, u32[]{:S(2)}, u32[]{:S(2)}) collective-permute-start(bf16[128,1024]{1,0:T(8,128)(2,1)S(1)} %get-tuple-element.71), channel_id=1, source_target_pairs={{0,6},{2,4},{4,2},{6,0},{8,14},{10,12},{12,10},{14,8},{16,22},{18,... | collective-permute-start | bytes 786440 | tf_op jit(solution)/shard_map/ppermute | solution.py:19
  63.7 9.7 %collective-permute-start.16 = (bf16[512,1024]{1,0:T(8,128)(2,1)S(1)}, bf16[512,1024]{1,0:T(8,128)(2,1)}, u32[]{:S(2)}, u32[]{:S(2)}) collective-permute-start(bf16[512,1024]{1,0:T(8,128)(2,1)S(1)} %pad_maximum_fusion.3), channel_id=1, source_target_pairs={{0,1},{1,0},{2,3},{3,2},{4,5},{5,4},{6,7},{7,6},{8,9},{9,8},{10,11... | collective-permute-start | bytes 3145736 | tf_op jit(solution)/shard_map/ppermute | solution.py:19
  63.8 31.7 %collective-permute-start.17 = (bf16[2,1024,256]{2,1,0:T(8,128)(2,1)}, bf16[2,1024,256]{2,1,0:T(8,128)(2,1)S(1)}, u32[]{:S(2)}, u32[]{:S(2)}) collective-permute-start(bf16[2,1024,256]{2,1,0:T(8,128)(2,1)} %pad_maximum_fusion.2), channel_id=1, source_target_pairs={{0,2},{2,0},{4,6},{6,4},{8,10},{10,8},{12,14},{14,12},{16,18},{18,... | collective-permute-start | bytes 3145736 | tf_op jit(solution)/shard_map/ppermute | solution.py:19
  65.1 30.4 %collective-permute-start.18 = (bf16[2,1024,256]{2,1,0:T(8,128)(2,1)}, bf16[2,1024,256]{2,1,0:T(8,128)(2,1)S(1)}, u32[]{:S(2)}, u32[]{:S(2)}) collective-permute-start(bf16[2,1024,256]{2,1,0:T(8,128)(2,1)} %pad_maximum_fusion.2), channel_id=1, source_target_pairs={{0,4},{2,6},{4,0},{6,2},{8,12},{10,14},{12,8},{14,10},{16,20},{18,... | collective-permute-start | bytes 3145736 | tf_op jit(solution)/shard_map/ppermute | solution.py:19
  69.7 25.8 %collective-permute-start.14 = (bf16[512,512]{1,0:T(8,128)(2,1)S(1)}, bf16[512,512]{1,0:T(8,128)(2,1)S(1)}, u32[]{:S(2)}, u32[]{:S(2)}) collective-permute-start(bf16[512,512]{1,0:T(8,128)(2,1)S(1)} %convolution_add_fusion.1), channel_id=1, source_target_pairs={{0,16},{2,18},{4,20},{6,22},{8,24},{10,26},{12,28},{14,30},{16,0},... | collective-permute-start | bytes 1572872 | tf_op jit(solution)/shard_map/ppermute | solution.py:19
  71.2 24.2 %collective-permute-start.15 = (bf16[1024,256]{1,0:T(8,128)(2,1)S(1)}, bf16[1024,256]{1,0:T(8,128)(2,1)S(1)}, u32[]{:S(2)}, u32[]{:S(2)}) collective-permute-start(bf16[1024,256]{1,0:T(8,128)(2,1)S(1)} %get-tuple-element.76), channel_id=1, source_target_pairs={{0,8},{2,10},{4,12},{6,14},{8,0},{10,2},{12,4},{14,6},{16,24},{18,... | collective-permute-start | bytes 1572872 | tf_op jit(solution)/shard_map/ppermute | solution.py:19
  75.4 20.1 %copy-start.6 = (bf16[512,1024]{1,0:T(8,128)(2,1)S(1)}, bf16[512,1024]{1,0:T(8,128)(2,1)}, u32[]{:S(2)}) copy-start(bf16[512,1024]{1,0:T(8,128)(2,1)} %copy-done.5) | copy-start | bytes 3145732
  98.7 19.6 %copy-start.1 = (bf16[2,1024,256]{2,1,0:T(8,128)(2,1)S(1)}, bf16[2,1024,256]{2,1,0:T(8,128)(2,1)}, u32[]{:S(2)}) copy-start(bf16[2,1024,256]{2,1,0:T(8,128)(2,1)} %pad_maximum_fusion.2) | copy-start | bytes 3145732
  98.7 3.9 %collective-permute-start.19 = (f32[8,512]{1,0:T(8,128)S(1)}, f32[8,512]{1,0:T(8,128)S(1)}, u32[]{:S(2)}, u32[]{:S(2)}) collective-permute-start(f32[8,512]{1,0:T(8,128)S(1)} %convert_add_fusion), channel_id=1, source_target_pairs={{0,8},{2,10},{4,12},{6,14},{8,16},{10,18},{12,20},{14,22},{16,24},... | collective-permute-start | bytes 49160 | tf_op jit(solution)/shard_map/ppermute | solution.py:291
  104.1 4.3 %collective-permute-start.20 = (f32[32,256]{1,0:T(8,128)S(1)}, f32[32,256]{1,0:T(8,128)S(1)}, u32[]{:S(2)}, u32[]{:S(2)}) collective-permute-start(f32[32,256]{1,0:T(8,128)S(1)} %pad_maximum_fusion.9), channel_id=1, source_target_pairs={{0,8},{2,10},{4,12},{6,14},{8,0},{10,2},{12,4},{14,6},{16,24},{18,... | collective-permute-start | bytes 98312 | tf_op jit(solution)/shard_map/ppermute | solution.py:19
  106.5 11.8 %collective-permute-start.22 = (bf16[1024,256]{1,0:T(8,128)(2,1)S(1)}, bf16[1024,256]{1,0:T(8,128)(2,1)S(1)}, u32[]{:S(2)}, u32[]{:S(2)}) collective-permute-start(bf16[1024,256]{1,0:T(8,128)(2,1)S(1)} %slice_bitcast_fusion.1), channel_id=1, source_target_pairs={{0,4},{2,6},{4,0},{6,2},{8,12},{10,14},{12,8},{14,10},{16,20},{18,... | collective-permute-start | bytes 1572872 | tf_op jit(solution)/shard_map/ppermute | solution.py:19
  108.4 5.2 %collective-permute-start.21 = (f32[24,256]{1,0:T(8,128)S(1)}, f32[24,256]{1,0:T(8,128)S(1)}, u32[]{:S(2)}, u32[]{:S(2)}) collective-permute-start(f32[24,256]{1,0:T(8,128)S(1)} %pad_maximum_fusion.10), channel_id=1, source_target_pairs={{0,16},{2,18},{4,20},{6,22},{8,24},{10,26},{12,28},{14,30},{16,0},... | collective-permute-start | bytes 73736 | tf_op jit(solution)/shard_map/ppermute | solution.py:19
  111.6 11.0 %collective-permute-start.23 = (bf16[1024,256]{1,0:T(8,128)(2,1)S(1)}, bf16[1024,256]{1,0:T(8,128)(2,1)S(1)}, u32[]{:S(2)}, u32[]{:S(2)}) collective-permute-start(bf16[1024,256]{1,0:T(8,128)(2,1)S(1)} %slice_bitcast_fusion), channel_id=1, source_target_pairs={{0,2},{2,0},{4,6},{6,4},{8,10},{10,8},{12,14},{14,12},{16,18},{18,... | collective-permute-start | bytes 1572872 | tf_op jit(solution)/shard_map/ppermute | solution.py:19
  112.2 12.1 %collective-permute-start.24 = (bf16[512,256]{1,0:T(8,128)(2,1)S(1)}, bf16[512,256]{1,0:T(8,128)(2,1)S(1)}, u32[]{:S(2)}, u32[]{:S(2)}) collective-permute-start(bf16[512,256]{1,0:T(8,128)(2,1)S(1)} %get-tuple-element.134), channel_id=1, source_target_pairs={{0,16},{2,18},{4,20},{6,22},{8,24},{10,26},{12,28},{14,30},{16,0},... | collective-permute-start | bytes 786440 | tf_op jit(solution)/shard_map/ppermute | solution.py:19
  140.1 2.1 %collective-permute-start.25 = (bf16[256,1024]{1,0:T(8,128)(2,1)}, bf16[256,1024]{1,0:T(8,128)(2,1)S(1)}, u32[]{:S(2)}, u32[]{:S(2)}) collective-permute-start(bf16[256,1024]{1,0:T(8,128)(2,1)} %convolution_convert_fusion), channel_id=1, source_target_pairs={{0,1},{1,0},{2,3},{3,2},{4,5},{5,4},{6,7},{7,6},{8,9},{9,8},{10,11... | collective-permute-start | bytes 1572872 | tf_op jit(solution)/shard_map/ppermute | solution.py:19
  143.0 8.4 %collective-permute-start.26 = (bf16[128,1024]{1,0:T(8,128)(2,1)S(1)}, bf16[128,1024]{1,0:T(8,128)(2,1)S(1)}, u32[]{:S(2)}, u32[]{:S(2)}) collective-permute-start(bf16[128,1024]{1,0:T(8,128)(2,1)S(1)} %get-tuple-element.112), channel_id=1, source_target_pairs={{0,8},{2,10},{4,12},{6,14},{8,0},{10,2},{12,4},{14,6},{16,24},{18,... | collective-permute-start | bytes 786440 | tf_op jit(solution)/shard_map/ppermute | solution.py:19
  (6 other events, 22.8 us)
